TPU v7x, 32 devices: a whole 2x2x4 slice. The times are simulated.
32 devices in a mesh: seq: 4 (over z), head: 8 (over y, x, core).
Axes of the slice: x: 2, y: 2, z: 4, core: 2. Of those that a mesh axis runs over, the one named last changes fastest.
Arguments:
- values: bfloat16 [4096, 8192], P('seq', 'head'), may hold values from -6 to 6
- gate_z: bfloat16 [4096, 8192], P('seq', 'head'), may hold values from -6 to 6
- b_keys: bfloat16 [4096, 8, 128], P('seq'), may hold values from -0.5 to 0.5
- c_queries: bfloat16 [4096, 8, 128], P('seq'), may hold values from -6 to 6
- log_decay: float32 [4096, 128], P('seq', 'head'), may hold values from -2.5 to 0
- level_weight: float32 [4096, 128, 7], P('seq', 'head'), may hold values from 0.2 to 2
- doc_start: int32 [64], replicated, may hold values 0 or 1
- norm_gain: float32 [8192], replicated, may hold values from 0.25 to 1.75
Outputs:
- normed: bfloat16 [4096, 8192], P(('seq', 'head'))
All inputs are finite; a program needn't handle non-finite values.
Results may differ from a plain program's by a relative error of at most 0.0049.
Values may be sent and summed in bfloat16 or wider, within the bound.
No kernel may reach another device: no remote copies, remote signals or barrier semaphores. Data moves between devices by JAX's collectives and lax.ppermute only.
A program may use at most 192 MiB of HBM per device.

v0:
```python
import functools

import jax
import jax.numpy as jnp
from jax import lax
from jax.experimental import pallas as pl
from jax.experimental.pallas import tpu as pltpu
from jax.sharding import PartitionSpec as P

MIXER_HEADS = 128
GROUPS = 8
SPAN = 64
TILE = 2 * SPAN
LANES = 128
SUBLANES = 8
NEVER = -1e30
HIGHEST = lax.Precision.HIGHEST
MIB = 2**20


def dot(left, right, contract=((1,), (0,)), precision=None):
    return lax.dot_general(
        left, right, (contract, ((), ())), precision=precision, preferred_element_type=jnp.float32
    )


def iota(shape, axis):
    return lax.broadcasted_iota(jnp.int32, shape, axis)


def halves(coef):
    high = coef.astype(jnp.bfloat16)
    low = (coef - high.astype(jnp.float32)).astype(jnp.bfloat16)
    return jnp.concatenate([high, low], axis=1)


def spread(first, width, head_dim):
    row = jnp.bitwise_and(iota((2 * LANES, width), 0), LANES - 1)
    head = jnp.right_shift(iota((2 * LANES, width), 1), head_dim.bit_length() - 1)
    return jnp.where(row == head + first, 1.0, 0.0).astype(jnp.bfloat16)


def head_row(column, width, head_dim):
    shape = (column.shape[0], width)
    head = jnp.right_shift(iota(shape, 1), head_dim.bit_length() - 1)
    return jnp.sum(jnp.where(head == iota(shape, 0), column, 0.0), axis=0, keepdims=True)


def stack_rows(pieces):
    rows = sum(piece.shape[0] for piece in pieces)
    if rows < LANES:
        pieces = pieces + [jnp.zeros((LANES - rows, LANES), jnp.float32)]
    return jnp.transpose(jnp.concatenate(pieces, axis=0))


def state_kernel(head_dim, docs, decay, keys, inputs, state, message, through):
    heads, tokens = decay.shape
    width = inputs.shape[1]
    tiles = tokens // TILE
    first = lax.axis_index("seq") * (tokens // SPAN)
    lane = iota((heads, TILE), 1)
    later = jnp.where(iota((TILE, TILE), 0) > iota((TILE, TILE), 1), 1.0, 0.0)
    stacked = jnp.concatenate([decay[:, b * TILE : (b + 1) * TILE] for b in range(tiles)], axis=0)
    suffix = dot(stacked, later, precision=HIGHEST)
    totals = jnp.sum(stacked, axis=1, keepdims=True)
    after = jnp.zeros((heads, 1), jnp.float32)
    closed = jnp.float32(0.0)
    rows = [None] * tiles
    for b in reversed(range(tiles)):
        second = NEVER * docs[first + 2 * b + 1].astype(jnp.float32)
        shut = jnp.where(lane < SPAN, closed + second, closed)
        rows[b] = jnp.exp(suffix[b * heads : (b + 1) * heads] + after + shut)
        closed = closed + second + NEVER * docs[first + 2 * b].astype(jnp.float32)
        after = after + totals[b * heads : (b + 1) * heads]
    columns = stack_rows(rows)
    owner = jnp.right_shift(iota((TILE, LANES), 1), heads.bit_length() - 1)
    shape = (2 * LANES, width)
    same = jnp.bitwise_and(iota(shape, 0), heads - 1) == jnp.right_shift(
        iota(shape, 1), head_dim.bit_length() - 1
    )
    one_hot = jnp.where(same, 1.0, 0.0).astype(jnp.bfloat16)
    total = jnp.zeros((keys.shape[1], width), jnp.float32)
    for b in range(tiles):
        scale = dot(halves(jnp.where(owner == b, columns, 0.0)), one_hot)
        piece = inputs[b * TILE : (b + 1) * TILE, :].astype(jnp.float32) * scale
        total += dot(
            keys[b * TILE : (b + 1) * TILE, :], piece.astype(jnp.bfloat16), ((0,), (0,))
        )
    state[...] = total
    message[...] = total.astype(jnp.bfloat16)
    row = head_row(jnp.exp(after + closed), width, head_dim)
    through[...] = jnp.broadcast_to(row, through.shape)


def local_kernel(
    head_dim, far, docs, decay, weight, inputs, queries, keys, out, coefs, slots, run, hot, now
):
    heads = decay.shape[0]
    width = inputs.shape[1]
    near = slots.shape[0]
    tile = pl.program_id(0)
    first = lax.axis_index("seq") * (pl.num_programs(0) * (TILE // SPAN)) + 2 * tile
    lane = iota((heads, TILE), 1)
    early = iota((TILE, TILE), 1) < SPAN

    @pl.when(tile == 0)
    def _():
        run[...] = jnp.zeros_like(run)
        for index in range(near + 1):
            hot[index] = spread((2 + index) * heads, width, head_dim)

    shut_first = NEVER * docs[first].astype(jnp.float32)
    shut_second = NEVER * docs[first + 1].astype(jnp.float32)
    upto = jnp.where(iota((TILE, TILE), 0) <= iota((TILE, TILE), 1), 1.0, 0.0)
    sums = dot(decay[...], upto, precision=HIGHEST)
    last = jnp.broadcast_to(sums[:, TILE - 1 :], sums.shape)
    total = last + (shut_first + shut_second)
    opened = sums + jnp.where(lane < SPAN, shut_first, shut_first + shut_second)
    own = sums + jnp.log(weight[0])
    beside = jnp.where(lane < SPAN, own, sums + jnp.log(weight[1]) + shut_second)
    since = [
        jnp.where(jnp.bitwise_and(tile, 2**k - 1) == 0, 0.0, run[k]) for k in range(near)
    ] + [run[near]]
    rows = [own, beside]
    rows += [jnp.exp(opened + since[k]) * weight[2 + k] for k in range(near)]
    rows += [jnp.exp(last - sums + jnp.where(lane < SPAN, shut_second, 0.0))]
    rows += [jnp.exp(opened + since[near]) * weight[2 + near + m] for m in range(far)]
    for k in range(near + 1):
        run[k] = since[k] + total
    columns = stack_rows(rows)
    terms = halves(columns)
    coefs[...] = terms

    span_queries = queries[...]
    scores = dot(span_queries, keys[...], ((1,), (1,)))
    causal = iota((TILE, TILE), 0) >= iota((TILE, TILE), 1)
    per_tile = LANES // head_dim
    lane_head = jnp.right_shift(iota((TILE, LANES), 1), head_dim.bit_length() - 1)
    for part in range(width // LANES):
        block = inputs[:, part * LANES : (part + 1) * LANES]
        left, right = [], []
        for inner in range(per_tile):
            head = part * per_tile + inner
            gap = jnp.where(
                early,
                jnp.broadcast_to(columns[:, heads + head : heads + head + 1], (TILE, TILE)),
                jnp.broadcast_to(columns[:, head : head + 1], (TILE, TILE)),
            )
            gap = jnp.where(causal, gap - sums[head : head + 1, :], NEVER)
            left.append((jnp.exp(gap) * scores).astype(jnp.bfloat16))
            right.append(jnp.where(lane_head == inner, block, jnp.zeros_like(block)))
        out[:, part * LANES : (part + 1) * LANES] = dot(
            jnp.concatenate(left, axis=1), jnp.concatenate(right, axis=0)
        )
    for k in range(near):

        @pl.when(jnp.bitwise_and(jnp.right_shift(tile, k), 1) == 1)
        def _(k=k):
            out[...] += dot(terms, hot[k]) * dot(span_queries, slots[k].astype(jnp.bfloat16))

    scaled = (inputs[...].astype(jnp.float32) * dot(terms, hot[near])).astype(jnp.bfloat16)
    now[...] = dot(keys[...], scaled, ((0,), (0,)))
    for k in range(near):
        ready = jnp.bitwise_and(tile, 2**k - 1) == 2**k - 1
        full = jnp.bitwise_and(jnp.right_shift(tile, k), 1) == 1

        @pl.when(jnp.logical_and(ready, full))
        def _(k=k):
            row = head_row(jnp.exp(since[k] + total)[:, :1], width, head_dim)
            now[...] += slots[k] * row

        @pl.when(jnp.logical_and(ready, jnp.logical_not(full)))
        def _(k=k):
            slots[k] = now[...]


def gate_kernel(head_dim, heads, first, me, local, coefs, queries, states, gate, *rest):
    outs, hot = rest[:-1], rest[-1]
    step = pl.program_id(0)
    far, _, width = states.shape

    @pl.when(step == 0)
    def _():
        for m in range(far):
            hot[m] = spread(first + m * heads, width, head_dim)

    total = local[...]
    for m in range(far):
        total += dot(coefs[...], hot[m]) * dot(queries[...], states[m])
    opened = gate[...].astype(jnp.float32)
    gated = (total * (0.5 * opened) * (1.0 + jnp.tanh(0.5 * opened))).astype(jnp.bfloat16)
    if len(outs) == 1:
        outs[0][0] = gated
        return
    for index, out in enumerate(outs):

        @pl.when(step == index)
        def _(out=out):
            out[...] = gated


def norm_kernel(sources, me, gain, *rest):
    out = rest[-1]
    step = pl.program_id(0)

    def write(blocks):
        blocks = [block.astype(jnp.float32) for block in blocks]
        count = sum(block.shape[1] for block in blocks)
        square = sum(jnp.sum(block * block, axis=1, keepdims=True) for block in blocks)
        scale = lax.rsqrt(square / count + 1e-05)
        at = 0
        for block in blocks:
            end = at + block.shape[1]
            out[:, at:end] = (block * scale * gain[:, at:end]).astype(out.dtype)
            at = end

    if sources is None:
        parts = rest[:-1]
        write([part[index] for index in range(parts[0].shape[0]) for part in parts])
        return
    for index, places in enumerate(sources):

        @pl.when(step == index)
        def _(places=places):
            write([rest[place][...] for place in places])


def params(limit):
    return pltpu.CompilerParams(vmem_limit_bytes=limit * MIB)


def body(values, gate_z, b_keys, c_queries, log_decay, level_weight, doc_start, norm_gain):
    tokens, width = values.shape
    heads_here = log_decay.shape[1]
    head_dim = width // heads_here
    state_size = b_keys.shape[2]
    tiles = tokens // TILE
    near = tiles.bit_length() - 1
    seq_count = lax.axis_size("seq")
    far = seq_count.bit_length() - 1
    head_count = lax.axis_size("head")
    head_index = lax.axis_index("head")
    group_index = head_index * heads_here // (MIXER_HEADS // GROUPS)
    key_rows = lax.dynamic_index_in_dim(b_keys, group_index, 1, keepdims=False)
    query_rows = lax.dynamic_index_in_dim(c_queries, group_index, 1, keepdims=False)
    decay = jnp.transpose(log_decay)
    weight = jnp.transpose(level_weight, (2, 1, 0))
    heads = SUBLANES
    if heads_here < heads:
        short = heads - heads_here
        decay = jnp.pad(decay, ((0, short), (0, 0)))
        weight = jnp.pad(weight, ((0, 0), (0, short), (0, 0)), constant_values=1.0)
    chunks = max(1, heads_here // heads)
    part = width // chunks
    levels = weight.shape[0]
    smem = pl.BlockSpec(memory_space=pltpu.SMEM)

    def state_call(c):
        return pl.pallas_call(
            functools.partial(state_kernel, head_dim),
            grid=(1,),
            in_specs=[
                smem,
                pl.BlockSpec((heads, tokens), lambda i: (c, 0)),
                pl.BlockSpec((tokens, state_size), lambda i: (0, 0)),
                pl.BlockSpec((tokens, part), lambda i: (0, c)),
            ],
            out_specs=[
                pl.BlockSpec((state_size, part), lambda i: (0, 0)),
                pl.BlockSpec((state_size, part), lambda i: (0, 0)),
                pl.BlockSpec((SUBLANES, part), lambda i: (0, 0)),
            ],
            out_shape=[
                jax.ShapeDtypeStruct((state_size, part), jnp.float32),
                jax.ShapeDtypeStruct((state_size, part), jnp.bfloat16),
                jax.ShapeDtypeStruct((SUBLANES, part), jnp.float32),
            ],
            compiler_params=params(16),
            cost_estimate=pl.CostEstimate(
                flops=4 * tokens * state_size * part, bytes_accessed=3 * tokens * part, transcendentals=0
            ),
            name="block_state",
        )(doc_start, decay, key_rows, values)

    def local_call(c):
        return pl.pallas_call(
            functools.partial(local_kernel, head_dim, far),
            grid=(tiles,),
            in_specs=[
                smem,
                pl.BlockSpec((heads, TILE), lambda i: (c, i)),
                pl.BlockSpec((levels, heads, TILE), lambda i: (0, c, i)),
                pl.BlockSpec((TILE, part), lambda i: (i, c)),
                pl.BlockSpec((TILE, state_size), lambda i: (i, 0)),
                pl.BlockSpec((TILE, state_size), lambda i: (i, 0)),
            ],
            out_specs=[
                pl.BlockSpec((TILE, part), lambda i: (i, 0)),
                pl.BlockSpec((TILE, 2 * LANES), lambda i: (i, 0)),
            ],
            out_shape=[
                jax.ShapeDtypeStruct((tokens, part), jnp.float32),
                jax.ShapeDtypeStruct((tokens, 2 * LANES), jnp.bfloat16),
            ],
            scratch_shapes=[
                pltpu.VMEM((near, state_size, part), jnp.float32),
                pltpu.VMEM((near + 1, heads, TILE), jnp.float32),
                pltpu.VMEM((near + 1, 2 * LANES, part), jnp.bfloat16),
                pltpu.VMEM((state_size, part), jnp.float32),
            ],
            compiler_params=params(16),
            cost_estimate=pl.CostEstimate(
                flops=16 * tokens * state_size * part, bytes_accessed=12 * tokens * part, transcendentals=0
            ),
            name="local_mixer",
        )(doc_start, decay, weight, values, query_rows, key_rows)

    rows = tokens // head_count
    direct = head_count == GROUPS
    me = jnp.reshape(head_index, (1,)).astype(jnp.int32)

    def gate_call(c, local, coefs, states):
        if direct:
            place = lambda i, s: jnp.bitwise_xor(i, s[0])
            out_specs = [pl.BlockSpec((rows, part), lambda i, s: (0, 0))] * head_count
            out_shape = [jax.ShapeDtypeStruct((rows, part), jnp.bfloat16)] * head_count
        else:
            place = lambda i, s: i
            out_specs = [pl.BlockSpec((1, rows, part), lambda i, s: (i, 0, 0))]
            out_shape = [jax.ShapeDtypeStruct((head_count, rows, part), jnp.bfloat16)]
        return pl.pallas_call(
            functools.partial(gate_kernel, head_dim, heads, (near + 3) * heads),
            grid_spec=pltpu.PrefetchScalarGridSpec(
                num_scalar_prefetch=1,
                grid=(head_count,),
                in_specs=[
                    pl.BlockSpec((rows, part), lambda i, s: (place(i, s), 0)),
                    pl.BlockSpec((rows, 2 * LANES), lambda i, s: (place(i, s), 0)),
                    pl.BlockSpec((rows, state_size), lambda i, s: (place(i, s), 0)),
                    pl.BlockSpec((far, state_size, part), lambda i, s: (0, 0, 0)),
                    pl.BlockSpec((rows, part), lambda i, s: (place(i, s), c)),
                ],
                out_specs=out_specs,
                scratch_shapes=[pltpu.VMEM((far, 2 * LANES, part), jnp.bfloat16)],
            ),
            out_shape=out_shape,
            compiler_params=params(16),
            cost_estimate=pl.CostEstimate(
                flops=4 * tokens * state_size * part, bytes_accessed=8 * tokens * part, transcendentals=0
            ),
            name="far_and_gate",
        )(me, local, coefs, query_rows, states, gate_z)

    owns, throughs, messages = zip(*[(s, t[:1], m) for s, m, t in map(state_call, range(chunks))])
    owns = list(owns)
    carried = [[None] * far for _ in range(chunks)]
    for bit in range(far):
        size = 2**bit
        for c in range(chunks):
            moving = messages[c] if bit == 0 else owns[c].astype(jnp.bfloat16)
            arrived = None
            for hop in range(1, size + 1):
                source = [base + size + hop - 2 for base in range(0, seq_count, 2 * size)]
                got = lax.ppermute(moving, "seq", [(s, s + 1) for s in source])
                arrived = got if arrived is None else arrived + got
                passed = got.astype(jnp.float32) * throughs[c]
                moving = passed.astype(jnp.bfloat16)
            carried[c][bit] = arrived
            owns[c] = owns[c] + passed
    locals_ = [local_call(c) for c in range(chunks)]

    pieces = []
    for c in range(chunks):
        local, coefs = locals_[c]
        out = gate_call(c, local, coefs, jnp.stack(carried[c]))
        if direct:
            got = [out[0]] + [None] * (head_count - 1)
            for apart in sorted(range(1, head_count), key=lambda k: -k.bit_count() * 8 - k):
                pairs = [(source, source ^ apart) for source in range(head_count)]
                got[apart] = lax.ppermute(out[apart], "head", pairs)
            pieces.append(got)
        else:
            pieces.append(lax.all_to_all(out[0], "head", split_axis=0, concat_axis=0))

    gain = jnp.reshape(norm_gain, (1, -1))
    group_width = width * head_count // GROUPS
    if direct:
        flat = [piece for got in pieces for piece in got]
        sources = [[c * head_count + k for c in range(chunks)] for k in range(head_count)]
        column = lambda i, s: (0, jnp.bitwise_xor(i, s[0]))
        in_specs = [pl.BlockSpec((rows, part), lambda i, s: (0, 0))] * len(flat)
    else:
        flat = pieces
        sources = None
        per_group = max(1, group_width // width)
        column = lambda i, s: (0, i)
        in_specs = [pl.BlockSpec((per_group, rows, part), lambda i, s: (i, 0, 0))] * len(flat)
    return pl.pallas_call(
        functools.partial(norm_kernel, sources),
        grid_spec=pltpu.PrefetchScalarGridSpec(
            num_scalar_prefetch=1,
            grid=(GROUPS,),
            in_specs=[pl.BlockSpec((1, group_width), column)] + in_specs,
            out_specs=pl.BlockSpec((rows, group_width), column),
        ),
        out_shape=jax.ShapeDtypeStruct((rows, width * head_count), jnp.bfloat16),
        compiler_params=params(16),
        cost_estimate=pl.CostEstimate(
            flops=8 * tokens * width, bytes_accessed=4 * tokens * width, transcendentals=0
        ),
        name="norm_rows",
    )(me, gain, *flat)


def solution(mesh):
    in_specs = (
        P("seq", "head"),
        P("seq", "head"),
        P("seq", None, None),
        P("seq", None, None),
        P("seq", "head"),
        P("seq", "head", None),
        P(),
        P(),
    )
    out_specs = P(("seq", "head"), None)
    return jax.shard_map(body, mesh=mesh, in_specs=in_specs, out_specs=out_specs, check_vma=False)
```

profile of v0, /device:TPU:25, one launch (start us, length us, event | category | flops | bytes accessed | tf_op | source)
XLA Modules:
  0.0 97.0 jit_solution(3892414850128379696)
XLA Ops:
  0.0 1.6 %copy-done = bf16[1024,8,128]{2,1,0:T(8,128)(2,1)S(1)} copy-done((bf16[1024,8,128]{2,1,0:T(8,128)(2,1)S(1)}, bf16[1024,8,128]{2,1,0:T(8,128)(2,1)}, u32[]{:S(2)}) %copy-start) | copy-done | bytes 2097176
  2.2 1.6 %copy-done.1 = bf16[1024,1024]{1,0:T(8,128)(2,1)S(1)} copy-done((bf16[1024,1024]{1,0:T(8,128)(2,1)S(1)}, bf16[1024,1024]{1,0:T(8,128)(2,1)}, u32[]{:S(2)}) %copy-start.1) | copy-done | bytes 2097176
  5.3 2.4 %block_state.3 = (f32[128,512]{1,0:T(8,128)S(1)}, bf16[128,512]{1,0:T(8,128)(2,1)S(1)}, f32[8,512]{1,0:T(8,128)S(1)}) custom-call(s32[64]{0:T(128)S(1)} %copy-done.7, f32[16,1024]{1,0:T(8,128)S(1)} %bitcast.26, bf16[1024,128]{1,0:T(8,128)(2,1)S(1)} %bitcast.18, bf16[1024,1024]{1,0:T(8,128)(2,1)S(1)} %copy-done.1), custom_call_target="tpu_custom_call" | custom-call | flops 268435456 | bytes 1572864 | tf_op jit(solution)/shard_map/block_state/pallas_call | solution.py:259
  7.7 1.4 %collective-permute-start.10 = (bf16[128,512]{1,0:T(8,128)(2,1)S(1)}, bf16[128,512]{1,0:T(8,128)(2,1)S(1)}, u32[]{:S(2)}, u32[]{:S(2)}) collective-permute-start(bf16[128,512]{1,0:T(8,128)(2,1)S(1)} %get-tuple-element.46), channel_id=1, source_target_pairs={{0,8},{16,24},{1,9},{17,25},{2,10},{18,26},{3,11},{19,27},{4,12},{... | collective-permute-start | bytes 393224 | tf_op jit(solution)/shard_map/ppermute | solution.py:364
  9.1 2.4 %block_state.2 = (f32[128,512]{1,0:T(8,128)S(1)}, bf16[128,512]{1,0:T(8,128)(2,1)S(1)}, f32[8,512]{1,0:T(8,128)S(1)}) custom-call(s32[64]{0:T(128)S(1)} %copy-done.7, f32[16,1024]{1,0:T(8,128)S(1)} %bitcast.27, bf16[1024,128]{1,0:T(8,128)(2,1)S(1)} %bitcast.19, bf16[1024,1024]{1,0:T(8,128)(2,1)S(1)} %copy-done.1), custom_call_target="tpu_custom_call" | custom-call | flops 268435456 | bytes 1572864 | tf_op jit(solution)/shard_map/block_state/pallas_call | solution.py:259
  11.5 1.3 %collective-permute-start = (bf16[128,512]{1,0:T(8,128)(2,1)S(1)}, bf16[128,512]{1,0:T(8,128)(2,1)S(1)}, u32[]{:S(2)}, u32[]{:S(2)}) collective-permute-start(bf16[128,512]{1,0:T(8,128)(2,1)S(1)} %get-tuple-element.33), channel_id=1, source_target_pairs={{0,8},{16,24},{1,9},{17,25},{2,10},{18,26},{3,11},{19,27},{4,12},{... | collective-permute-start | bytes 393224 | tf_op jit(solution)/shard_map/ppermute | solution.py:364
  12.8 2.1 %constant_dynamic-slice_fusion.1 = bf16[1024,1,128]{2,1,0:T(2,128)(2,1)S(1)} fusion(bf16[1024,8,128]{2,1,0:T(8,128)(2,1)} %param.11, s32[]{:T(128)S(6)} %select_n.11), kind=kLoop, calls=%fused_computation.11 | loop fusion | bytes 524292 | tf_op jit(solution)/shard_map/jit(dynamic_index_in_dim)/dynamic_slice | solution.py:245
  15.0 15.3 %local_mixer.3 = (f32[1024,512]{1,0:T(8,128)S(1)}, bf16[1024,256]{1,0:T(8,128)(2,1)S(1)}) custom-call(s32[64]{0:T(128)S(1)} %copy-done.8, f32[16,1024]{1,0:T(8,128)S(1)} %bitcast.28, f32[7,16,1024]{2,1,0:T(8,128)S(1)} %bitcast.31, bf16[1024,1024]{1,0:T(8,128)(2,1)S(1)} %copy-done.2, bf16[1024,128]{1,0:T(8,128)(2,1)S(1)} %bitcast.22, ...), custom_call_target="tpu_custom_call" | custom-call | flops 1073741824 | bytes 6291456 | tf_op jit(solution)/shard_map/local_mixer/pallas_call | solution.py:286
  30.4 15.3 %local_mixer.2 = (f32[1024,512]{1,0:T(8,128)S(1)}, bf16[1024,256]{1,0:T(8,128)(2,1)S(1)}) custom-call(s32[64]{0:T(128)S(1)} %copy-done.8, f32[16,1024]{1,0:T(8,128)S(1)} %bitcast.29, f32[7,16,1024]{2,1,0:T(8,128)S(1)} %bitcast.32, bf16[1024,1024]{1,0:T(8,128)(2,1)S(1)} %copy-done.2, bf16[1024,128]{1,0:T(8,128)(2,1)S(1)} %bitcast.23, ...), custom_call_target="tpu_custom_call" | custom-call | flops 1073741824 | bytes 6291456 | tf_op jit(solution)/shard_map/local_mixer/pallas_call | solution.py:286
  47.3 1.3 %collective-permute-start.12 = (bf16[128,512]{1,0:T(8,128)(2,1)S(1)}, bf16[128,512]{1,0:T(8,128)(2,1)S(1)}, u32[]{:S(2)}, u32[]{:S(2)}) collective-permute-start(bf16[128,512]{1,0:T(8,128)(2,1)S(1)} %multiply_convert_fusion), channel_id=1, source_target_pairs={{16,24},{17,25},{18,26},{19,27},{20,28},{21,29},{22,30},{23,31}} | collective-permute-start | bytes 393224 | tf_op jit(solution)/shard_map/ppermute | solution.py:364
  48.7 1.3 %collective-permute-start.2 = (bf16[128,512]{1,0:T(8,128)(2,1)S(1)}, bf16[128,512]{1,0:T(8,128)(2,1)S(1)}, u32[]{:S(2)}, u32[]{:S(2)}) collective-permute-start(bf16[128,512]{1,0:T(8,128)(2,1)S(1)} %multiply_convert_fusion.1), channel_id=1, source_target_pairs={{16,24},{17,25},{18,26},{19,27},{20,28},{21,29},{22,30},{23,31}} | collective-permute-start | bytes 393224 | tf_op jit(solution)/shard_map/ppermute | solution.py:364
  50.0 7.4 %collective-permute-done.12 = bf16[128,512]{1,0:T(8,128)(2,1)S(1)} collective-permute-done((bf16[128,512]{1,0:T(8,128)(2,1)S(1)}, bf16[128,512]{1,0:T(8,128)(2,1)S(1)}, u32[]{:S(2)}, u32[]{:S(2)}) %collective-permute-start.12) | collective-permute-done | bytes 131104 | tf_op jit(solution)/shard_map/ppermute | solution.py:364
  57.4 3.4 %far_and_gate.3 = (bf16[128,512]{1,0:T(8,128)(2,1)S(1)}, bf16[128,512]{1,0:T(8,128)(2,1)S(1)}, bf16[128,512]{1,0:T(8,128)(2,1)S(1)}, bf16[128,512]{1,0:T(8,128)(...) custom-call(s32[1]{0:T(128)} %bitcast.me, ...), custom_call_target="tpu_custom_call" | custom-call | flops 268435456 | bytes 4194304 | tf_op jit(solution)/shard_map/far_and_gate/pallas_call | solution.py:331
  60.9 5.2 %collective-permute-start.13 = (bf16[128,512]{1,0:T(8,128)(2,1)S(1)}, bf16[128,512]{1,0:T(8,128)(2,1)S(1)}, u32[]{:S(2)}, u32[]{:S(2)}) collective-permute-start(bf16[128,512]{1,0:T(8,128)(2,1)S(1)} %get-tuple-element.50), channel_id=1, source_target_pairs={{0,1},{1,0},{2,3},{3,2},{4,5},{5,4},{6,7},{7,6},{8,9},{9,8},{10,11... | collective-permute-start | bytes 393224 | tf_op jit(solution)/shard_map/ppermute | solution.py:380
  67.8 1.2 %collective-permute-start.16 = (bf16[128,512]{1,0:T(8,128)(2,1)S(1)}, bf16[128,512]{1,0:T(8,128)(2,1)S(1)}, u32[]{:S(2)}, u32[]{:S(2)}) collective-permute-start(bf16[128,512]{1,0:T(8,128)(2,1)S(1)} %get-tuple-element.53), channel_id=1, source_target_pairs={{0,4},{1,5},{2,6},{3,7},{4,0},{5,1},{6,2},{7,3},{8,12},{9,13},{10,... | collective-permute-start | bytes 393224 | tf_op jit(solution)/shard_map/ppermute | solution.py:380
  69.6 3.4 %far_and_gate.2 = (bf16[128,512]{1,0:T(8,128)(2,1)S(1)}, bf16[128,512]{1,0:T(8,128)(2,1)S(1)}, bf16[128,512]{1,0:T(8,128)(2,1)S(1)}, bf16[128,512]{1,0:T(8,128)(...) custom-call(s32[1]{0:T(128)} %bitcast.me, ...), custom_call_target="tpu_custom_call" | custom-call | flops 268435456 | bytes 4194304 | tf_op jit(solution)/shard_map/far_and_gate/pallas_call | solution.py:331
  73.1 2.2 %collective-permute-start.18 = (bf16[128,512]{1,0:T(8,128)(2,1)S(1)}, bf16[128,512]{1,0:T(8,128)(2,1)S(1)}, u32[]{:S(2)}, u32[]{:S(2)}) collective-permute-start(bf16[128,512]{1,0:T(8,128)(2,1)S(1)} %get-tuple-element.55), channel_id=1, source_target_pairs={{0,6},{1,7},{2,4},{3,5},{4,2},{5,3},{6,0},{7,1},{8,14},{9,15},{10,... | collective-permute-start | bytes 393224 | tf_op jit(solution)/shard_map/ppermute | solution.py:380
  80.3 2.1 %collective-permute-done.19.rest_15_ = bf16[128,512]{1,0:T(8,128)(2,1)S(1)} collective-permute-done((bf16[128,512]{1,0:T(8,128)(2,1)S(1)}, bf16[128,512]{1,0:T(8,128)(2,1)S(1)}, u32[]{:S(2)}, u32[]{:S(2)}) %collective-permute-start.19) | collective-permute-done | bytes 131104 | tf_op jit(solution)/shard_map/ppermute | solution.py:380
  83.4 1.2 %collective-permute-start.8 = (bf16[128,512]{1,0:T(8,128)(2,1)S(1)}, bf16[128,512]{1,0:T(8,128)(2,1)S(1)}, u32[]{:S(2)}, u32[]{:S(2)}) collective-permute-start(bf16[128,512]{1,0:T(8,128)(2,1)S(1)} %get-tuple-element.42), channel_id=1, source_target_pairs={{0,6},{1,7},{2,4},{3,5},{4,2},{5,3},{6,0},{7,1},{8,14},{9,15},{10,... | collective-permute-start | bytes 393224 | tf_op jit(solution)/shard_map/ppermute | solution.py:380
  84.8 2.3 %collective-permute-start.9 = (bf16[128,512]{1,0:T(8,128)(2,1)S(1)}, bf16[128,512]{1,0:T(8,128)(2,1)S(1)}, u32[]{:S(2)}, u32[]{:S(2)}) collective-permute-start(bf16[128,512]{1,0:T(8,128)(2,1)S(1)} %get-tuple-element.43), channel_id=1, source_target_pairs={{0,7},{1,6},{2,5},{3,4},{4,3},{5,2},{6,1},{7,0},{8,15},{9,14},{10,... | collective-permute-start | bytes 393224 | tf_op jit(solution)/shard_map/ppermute | solution.py:380
  87.1 1.4 %collective-permute-done.5.rest_3_ = bf16[128,512]{1,0:T(8,128)(2,1)S(1)} collective-permute-done((bf16[128,512]{1,0:T(8,128)(2,1)S(1)}, bf16[128,512]{1,0:T(8,128)(2,1)S(1)}, u32[]{:S(2)}, u32[]{:S(2)}) %collective-permute-start.5) | collective-permute-done | bytes 131104 | tf_op jit(solution)/shard_map/ppermute | solution.py:380
  88.5 1.9 %collective-permute-done.8.rest_6_ = bf16[128,512]{1,0:T(8,128)(2,1)S(1)} collective-permute-done((bf16[128,512]{1,0:T(8,128)(2,1)S(1)}, bf16[128,512]{1,0:T(8,128)(2,1)S(1)}, u32[]{:S(2)}, u32[]{:S(2)}) %collective-permute-start.8) | collective-permute-done | bytes 131104 | tf_op jit(solution)/shard_map/ppermute | solution.py:380
  90.4 2.9 %collective-permute-done.9.rest_7_ = bf16[128,512]{1,0:T(8,128)(2,1)S(1)} collective-permute-done((bf16[128,512]{1,0:T(8,128)(2,1)S(1)}, bf16[128,512]{1,0:T(8,128)(2,1)S(1)}, u32[]{:S(2)}, u32[]{:S(2)}) %collective-permute-start.9) | collective-permute-done | bytes 131104 | tf_op jit(solution)/shard_map/ppermute | solution.py:380
  93.3 3.8 %norm_rows.1 = bf16[128,8192]{1,0:T(8,128)(2,1)} custom-call(s32[1]{0:T(128)} %bitcast.me, f32[1,8192]{1,0:T(1,128)S(1)} %bitcast.30, bf16[128,512]{1,0:T(8,128)(2,1)S(1)} %get-tuple-element.36.rest_0_, bf16[128,512]{1,0:T(8,128)(2,1)S(1)} %collective-permute-done.3.rest_1_, bf16[128,512]{1,0:T(8,128)(2,1)S(1)} %collective-permute-done.4.rest_2_, ...), custom_call_target="tpu_custom_call" | custom-call | flops 8388608 | bytes 4194304 | tf_op jit(solution)/shard_map/norm_rows/pallas_call | solution.py:398
  (57 shorter events, 12.3 us)
Async XLA Ops:
  7.7 7.4 %copy-start.2 = (bf16[1024,1024]{1,0:T(8,128)(2,1)S(1)}, bf16[1024,1024]{1,0:T(8,128)(2,1)}, u32[]{:S(2)}) copy-start(bf16[1024,1024]{1,0:T(8,128)(2,1)} %inputs.7) | copy-start | bytes 6291460
  7.7 7.3 %copy-start.5 = (f32[1024,16]{0,1:T(8,128)S(1)}, f32[1024,16]{0,1:T(8,128)}, u32[]{:S(2)}) copy-start(f32[1024,16]{0,1:T(8,128)} %param.12) | copy-start | bytes 196612
  7.7 38.0 %collective-permute-start.10 = (bf16[128,512]{1,0:T(8,128)(2,1)S(1)}, bf16[128,512]{1,0:T(8,128)(2,1)S(1)}, u32[]{:S(2)}, u32[]{:S(2)}) collective-permute-start(bf16[128,512]{1,0:T(8,128)(2,1)S(1)} %get-tuple-element.46), channel_id=1, source_target_pairs={{0,8},{16,24},{1,9},{17,25},{2,10},{18,26},{3,11},{19,27},{4,12},{... | collective-permute-start | bytes 393224 | tf_op jit(solution)/shard_map/ppermute | solution.py:364
  11.5 35.1 %collective-permute-start = (bf16[128,512]{1,0:T(8,128)(2,1)S(1)}, bf16[128,512]{1,0:T(8,128)(2,1)S(1)}, u32[]{:S(2)}, u32[]{:S(2)}) collective-permute-start(bf16[128,512]{1,0:T(8,128)(2,1)S(1)} %get-tuple-element.33), channel_id=1, source_target_pairs={{0,8},{16,24},{1,9},{17,25},{2,10},{18,26},{3,11},{19,27},{4,12},{... | collective-permute-start | bytes 393224 | tf_op jit(solution)/shard_map/ppermute | solution.py:364
  45.7 11.7 %copy-start.3 = (bf16[1024,1024]{1,0:T(8,128)(2,1)S(1)}, bf16[1024,1024]{1,0:T(8,128)(2,1)}, u32[]{:S(2)}) copy-start(bf16[1024,1024]{1,0:T(8,128)(2,1)} %gate.3) | copy-start | bytes 6291460
  45.8 1.5 %collective-permute-start.11 = (bf16[128,512]{1,0:T(8,128)(2,1)S(1)}, bf16[128,512]{1,0:T(8,128)(2,1)S(1)}, u32[]{:S(2)}, u32[]{:S(2)}) collective-permute-start(bf16[128,512]{1,0:T(8,128)(2,1)S(1)} %add_convert_fusion), channel_id=1, source_target_pairs={{8,16},{9,17},{10,18},{11,19},{12,20},{13,21},{14,22},{15,23}} | collective-permute-start | bytes 393224 | tf_op jit(solution)/shard_map/ppermute | solution.py:364
  46.6 2.0 %collective-permute-start.1 = (bf16[128,512]{1,0:T(8,128)(2,1)S(1)}, bf16[128,512]{1,0:T(8,128)(2,1)S(1)}, u32[]{:S(2)}, u32[]{:S(2)}) collective-permute-start(bf16[128,512]{1,0:T(8,128)(2,1)S(1)} %add_convert_fusion.1), channel_id=1, source_target_pairs={{8,16},{9,17},{10,18},{11,19},{12,20},{13,21},{14,22},{15,23}} | collective-permute-start | bytes 393224 | tf_op jit(solution)/shard_map/ppermute | solution.py:364
  47.3 10.0 %collective-permute-start.12 = (bf16[128,512]{1,0:T(8,128)(2,1)S(1)}, bf16[128,512]{1,0:T(8,128)(2,1)S(1)}, u32[]{:S(2)}, u32[]{:S(2)}) collective-permute-start(bf16[128,512]{1,0:T(8,128)(2,1)S(1)} %multiply_convert_fusion), channel_id=1, source_target_pairs={{16,24},{17,25},{18,26},{19,27},{20,28},{21,29},{22,30},{23,31}} | collective-permute-start | bytes 393224 | tf_op jit(solution)/shard_map/ppermute | solution.py:364
  48.7 20.3 %collective-permute-start.2 = (bf16[128,512]{1,0:T(8,128)(2,1)S(1)}, bf16[128,512]{1,0:T(8,128)(2,1)S(1)}, u32[]{:S(2)}, u32[]{:S(2)}) collective-permute-start(bf16[128,512]{1,0:T(8,128)(2,1)S(1)} %multiply_convert_fusion.1), channel_id=1, source_target_pairs={{16,24},{17,25},{18,26},{19,27},{20,28},{21,29},{22,30},{23,31}} | collective-permute-start | bytes 393224 | tf_op jit(solution)/shard_map/ppermute | solution.py:364
  60.9 12.2 %collective-permute-start.13 = (bf16[128,512]{1,0:T(8,128)(2,1)S(1)}, bf16[128,512]{1,0:T(8,128)(2,1)S(1)}, u32[]{:S(2)}, u32[]{:S(2)}) collective-permute-start(bf16[128,512]{1,0:T(8,128)(2,1)S(1)} %get-tuple-element.50), channel_id=1, source_target_pairs={{0,1},{1,0},{2,3},{3,2},{4,5},{5,4},{6,7},{7,6},{8,9},{9,8},{10,11... | collective-permute-start | bytes 393224 | tf_op jit(solution)/shard_map/ppermute | solution.py:380
  66.0 9.2 %collective-permute-start.14 = (bf16[128,512]{1,0:T(8,128)(2,1)S(1)}, bf16[128,512]{1,0:T(8,128)(2,1)S(1)}, u32[]{:S(2)}, u32[]{:S(2)}) collective-permute-start(bf16[128,512]{1,0:T(8,128)(2,1)S(1)} %get-tuple-element.51), channel_id=1, source_target_pairs={{0,2},{1,3},{2,0},{3,1},{4,6},{5,7},{6,4},{7,5},{8,10},{9,11},{10,... | collective-permute-start | bytes 393224 | tf_op jit(solution)/shard_map/ppermute | solution.py:380
  67.3 8.4 %collective-permute-start.15 = (bf16[128,512]{1,0:T(8,128)(2,1)S(1)}, bf16[128,512]{1,0:T(8,128)(2,1)S(1)}, u32[]{:S(2)}, u32[]{:S(2)}) collective-permute-start(bf16[128,512]{1,0:T(8,128)(2,1)S(1)} %get-tuple-element.52), channel_id=1, source_target_pairs={{0,3},{1,2},{2,1},{3,0},{4,7},{5,6},{6,5},{7,4},{8,11},{9,10},{10,... | collective-permute-start | bytes 393224 | tf_op jit(solution)/shard_map/ppermute | solution.py:380
  67.8 8.1 %collective-permute-start.16 = (bf16[128,512]{1,0:T(8,128)(2,1)S(1)}, bf16[128,512]{1,0:T(8,128)(2,1)S(1)}, u32[]{:S(2)}, u32[]{:S(2)}) collective-permute-start(bf16[128,512]{1,0:T(8,128)(2,1)S(1)} %get-tuple-element.53), channel_id=1, source_target_pairs={{0,4},{1,5},{2,6},{3,7},{4,0},{5,1},{6,2},{7,3},{8,12},{9,13},{10,... | collective-permute-start | bytes 393224 | tf_op jit(solution)/shard_map/ppermute | solution.py:380
  69.0 8.1 %collective-permute-start.17 = (bf16[128,512]{1,0:T(8,128)(2,1)S(1)}, bf16[128,512]{1,0:T(8,128)(2,1)S(1)}, u32[]{:S(2)}, u32[]{:S(2)}) collective-permute-start(bf16[128,512]{1,0:T(8,128)(2,1)S(1)} %get-tuple-element.54), channel_id=1, source_target_pairs={{0,5},{1,4},{2,7},{3,6},{4,1},{5,0},{6,3},{7,2},{8,13},{9,12},{10,... | collective-permute-start | bytes 393224 | tf_op jit(solution)/shard_map/ppermute | solution.py:380
  69.6 23.7 %copy-start.6 = (f32[8192]{0:T(1024)S(1)}, f32[8192]{0:T(1024)}, u32[]{:S(2)}) copy-start(f32[8192]{0:T(1024)} %param.15) | copy-start | bytes 98308
  73.1 6.0 %collective-permute-start.18 = (bf16[128,512]{1,0:T(8,128)(2,1)S(1)}, bf16[128,512]{1,0:T(8,128)(2,1)S(1)}, u32[]{:S(2)}, u32[]{:S(2)}) collective-permute-start(bf16[128,512]{1,0:T(8,128)(2,1)S(1)} %get-tuple-element.55), channel_id=1, source_target_pairs={{0,6},{1,7},{2,4},{3,5},{4,2},{5,3},{6,0},{7,1},{8,14},{9,15},{10,... | collective-permute-start | bytes 393224 | tf_op jit(solution)/shard_map/ppermute | solution.py:380
  75.3 7.1 %collective-permute-start.19 = (bf16[128,512]{1,0:T(8,128)(2,1)S(1)}, bf16[128,512]{1,0:T(8,128)(2,1)S(1)}, u32[]{:S(2)}, u32[]{:S(2)}) collective-permute-start(bf16[128,512]{1,0:T(8,128)(2,1)S(1)} %get-tuple-element.56), channel_id=1, source_target_pairs={{0,7},{1,6},{2,5},{3,4},{4,3},{5,2},{6,1},{7,0},{8,15},{9,14},{10,... | collective-permute-start | bytes 393224 | tf_op jit(solution)/shard_map/ppermute | solution.py:380
  75.7 7.7 %collective-permute-start.3 = (bf16[128,512]{1,0:T(8,128)(2,1)S(1)}, bf16[128,512]{1,0:T(8,128)(2,1)S(1)}, u32[]{:S(2)}, u32[]{:S(2)}) collective-permute-start(bf16[128,512]{1,0:T(8,128)(2,1)S(1)} %get-tuple-element.37), channel_id=1, source_target_pairs={{0,1},{1,0},{2,3},{3,2},{4,5},{5,4},{6,7},{7,6},{8,9},{9,8},{10,11... | collective-permute-start | bytes 393224 | tf_op jit(solution)/shard_map/ppermute | solution.py:380
  75.9 8.9 %collective-permute-start.4 = (bf16[128,512]{1,0:T(8,128)(2,1)S(1)}, bf16[128,512]{1,0:T(8,128)(2,1)S(1)}, u32[]{:S(2)}, u32[]{:S(2)}) collective-permute-start(bf16[128,512]{1,0:T(8,128)(2,1)S(1)} %get-tuple-element.38), channel_id=1, source_target_pairs={{0,2},{1,3},{2,0},{3,1},{4,6},{5,7},{6,4},{7,5},{8,10},{9,11},{10,... | collective-permute-start | bytes 393224 | tf_op jit(solution)/shard_map/ppermute | solution.py:380
  77.1 11.4 %collective-permute-start.5 = (bf16[128,512]{1,0:T(8,128)(2,1)S(1)}, bf16[128,512]{1,0:T(8,128)(2,1)S(1)}, u32[]{:S(2)}, u32[]{:S(2)}) collective-permute-start(bf16[128,512]{1,0:T(8,128)(2,1)S(1)} %get-tuple-element.39), channel_id=1, source_target_pairs={{0,3},{1,2},{2,1},{3,0},{4,7},{5,6},{6,5},{7,4},{8,11},{9,10},{10,... | collective-permute-start | bytes 393224 | tf_op jit(solution)/shard_map/ppermute | solution.py:380
  79.1 9.4 %collective-permute-start.6 = (bf16[128,512]{1,0:T(8,128)(2,1)S(1)}, bf16[128,512]{1,0:T(8,128)(2,1)S(1)}, u32[]{:S(2)}, u32[]{:S(2)}) collective-permute-start(bf16[128,512]{1,0:T(8,128)(2,1)S(1)} %get-tuple-element.40), channel_id=1, source_target_pairs={{0,4},{1,5},{2,6},{3,7},{4,0},{5,1},{6,2},{7,3},{8,12},{9,13},{10,... | collective-permute-start | bytes 393224 | tf_op jit(solution)/shard_map/ppermute | solution.py:380
  82.4 6.1 %collective-permute-start.7 = (bf16[128,512]{1,0:T(8,128)(2,1)S(1)}, bf16[128,512]{1,0:T(8,128)(2,1)S(1)}, u32[]{:S(2)}, u32[]{:S(2)}) collective-permute-start(bf16[128,512]{1,0:T(8,128)(2,1)S(1)} %get-tuple-element.41), channel_id=1, source_target_pairs={{0,5},{1,4},{2,7},{3,6},{4,1},{5,0},{6,3},{7,2},{8,13},{9,12},{10,... | collective-permute-start | bytes 393224 | tf_op jit(solution)/shard_map/ppermute | solution.py:380
  83.4 7.0 %collective-permute-start.8 = (bf16[128,512]{1,0:T(8,128)(2,1)S(1)}, bf16[128,512]{1,0:T(8,128)(2,1)S(1)}, u32[]{:S(2)}, u32[]{:S(2)}) collective-permute-start(bf16[128,512]{1,0:T(8,128)(2,1)S(1)} %get-tuple-element.42), channel_id=1, source_target_pairs={{0,6},{1,7},{2,4},{3,5},{4,2},{5,3},{6,0},{7,1},{8,14},{9,15},{10,... | collective-permute-start | bytes 393224 | tf_op jit(solution)/shard_map/ppermute | solution.py:380
  84.8 8.5 %collective-permute-start.9 = (bf16[128,512]{1,0:T(8,128)(2,1)S(1)}, bf16[128,512]{1,0:T(8,128)(2,1)S(1)}, u32[]{:S(2)}, u32[]{:S(2)}) collective-permute-start(bf16[128,512]{1,0:T(8,128)(2,1)S(1)} %get-tuple-element.43), channel_id=1, source_target_pairs={{0,7},{1,6},{2,5},{3,4},{4,3},{5,2},{6,1},{7,0},{8,15},{9,14},{10,... | collective-permute-start | bytes 393224 | tf_op jit(solution)/shard_map/ppermute | solution.py:380
  (6 other events, 19.4 us)
where the time goes:
time: 97.4 us; the launch traced here: 97 us
  Pallas kernels  46 us (47%)
  starting transfers between devices  26.1 us (27%)
  waiting for transfers between devices  17 us (17%)
  local copies, waits for them, and re-layouts  7.47 us (8%)
    pallas_call x2, Pallas kernels, local_call(): pl.pallas_call(functools.partial(local_kernel, head_dim, far), grid=(tile...  30.6 us
    ppermute x14, starting transfers between devices, body(): got[apart] = lax.ppermute(out[apart], 'head', pairs)  19.3 us
    ppermute x14, waiting for transfers between devices, body(): got[apart] = lax.ppermute(out[apart], 'head', pairs)  9.6 us
    ppermute x6, waiting for transfers between devices, body(): got = lax.ppermute(moving, 'seq', [(s, s + 1) for s in source])  7.38 us
    pallas_call x2, Pallas kernels, gate_call(): pl.pallas_call(functools.partial(gate_kernel, head_dim, heads, (near + 3)...  6.84 us
    ppermute x6, starting transfers between devices, body(): got = lax.ppermute(moving, 'seq', [(s, s + 1) for s in source])  6.77 us
    unnamed x22, local copies, waits for them, and re-layouts  4.78 us
    pallas_call x2, Pallas kernels, state_call(): pl.pallas_call(functools.partial(state_kernel, head_dim), grid=(1,), in_s...  4.75 us
  transfers between devices with their start and end apart: 20, of which 7 were waited for; matrix products, arithmetic and copies ran while one was open for 2% of the time, Pallas kernels for 41%

commit v1 on v0

v1 whole, which is shorter than its diff:
```python
import functools

import jax
import jax.numpy as jnp
from jax import lax
from jax.experimental import pallas as pl
from jax.experimental.pallas import tpu as pltpu
from jax.sharding import PartitionSpec as P

MIXER_HEADS = 128
GROUPS = 8
SPAN = 64
TILE = 2 * SPAN
LANES = 128
SUBLANES = 8
NEVER = -1e30
HIGHEST = lax.Precision.HIGHEST
MIB = 2**20


def dot(left, right, contract=((1,), (0,)), precision=None):
    return lax.dot_general(
        left, right, (contract, ((), ())), precision=precision, preferred_element_type=jnp.float32
    )


def iota(shape, axis):
    return lax.broadcasted_iota(jnp.int32, shape, axis)


def halves(coef):
    high = coef.astype(jnp.bfloat16)
    low = (coef - high.astype(jnp.float32)).astype(jnp.bfloat16)
    return jnp.concatenate([high, low], axis=1)


def spread(first, width, head_dim):
    row = jnp.bitwise_and(iota((2 * LANES, width), 0), LANES - 1)
    head = jnp.right_shift(iota((2 * LANES, width), 1), head_dim.bit_length() - 1)
    return jnp.where(row == head + first, 1.0, 0.0).astype(jnp.bfloat16)


def head_row(column, width, head_dim):
    shape = (column.shape[0], width)
    head = jnp.right_shift(iota(shape, 1), head_dim.bit_length() - 1)
    return jnp.sum(jnp.where(head == iota(shape, 0), column, 0.0), axis=0, keepdims=True)


def stack_rows(pieces):
    rows = sum(piece.shape[0] for piece in pieces)
    if rows < LANES:
        pieces = pieces + [jnp.zeros((LANES - rows, LANES), jnp.float32)]
    return jnp.transpose(jnp.concatenate(pieces, axis=0))


def tile_rows(decay):
    tiles = decay.shape[1] // TILE
    return jnp.concatenate([decay[:, b * TILE : (b + 1) * TILE] for b in range(tiles)], axis=0)


def resets(docs, tiles):
    first = lax.axis_index("seq") * (tiles * (TILE // SPAN))
    shut = [NEVER * docs[first + s].astype(jnp.float32) for s in range(tiles * (TILE // SPAN))]
    return [shut[2 * b : 2 * b + 2] for b in range(tiles)]


def state_kernel(
    head_dim, column, pieces, docs, decay, keys, values, state, message, through, inputs, arrived
):
    heads, tokens = decay.shape
    width = inputs.shape[1]
    tiles = tokens // TILE
    rows = tokens // pieces
    copies = [
        pltpu.make_async_copy(
            values.at[pl.ds(i * rows, rows), pl.ds(column, width)],
            inputs.at[pl.ds(i * rows, rows), :],
            arrived.at[i],
        )
        for i in range(pieces)
    ]
    for copy in copies:
        copy.start()
    shut = resets(docs, tiles)
    lane = iota((heads, TILE), 1)
    later = jnp.where(iota((TILE, TILE), 0) > iota((TILE, TILE), 1), 1.0, 0.0)
    stacked = tile_rows(decay)
    suffix = dot(stacked, later, precision=HIGHEST)
    totals = jnp.sum(stacked, axis=1, keepdims=True)
    after = jnp.zeros((heads, 1), jnp.float32)
    closed = jnp.float32(0.0)
    scales = [None] * tiles
    for b in reversed(range(tiles)):
        ends = jnp.where(lane < SPAN, closed + shut[b][1], closed)
        scales[b] = jnp.exp(suffix[b * heads : (b + 1) * heads] + after + ends)
        closed = closed + shut[b][1] + shut[b][0]
        after = after + totals[b * heads : (b + 1) * heads]
    terms = halves(stack_rows(scales))
    row = head_row(jnp.exp(after + closed), width, head_dim)
    through[...] = jnp.broadcast_to(row, through.shape)
    owner = jnp.right_shift(
        jnp.bitwise_and(iota((1, 2 * LANES), 1), LANES - 1), heads.bit_length() - 1
    )
    shape = (2 * LANES, width)
    same = jnp.bitwise_and(iota(shape, 0), heads - 1) == jnp.right_shift(
        iota(shape, 1), head_dim.bit_length() - 1
    )
    one_hot = jnp.where(same, 1.0, 0.0).astype(jnp.bfloat16)
    chosen = [
        terms * jnp.where(owner == b, 1.0, 0.0).astype(jnp.bfloat16) for b in range(tiles)
    ]
    total = jnp.zeros(state.shape, jnp.float32)
    for i in range(pieces):
        span = tiles // pieces
        scale = dot(jnp.concatenate(chosen[i * span : (i + 1) * span], axis=0), one_hot)
        copies[i].wait()
        scaled = inputs[i * rows : (i + 1) * rows, :].astype(jnp.float32) * scale
        total += dot(
            keys[i * rows : (i + 1) * rows, :], scaled.astype(jnp.bfloat16), ((0,), (0,))
        )
    state[...] = total
    message[...] = total.astype(jnp.bfloat16)


def local_kernel(
    head_dim, column, far, docs, decay, weight, values, queries, keys, follow, out, coefs
):
    del follow
    heads, tokens = decay.shape
    width = out.shape[1]
    tiles = tokens // TILE
    near = tiles.bit_length() - 1
    shut = resets(docs, tiles)
    lane = iota((heads, TILE), 1)
    upto = jnp.where(iota((TILE, TILE), 0) <= iota((TILE, TILE), 1), 1.0, 0.0)
    all_sums = dot(tile_rows(decay[...]), upto, precision=HIGHEST)
    causal = iota((TILE, TILE), 0) >= iota((TILE, TILE), 1)
    per_tile = LANES // head_dim
    lane_head = jnp.right_shift(iota((TILE, LANES), 1), head_dim.bit_length() - 1)
    shape = (LANES, heads * TILE)
    row, col = iota(shape, 0), iota(shape, 1)
    group = jnp.right_shift(row, heads.bit_length() - 1)
    fits = jnp.bitwise_and(row, heads - 1) == jnp.right_shift(col, TILE.bit_length() - 1)
    older = jnp.bitwise_and(col, TILE - 1) < SPAN
    low, high = jnp.where(older, 3, 0), jnp.where(older, 6, 3)
    place = fits & (group >= low) & (group < high)
    place = jnp.where(place, 1.0, 0.0).astype(jnp.bfloat16)
    hot = [spread((6 + i) * heads, width, head_dim) for i in range(near + 1)]

    totals, slots = [], [None] * near
    for b in range(tiles):
        tokens_here = slice(b * TILE, (b + 1) * TILE)
        sums = all_sums[b * heads : (b + 1) * heads]
        scale = [weight[level, :, tokens_here] for level in range(weight.shape[0])]
        last = jnp.broadcast_to(sums[:, TILE - 1 :], sums.shape)
        opened = sums + jnp.where(lane < SPAN, shut[b][0], shut[b][0] + shut[b][1])
        own = sums + jnp.log(scale[0])
        beside = jnp.where(lane < SPAN, own, sums + jnp.log(scale[1]) + shut[b][1])
        rows = []
        for value in (own, beside):
            for _ in range(3):
                term = value.astype(jnp.bfloat16).astype(jnp.float32)
                rows.append(term)
                value = value - term
        levels = [k for k in range(near) if (b >> k) & 1]
        for k in range(near):
            if k in levels:
                since = sum(totals[(b >> k) << k : b], jnp.zeros_like(sums))
                rows.append(jnp.exp(opened + since) * scale[2 + k])
            else:
                rows.append(jnp.zeros_like(sums))
        rows.append(jnp.exp(last - sums + jnp.where(lane < SPAN, shut[b][1], 0.0)))
        since = sum(totals, jnp.zeros_like(sums))
        rows += [jnp.exp(opened + since) * scale[2 + near + m] for m in range(far)]
        totals.append(last + (shut[b][0] + shut[b][1]))
        terms = halves(stack_rows(rows))
        coefs[tokens_here, :] = terms

        span_queries = queries[tokens_here, :]
        scores = jnp.where(causal, dot(span_queries, keys[tokens_here, :], ((1,), (1,))), 0.0)
        gaps = dot(terms[:, :LANES], place)
        block = values[tokens_here, column : column + width]
        parts = []
        for part in range(width // LANES):
            here = block[:, part * LANES : (part + 1) * LANES]
            left, right = [], []
            for inner in range(per_tile):
                head = part * per_tile + inner
                gap = gaps[:, head * TILE : (head + 1) * TILE] - sums[head : head + 1, :]
                left.append((jnp.exp(jnp.minimum(gap, 80.0)) * scores).astype(jnp.bfloat16))
                right.append(jnp.where(lane_head == inner, here, jnp.zeros_like(here)))
            parts.append(dot(jnp.concatenate(left, axis=1), jnp.concatenate(right, axis=0)))
        mixed = jnp.concatenate(parts, axis=1)
        for k in levels:
            mixed += dot(terms, hot[k]) * dot(span_queries, slots[k].astype(jnp.bfloat16))
        out[tokens_here, :] = mixed

        if b == tiles - 1:
            break
        scaled = (block.astype(jnp.float32) * dot(terms, hot[near])).astype(jnp.bfloat16)
        now = dot(keys[tokens_here, :], scaled, ((0,), (0,)))
        for k in range(near):
            if not (b >> k) & 1:
                slots[k] = now
                break
            since = sum(totals[(b >> k) << k :])
            now = now + slots[k] * head_row(jnp.exp(since)[:, :1], width, head_dim)


def gate_kernel(head_dim, heads, first, column, xor, me, local, coefs, queries, states, gate, *outs):
    count = len(outs) if xor else outs[0].shape[0]
    rows = local.shape[0] // count
    far, _, width = states.shape
    hot = [spread(first + m * heads, width, head_dim) for m in range(far)]
    arrived = [states[m] for m in range(far)]

    def rows_of(place):
        start = place * rows
        here = pl.ds(pl.multiple_of(start, rows), rows)
        total = local[here, :]
        for m in range(far):
            total += dot(coefs[here, :], hot[m]) * dot(queries[here, :], arrived[m])
        opened = 0.5 * gate[here, column : column + width].astype(jnp.float32)
        return (total * opened * (1.0 + jnp.tanh(opened))).astype(jnp.bfloat16)

    if xor:
        for index, out in enumerate(outs):
            out[...] = rows_of(jnp.bitwise_xor(me[0], index))
    else:

        @pl.loop(0, count)
        def _(index):
            outs[0][index] = rows_of(index)


def norm_kernel(sources, me, gain, *rest):
    out = rest[-1]
    step = pl.program_id(0)

    def write(blocks):
        blocks = [block.astype(jnp.float32) for block in blocks]
        count = sum(block.shape[1] for block in blocks)
        square = sum(jnp.sum(block * block, axis=1, keepdims=True) for block in blocks)
        scale = lax.rsqrt(square / count + 1e-05)
        at = 0
        for block in blocks:
            end = at + block.shape[1]
            out[:, at:end] = (block * scale * gain[:, at:end]).astype(out.dtype)
            at = end

    if sources is None:
        parts = rest[:-1]
        write([part[index] for index in range(parts[0].shape[0]) for part in parts])
        return
    for index, places in enumerate(sources):

        @pl.when(step == index)
        def _(places=places):
            write([rest[place][...] for place in places])


def params(limit):
    return pltpu.CompilerParams(vmem_limit_bytes=limit * MIB)


def body(values, gate_z, b_keys, c_queries, log_decay, level_weight, doc_start, norm_gain):
    tokens, width = values.shape
    heads_here = log_decay.shape[1]
    head_dim = width // heads_here
    state_size = b_keys.shape[2]
    tiles = tokens // TILE
    near = tiles.bit_length() - 1
    seq_count = lax.axis_size("seq")
    far = seq_count.bit_length() - 1
    head_count = lax.axis_size("head")
    head_index = lax.axis_index("head")
    group_index = head_index * heads_here // (MIXER_HEADS // GROUPS)
    key_rows = lax.dynamic_index_in_dim(b_keys, group_index, 1, keepdims=False)
    query_rows = lax.dynamic_index_in_dim(c_queries, group_index, 1, keepdims=False)
    decay = jnp.transpose(log_decay)
    weight = jnp.transpose(level_weight, (2, 1, 0))
    heads = SUBLANES
    if heads_here < heads:
        short = heads - heads_here
        decay = jnp.pad(decay, ((0, short), (0, 0)))
        weight = jnp.pad(weight, ((0, 0), (0, short), (0, 0)), constant_values=1.0)
    chunks = max(1, heads_here // heads)
    part = width // chunks
    levels = weight.shape[0]
    smem = pl.BlockSpec(memory_space=pltpu.SMEM)
    decays = [decay[c * heads : (c + 1) * heads] for c in range(chunks)]
    weights = [weight[:, c * heads : (c + 1) * heads] for c in range(chunks)]

    whole = pl.BlockSpec(memory_space=pltpu.VMEM)
    anywhere = pl.BlockSpec(memory_space=pl.ANY)

    def state_call(c):
        pieces = min(4, tiles)
        return pl.pallas_call(
            functools.partial(state_kernel, head_dim, c * part, pieces),
            in_specs=[smem, whole, whole, anywhere],
            out_specs=[whole, whole, whole],
            out_shape=[
                jax.ShapeDtypeStruct((state_size, part), jnp.float32),
                jax.ShapeDtypeStruct((state_size, part), jnp.bfloat16),
                jax.ShapeDtypeStruct((SUBLANES, part), jnp.float32),
            ],
            scratch_shapes=[
                pltpu.VMEM((tokens, part), jnp.bfloat16),
                pltpu.SemaphoreType.DMA((pieces,)),
            ],
            compiler_params=params(16),
            cost_estimate=pl.CostEstimate(
                flops=4 * tokens * state_size * part, bytes_accessed=3 * tokens * part, transcendentals=0
            ),
            name="block_state",
        )(doc_start, decays[c], key_rows, values)

    def local_call(c, follow):
        return pl.pallas_call(
            functools.partial(local_kernel, head_dim, c * part, far),
            in_specs=[smem, whole, whole, whole, whole, whole, anywhere],
            out_specs=[whole, whole],
            out_shape=[
                jax.ShapeDtypeStruct((tokens, part), jnp.float32),
                jax.ShapeDtypeStruct((tokens, 2 * LANES), jnp.bfloat16),
            ],
            compiler_params=params(16),
            cost_estimate=pl.CostEstimate(
                flops=16 * tokens * state_size * part, bytes_accessed=12 * tokens * part, transcendentals=0
            ),
            name="local_mixer",
        )(doc_start, decays[c], weights[c], values, query_rows, key_rows, follow)

    rows = tokens // head_count
    direct = head_count == GROUPS
    me = jnp.reshape(head_index, (1,)).astype(jnp.int32)

    def gate_call(c, local, coefs, states):
        if direct:
            out_shape = [jax.ShapeDtypeStruct((rows, part), jnp.bfloat16)] * head_count
        else:
            out_shape = [jax.ShapeDtypeStruct((head_count, rows, part), jnp.bfloat16)]
        return pl.pallas_call(
            functools.partial(gate_kernel, head_dim, heads, (near + 7) * heads, c * part, direct),
            in_specs=[smem, whole, whole, whole, whole, whole],
            out_specs=[whole] * len(out_shape),
            out_shape=out_shape,
            compiler_params=params(16),
            cost_estimate=pl.CostEstimate(
                flops=4 * tokens * state_size * part, bytes_accessed=8 * tokens * part, transcendentals=0
            ),
            name="far_and_gate",
        )(me, local, coefs, query_rows, states, gate_z)

    owns, throughs, messages = zip(*[(s, t[:1], m) for s, m, t in map(state_call, range(chunks))])
    owns = list(owns)
    carried = [[None] * far for _ in range(chunks)]
    locals_ = [local_call(0, messages[-1])]
    for bit in range(far):
        size = 2**bit
        for c in range(chunks):
            moving = messages[c] if bit == 0 else owns[c].astype(jnp.bfloat16)
            if bit == 1 and len(locals_) == c and c:
                locals_.append(local_call(c, moving))
            arrived = None
            for hop in range(1, size + 1):
                source = [base + size + hop - 2 for base in range(0, seq_count, 2 * size)]
                got = lax.ppermute(moving, "seq", [(s, s + 1) for s in source])
                arrived = got if arrived is None else arrived + got
                passed = got.astype(jnp.float32) * throughs[c]
                moving = passed.astype(jnp.bfloat16)
            carried[c][bit] = arrived
            owns[c] = owns[c] + passed
    for c in range(len(locals_), chunks):
        locals_.append(local_call(c, messages[-1]))

    pieces = []
    for c in range(chunks):
        local, coefs = locals_[c]
        out = gate_call(c, local, coefs, jnp.stack(carried[c]))
        if direct:
            got = [out[0]] + [None] * (head_count - 1)
            for apart in sorted(range(1, head_count), key=lambda k: -k.bit_count() * 8 - k):
                pairs = [(source, source ^ apart) for source in range(head_count)]
                got[apart] = lax.ppermute(out[apart], "head", pairs)
            pieces.append(got)
        else:
            pieces.append(lax.all_to_all(out[0], "head", split_axis=0, concat_axis=0))

    gain = jnp.reshape(norm_gain, (1, -1))
    group_width = width * head_count // GROUPS
    if direct:
        flat = [piece for got in pieces for piece in got]
        sources = [[c * head_count + k for c in range(chunks)] for k in range(head_count)]
        column = lambda i, s: (0, jnp.bitwise_xor(i, s[0]))
        in_specs = [pl.BlockSpec((rows, part), lambda i, s: (0, 0))] * len(flat)
    else:
        flat = pieces
        sources = None
        per_group = max(1, group_width // width)
        column = lambda i, s: (0, i)
        in_specs = [pl.BlockSpec((per_group, rows, part), lambda i, s: (i, 0, 0))] * len(flat)
    return pl.pallas_call(
        functools.partial(norm_kernel, sources),
        grid_spec=pltpu.PrefetchScalarGridSpec(
            num_scalar_prefetch=1,
            grid=(GROUPS,),
            in_specs=[pl.BlockSpec((1, group_width), column)] + in_specs,
            out_specs=pl.BlockSpec((rows, group_width), column),
        ),
        out_shape=jax.ShapeDtypeStruct((rows, width * head_count), jnp.bfloat16),
        compiler_params=params(16),
        cost_estimate=pl.CostEstimate(
            flops=8 * tokens * width, bytes_accessed=4 * tokens * width, transcendentals=0
        ),
        name="norm_rows",
    )(me, gain, *flat)


def solution(mesh):
    in_specs = (
        P("seq", "head"),
        P("seq", "head"),
        P("seq", None, None),
        P("seq", None, None),
        P("seq", "head"),
        P("seq", "head", None),
        P(),
        P(),
    )
    out_specs = P(("seq", "head"), None)
    return jax.shard_map(body, mesh=mesh, in_specs=in_specs, out_specs=out_specs, check_vma=False)
```

time: 97.4 us -> 72.9 us (0.75)
  the two profiles are of different devices: /device:TPU:25 before, /device:TPU:29 now
where the time goes in v1:
time: 72.9 us; the launch traced here: 72.6 us
  Pallas kernels  22.6 us (31%)
  starting transfers between devices  22.2 us (30%)
  waiting for transfers between devices  20.6 us (28%)
  local copies, waits for them, and re-layouts  6.68 us (9%)
    ppermute x14, waiting for transfers between devices, body(): got[apart] = lax.ppermute(out[apart], 'head', pairs)  15.8 us
    ppermute x14, starting transfers between devices, body(): got[apart] = lax.ppermute(out[apart], 'head', pairs)  15.5 us
    pallas_call x2, Pallas kernels, local_call(): pl.pallas_call(functools.partial(local_kernel, head_dim, c * part, far),...  10.7 us
    ppermute x6, starting transfers between devices, body(): got = lax.ppermute(moving, 'seq', [(s, s + 1) for s in source])  6.69 us
    ppermute x6, waiting for transfers between devices, body(): got = lax.ppermute(moving, 'seq', [(s, s + 1) for s in source])  4.87 us
    pallas_call x2, Pallas kernels, state_call(): pl.pallas_call(functools.partial(state_kernel, head_dim, c * part, pieces...  4.75 us
    pallas_call x1, Pallas kernels, body(): pl.pallas_call(functools.partial(norm_kernel, sources), grid_spec=pltpu.P...  3.8 us
    pallas_call x2, Pallas kernels, gate_call(): pl.pallas_call(functools.partial(gate_kernel, head_dim, heads, (near + 7)...  3.34 us
  transfers between devices with their start and end apart: 20, of which 4 were waited for; matrix products, arithmetic and copies ran while one was open for 3% of the time, Pallas kernels for 23%

profile of v1, /device:TPU:29, one launch (start us, length us, event | category | flops | bytes accessed | tf_op | source)
XLA Modules:
  0.0 72.6 jit_solution(557796411812562238)
XLA Ops:
  2.2 1.6 %copy-done.1 = bf16[1024,1024]{1,0:T(8,128)(2,1)S(1)} copy-done((bf16[1024,1024]{1,0:T(8,128)(2,1)S(1)}, bf16[1024,1024]{1,0:T(8,128)(2,1)}, u32[]{:S(2)}) %copy-start.1) | copy-done | bytes 2097176
  4.5 2.4 %block_state.3 = (f32[128,512]{1,0:T(8,128)S(1)}, bf16[128,512]{1,0:T(8,128)(2,1)S(1)}, f32[8,512]{1,0:T(8,128)S(1)}) custom-call(s32[64]{0:T(128)S(1)} %copy-done.5, f32[8,1024]{1,0:T(8,128)S(1)} %get-tuple-element.60.decay, bf16[1024,128]{1,0:T(8,128)(2,1)S(1)} %bitcast.18, bf16[1024,1024]{1,0:T(8,128)(2,1)S(1)} %copy-done.1), custom_call_target="tpu_custom_call" | custom-call | flops 268435456 | bytes 1572864 | tf_op jit(solution)/shard_map/block_state/pallas_call | solution.py:299
  6.9 1.3 %collective-permute-start = (bf16[128,512]{1,0:T(8,128)(2,1)S(1)}, bf16[128,512]{1,0:T(8,128)(2,1)S(1)}, u32[]{:S(2)}, u32[]{:S(2)}) collective-permute-start(bf16[128,512]{1,0:T(8,128)(2,1)S(1)} %get-tuple-element.34), channel_id=1, source_target_pairs={{0,8},{16,24},{1,9},{17,25},{2,10},{18,26},{3,11},{19,27},{4,12},{... | collective-permute-start | bytes 393224 | tf_op jit(solution)/shard_map/ppermute | solution.py:369
  8.2 2.4 %block_state.2 = (f32[128,512]{1,0:T(8,128)S(1)}, bf16[128,512]{1,0:T(8,128)(2,1)S(1)}, f32[8,512]{1,0:T(8,128)S(1)}) custom-call(s32[64]{0:T(128)S(1)} %copy-done.5, f32[8,1024]{1,0:T(8,128)S(1)} %get-tuple-element.59.decay, bf16[1024,128]{1,0:T(8,128)(2,1)S(1)} %bitcast.19, bf16[1024,1024]{1,0:T(8,128)(2,1)S(1)} %copy-done.2), custom_call_target="tpu_custom_call" | custom-call | flops 268435456 | bytes 1572864 | tf_op jit(solution)/shard_map/block_state/pallas_call | solution.py:299
  10.6 1.3 %collective-permute-start.10 = (bf16[128,512]{1,0:T(8,128)(2,1)S(1)}, bf16[128,512]{1,0:T(8,128)(2,1)S(1)}, u32[]{:S(2)}, u32[]{:S(2)}) collective-permute-start(bf16[128,512]{1,0:T(8,128)(2,1)S(1)} %get-tuple-element.31.follow), channel_id=1, source_target_pairs={{0,8},{16,24},{1,9},{17,25},{2,10},{18,26},{3,11},{19,27},{4,12},{... | collective-permute-start | bytes 393224 | tf_op jit(solution)/shard_map/ppermute | solution.py:369
  11.9 2.1 %constant_dynamic-slice_fusion.1 = bf16[1024,1,128]{2,1,0:T(2,128)(2,1)S(1)} fusion(bf16[1024,8,128]{2,1,0:T(8,128)(2,1)} %param.11, s32[]{:T(128)S(6)} %select_n.11), kind=kLoop, calls=%fused_computation.11 | loop fusion | bytes 524292 | tf_op jit(solution)/shard_map/jit(dynamic_index_in_dim)/dynamic_slice | solution.py:279
  14.1 5.4 %local_mixer.2 = (f32[1024,512]{1,0:T(8,128)S(1)}, bf16[1024,256]{1,0:T(8,128)(2,1)S(1)}) custom-call(s32[64]{0:T(128)S(1)} %copy-done.6, f32[8,1024]{1,0:T(8,128)S(1)} %get-tuple-element.60.decay, f32[7,8,1024]{2,1,0:T(8,128)S(1)} %get-tuple-element.58.weight, bf16[1024,1024]{1,0:T(8,128)(2,1)S(1)} %copy-done.2, bf16[1024,128]{1,0:T(8,128)(2,1)S(1)} %bitcast.22, ...), custom_call_target="tpu_custom_call" | custom-call | flops 1073741824 | bytes 6291456 | tf_op jit(solution)/shard_map/local_mixer/pallas_call | solution.py:320
  21.2 5.4 %local_mixer.3 = (f32[1024,512]{1,0:T(8,128)S(1)}, bf16[1024,256]{1,0:T(8,128)(2,1)S(1)}) custom-call(s32[64]{0:T(128)S(1)} %copy-done.6, f32[8,1024]{1,0:T(8,128)S(1)} %get-tuple-element.59.decay, f32[7,8,1024]{2,1,0:T(8,128)S(1)} %get-tuple-element.57.weight, bf16[1024,1024]{1,0:T(8,128)(2,1)S(1)} %copy-done.2, bf16[1024,128]{1,0:T(8,128)(2,1)S(1)} %bitcast.23, ...), custom_call_target="tpu_custom_call" | custom-call | flops 1073741824 | bytes 6291456 | tf_op jit(solution)/shard_map/local_mixer/pallas_call | solution.py:320
  26.6 1.3 %collective-permute-start.12 = (bf16[128,512]{1,0:T(8,128)(2,1)S(1)}, bf16[128,512]{1,0:T(8,128)(2,1)S(1)}, u32[]{:S(2)}, u32[]{:S(2)}) collective-permute-start(bf16[128,512]{1,0:T(8,128)(2,1)S(1)} %multiply_convert_fusion), channel_id=1, source_target_pairs={{16,24},{17,25},{18,26},{19,27},{20,28},{21,29},{22,30},{23,31}} | collective-permute-start | bytes 393224 | tf_op jit(solution)/shard_map/ppermute | solution.py:369
  27.9 1.3 %collective-permute-start.2 = (bf16[128,512]{1,0:T(8,128)(2,1)S(1)}, bf16[128,512]{1,0:T(8,128)(2,1)S(1)}, u32[]{:S(2)}, u32[]{:S(2)}) collective-permute-start(bf16[128,512]{1,0:T(8,128)(2,1)S(1)} %multiply_convert_fusion.1), channel_id=1, source_target_pairs={{16,24},{17,25},{18,26},{19,27},{20,28},{21,29},{22,30},{23,31}} | collective-permute-start | bytes 393224 | tf_op jit(solution)/shard_map/ppermute | solution.py:369
  29.2 4.9 %collective-permute-done.12 = bf16[128,512]{1,0:T(8,128)(2,1)S(1)} collective-permute-done((bf16[128,512]{1,0:T(8,128)(2,1)S(1)}, bf16[128,512]{1,0:T(8,128)(2,1)S(1)}, u32[]{:S(2)}, u32[]{:S(2)}) %collective-permute-start.12) | collective-permute-done | bytes 131104 | tf_op jit(solution)/shard_map/ppermute | solution.py:369
  34.2 1.7 %far_and_gate.3 = (bf16[128,512]{1,0:T(8,128)(2,1)S(1)}, bf16[128,512]{1,0:T(8,128)(2,1)S(1)}, bf16[128,512]{1,0:T(8,128)(2,1)S(1)}, bf16[128,512]{1,0:T(8,128)(...) custom-call(s32[1]{0:T(128)} %bitcast.me, ...), custom_call_target="tpu_custom_call" | custom-call | flops 268435456 | bytes 4194304 | tf_op jit(solution)/shard_map/far_and_gate/pallas_call | solution.py:344
  35.8 2.8 %collective-permute-start.13 = (bf16[128,512]{1,0:T(8,128)(2,1)S(1)}, bf16[128,512]{1,0:T(8,128)(2,1)S(1)}, u32[]{:S(2)}, u32[]{:S(2)}) collective-permute-start(bf16[128,512]{1,0:T(8,128)(2,1)S(1)} %get-tuple-element.50), channel_id=1, source_target_pairs={{0,1},{1,0},{2,3},{3,2},{4,5},{5,4},{6,7},{7,6},{8,9},{9,8},{10,11... | collective-permute-start | bytes 393224 | tf_op jit(solution)/shard_map/ppermute | solution.py:386
  38.6 1.2 %collective-permute-start.14 = (bf16[128,512]{1,0:T(8,128)(2,1)S(1)}, bf16[128,512]{1,0:T(8,128)(2,1)S(1)}, u32[]{:S(2)}, u32[]{:S(2)}) collective-permute-start(bf16[128,512]{1,0:T(8,128)(2,1)S(1)} %get-tuple-element.51), channel_id=1, source_target_pairs={{0,2},{1,3},{2,0},{3,1},{4,6},{5,7},{6,4},{7,5},{8,10},{9,11},{10,... | collective-permute-start | bytes 393224 | tf_op jit(solution)/shard_map/ppermute | solution.py:386
  40.5 1.6 %collective-permute-start.17 = (bf16[128,512]{1,0:T(8,128)(2,1)S(1)}, bf16[128,512]{1,0:T(8,128)(2,1)S(1)}, u32[]{:S(2)}, u32[]{:S(2)}) collective-permute-start(bf16[128,512]{1,0:T(8,128)(2,1)S(1)} %get-tuple-element.54), channel_id=1, source_target_pairs={{0,5},{1,4},{2,7},{3,6},{4,1},{5,0},{6,3},{7,2},{8,13},{9,12},{10,... | collective-permute-start | bytes 393224 | tf_op jit(solution)/shard_map/ppermute | solution.py:386
  42.2 1.7 %far_and_gate.2 = (bf16[128,512]{1,0:T(8,128)(2,1)S(1)}, bf16[128,512]{1,0:T(8,128)(2,1)S(1)}, bf16[128,512]{1,0:T(8,128)(2,1)S(1)}, bf16[128,512]{1,0:T(8,128)(...) custom-call(s32[1]{0:T(128)} %bitcast.me, ...), custom_call_target="tpu_custom_call" | custom-call | flops 268435456 | bytes 4194304 | tf_op jit(solution)/shard_map/far_and_gate/pallas_call | solution.py:344
  43.9 1.2 %collective-permute-start.18 = (bf16[128,512]{1,0:T(8,128)(2,1)S(1)}, bf16[128,512]{1,0:T(8,128)(2,1)S(1)}, u32[]{:S(2)}, u32[]{:S(2)}) collective-permute-start(bf16[128,512]{1,0:T(8,128)(2,1)S(1)} %get-tuple-element.55), channel_id=1, source_target_pairs={{0,6},{1,7},{2,4},{3,5},{4,2},{5,3},{6,0},{7,1},{8,14},{9,15},{10,... | collective-permute-start | bytes 393224 | tf_op jit(solution)/shard_map/ppermute | solution.py:386
  45.1 1.4 %collective-permute-start.19 = (bf16[128,512]{1,0:T(8,128)(2,1)S(1)}, bf16[128,512]{1,0:T(8,128)(2,1)S(1)}, u32[]{:S(2)}, u32[]{:S(2)}) collective-permute-start(bf16[128,512]{1,0:T(8,128)(2,1)S(1)} %get-tuple-element.56), channel_id=1, source_target_pairs={{0,7},{1,6},{2,5},{3,4},{4,3},{5,2},{6,1},{7,0},{8,15},{9,14},{10,... | collective-permute-start | bytes 393224 | tf_op jit(solution)/shard_map/ppermute | solution.py:386
  47.2 1.2 %collective-permute-start.4 = (bf16[128,512]{1,0:T(8,128)(2,1)S(1)}, bf16[128,512]{1,0:T(8,128)(2,1)S(1)}, u32[]{:S(2)}, u32[]{:S(2)}) collective-permute-start(bf16[128,512]{1,0:T(8,128)(2,1)S(1)} %get-tuple-element.39), channel_id=1, source_target_pairs={{0,2},{1,3},{2,0},{3,1},{4,6},{5,7},{6,4},{7,5},{8,10},{9,11},{10,... | collective-permute-start | bytes 393224 | tf_op jit(solution)/shard_map/ppermute | solution.py:386
  48.4 5.8 %collective-permute-done.17.rest_13_ = bf16[128,512]{1,0:T(8,128)(2,1)S(1)} collective-permute-done((bf16[128,512]{1,0:T(8,128)(2,1)S(1)}, bf16[128,512]{1,0:T(8,128)(2,1)S(1)}, u32[]{:S(2)}, u32[]{:S(2)}) %collective-permute-start.17) | collective-permute-done | bytes 131104 | tf_op jit(solution)/shard_map/ppermute | solution.py:386
  55.3 2.2 %collective-permute-start.7 = (bf16[128,512]{1,0:T(8,128)(2,1)S(1)}, bf16[128,512]{1,0:T(8,128)(2,1)S(1)}, u32[]{:S(2)}, u32[]{:S(2)}) collective-permute-start(bf16[128,512]{1,0:T(8,128)(2,1)S(1)} %get-tuple-element.42), channel_id=1, source_target_pairs={{0,5},{1,4},{2,7},{3,6},{4,1},{5,0},{6,3},{7,2},{8,13},{9,12},{10,... | collective-permute-start | bytes 393224 | tf_op jit(solution)/shard_map/ppermute | solution.py:386
  57.7 1.9 %collective-permute-start.9 = (bf16[128,512]{1,0:T(8,128)(2,1)S(1)}, bf16[128,512]{1,0:T(8,128)(2,1)S(1)}, u32[]{:S(2)}, u32[]{:S(2)}) collective-permute-start(bf16[128,512]{1,0:T(8,128)(2,1)S(1)} %get-tuple-element.44), channel_id=1, source_target_pairs={{0,7},{1,6},{2,5},{3,4},{4,3},{5,2},{6,1},{7,0},{8,15},{9,14},{10,... | collective-permute-start | bytes 393224 | tf_op jit(solution)/shard_map/ppermute | solution.py:386
  59.6 9.2 %collective-permute-done.7.rest_5_ = bf16[128,512]{1,0:T(8,128)(2,1)S(1)} collective-permute-done((bf16[128,512]{1,0:T(8,128)(2,1)S(1)}, bf16[128,512]{1,0:T(8,128)(2,1)S(1)}, u32[]{:S(2)}, u32[]{:S(2)}) %collective-permute-start.7) | collective-permute-done | bytes 131104 | tf_op jit(solution)/shard_map/ppermute | solution.py:386
  68.8 3.8 %norm_rows.1 = bf16[128,8192]{1,0:T(8,128)(2,1)} custom-call(s32[1]{0:T(128)} %bitcast.me, f32[1,8192]{1,0:T(1,128)S(1)} %bitcast.26, bf16[128,512]{1,0:T(8,128)(2,1)S(1)} %get-tuple-element.37.rest_0_, bf16[128,512]{1,0:T(8,128)(2,1)S(1)} %collective-permute-done.3.rest_1_, bf16[128,512]{1,0:T(8,128)(2,1)S(1)} %collective-permute-done.4.rest_2_, ...), custom_call_target="tpu_custom_call" | custom-call | flops 8388608 | bytes 4194304 | tf_op jit(solution)/shard_map/norm_rows/pallas_call | solution.py:404
  (55 shorter events, 7.3 us)
Async XLA Ops:
  4.5 7.4 %copy-start.7 = (f32[1024,16,7]{0,1,2:T(8,128)S(1)}, f32[1024,16,7]{0,1,2:T(8,128)}, u32[]{:S(2)}) copy-start(f32[1024,16,7]{0,1,2:T(8,128)} %param.13) | copy-start | bytes 1376260
  6.9 13.4 %collective-permute-start = (bf16[128,512]{1,0:T(8,128)(2,1)S(1)}, bf16[128,512]{1,0:T(8,128)(2,1)S(1)}, u32[]{:S(2)}, u32[]{:S(2)}) collective-permute-start(bf16[128,512]{1,0:T(8,128)(2,1)S(1)} %get-tuple-element.34), channel_id=1, source_target_pairs={{0,8},{16,24},{1,9},{17,25},{2,10},{18,26},{3,11},{19,27},{4,12},{... | collective-permute-start | bytes 393224 | tf_op jit(solution)/shard_map/ppermute | solution.py:369
  8.2 6.0 %copy-start.6 = (s32[64]{0:T(128)S(1)}, s32[64]{0:T(128)}, u32[]{:S(2)}) copy-start(s32[64]{0:T(128)} %docs.7) | copy-start | bytes 772
  10.6 8.9 %collective-permute-start.10 = (bf16[128,512]{1,0:T(8,128)(2,1)S(1)}, bf16[128,512]{1,0:T(8,128)(2,1)S(1)}, u32[]{:S(2)}, u32[]{:S(2)}) collective-permute-start(bf16[128,512]{1,0:T(8,128)(2,1)S(1)} %get-tuple-element.31.follow), channel_id=1, source_target_pairs={{0,8},{16,24},{1,9},{17,25},{2,10},{18,26},{3,11},{19,27},{4,12},{... | collective-permute-start | bytes 393224 | tf_op jit(solution)/shard_map/ppermute | solution.py:369
  19.6 7.0 %collective-permute-start.11 = (bf16[128,512]{1,0:T(8,128)(2,1)S(1)}, bf16[128,512]{1,0:T(8,128)(2,1)S(1)}, u32[]{:S(2)}, u32[]{:S(2)}) collective-permute-start(bf16[128,512]{1,0:T(8,128)(2,1)S(1)} %add_convert_fusion.follow), channel_id=1, source_target_pairs={{8,16},{9,17},{10,18},{11,19},{12,20},{13,21},{14,22},{15,23}} | collective-permute-start | bytes 393224 | tf_op jit(solution)/shard_map/ppermute | solution.py:369
  20.3 7.6 %collective-permute-start.1 = (bf16[128,512]{1,0:T(8,128)(2,1)S(1)}, bf16[128,512]{1,0:T(8,128)(2,1)S(1)}, u32[]{:S(2)}, u32[]{:S(2)}) collective-permute-start(bf16[128,512]{1,0:T(8,128)(2,1)S(1)} %add_convert_fusion.1), channel_id=1, source_target_pairs={{8,16},{9,17},{10,18},{11,19},{12,20},{13,21},{14,22},{15,23}} | collective-permute-start | bytes 393224 | tf_op jit(solution)/shard_map/ppermute | solution.py:369
  21.2 13.0 %copy-start.3 = (bf16[1024,1024]{1,0:T(8,128)(2,1)S(1)}, bf16[1024,1024]{1,0:T(8,128)(2,1)}, u32[]{:S(2)}) copy-start(bf16[1024,1024]{1,0:T(8,128)(2,1)} %gate.3) | copy-start | bytes 6291460
  26.6 7.5 %collective-permute-start.12 = (bf16[128,512]{1,0:T(8,128)(2,1)S(1)}, bf16[128,512]{1,0:T(8,128)(2,1)S(1)}, u32[]{:S(2)}, u32[]{:S(2)}) collective-permute-start(bf16[128,512]{1,0:T(8,128)(2,1)S(1)} %multiply_convert_fusion), channel_id=1, source_target_pairs={{16,24},{17,25},{18,26},{19,27},{20,28},{21,29},{22,30},{23,31}} | collective-permute-start | bytes 393224 | tf_op jit(solution)/shard_map/ppermute | solution.py:369
  27.9 12.6 %collective-permute-start.2 = (bf16[128,512]{1,0:T(8,128)(2,1)S(1)}, bf16[128,512]{1,0:T(8,128)(2,1)S(1)}, u32[]{:S(2)}, u32[]{:S(2)}) collective-permute-start(bf16[128,512]{1,0:T(8,128)(2,1)S(1)} %multiply_convert_fusion.1), channel_id=1, source_target_pairs={{16,24},{17,25},{18,26},{19,27},{20,28},{21,29},{22,30},{23,31}} | collective-permute-start | bytes 393224 | tf_op jit(solution)/shard_map/ppermute | solution.py:369
  35.8 8.1 %collective-permute-start.13 = (bf16[128,512]{1,0:T(8,128)(2,1)S(1)}, bf16[128,512]{1,0:T(8,128)(2,1)S(1)}, u32[]{:S(2)}, u32[]{:S(2)}) collective-permute-start(bf16[128,512]{1,0:T(8,128)(2,1)S(1)} %get-tuple-element.50), channel_id=1, source_target_pairs={{0,1},{1,0},{2,3},{3,2},{4,5},{5,4},{6,7},{7,6},{8,9},{9,8},{10,11... | collective-permute-start | bytes 393224 | tf_op jit(solution)/shard_map/ppermute | solution.py:386
  38.6 6.5 %collective-permute-start.14 = (bf16[128,512]{1,0:T(8,128)(2,1)S(1)}, bf16[128,512]{1,0:T(8,128)(2,1)S(1)}, u32[]{:S(2)}, u32[]{:S(2)}) collective-permute-start(bf16[128,512]{1,0:T(8,128)(2,1)S(1)} %get-tuple-element.51), channel_id=1, source_target_pairs={{0,2},{1,3},{2,0},{3,1},{4,6},{5,7},{6,4},{7,5},{8,10},{9,11},{10,... | collective-permute-start | bytes 393224 | tf_op jit(solution)/shard_map/ppermute | solution.py:386
  39.8 7.4 %collective-permute-start.15 = (bf16[128,512]{1,0:T(8,128)(2,1)S(1)}, bf16[128,512]{1,0:T(8,128)(2,1)S(1)}, u32[]{:S(2)}, u32[]{:S(2)}) collective-permute-start(bf16[128,512]{1,0:T(8,128)(2,1)S(1)} %get-tuple-element.52), channel_id=1, source_target_pairs={{0,3},{1,2},{2,1},{3,0},{4,7},{5,6},{6,5},{7,4},{8,11},{9,10},{10,... | collective-permute-start | bytes 393224 | tf_op jit(solution)/shard_map/ppermute | solution.py:386
  40.3 6.9 %collective-permute-start.16 = (bf16[128,512]{1,0:T(8,128)(2,1)S(1)}, bf16[128,512]{1,0:T(8,128)(2,1)S(1)}, u32[]{:S(2)}, u32[]{:S(2)}) collective-permute-start(bf16[128,512]{1,0:T(8,128)(2,1)S(1)} %get-tuple-element.53), channel_id=1, source_target_pairs={{0,4},{1,5},{2,6},{3,7},{4,0},{5,1},{6,2},{7,3},{8,12},{9,13},{10,... | collective-permute-start | bytes 393224 | tf_op jit(solution)/shard_map/ppermute | solution.py:386
  40.5 13.7 %collective-permute-start.17 = (bf16[128,512]{1,0:T(8,128)(2,1)S(1)}, bf16[128,512]{1,0:T(8,128)(2,1)S(1)}, u32[]{:S(2)}, u32[]{:S(2)}) collective-permute-start(bf16[128,512]{1,0:T(8,128)(2,1)S(1)} %get-tuple-element.54), channel_id=1, source_target_pairs={{0,5},{1,4},{2,7},{3,6},{4,1},{5,0},{6,3},{7,2},{8,13},{9,12},{10,... | collective-permute-start | bytes 393224 | tf_op jit(solution)/shard_map/ppermute | solution.py:386
  42.2 26.7 %copy-start.4 = (f32[8192]{0:T(1024)S(1)}, f32[8192]{0:T(1024)}, u32[]{:S(2)}) copy-start(f32[8192]{0:T(1024)} %param.15) | copy-start | bytes 98308
  43.9 11.3 %collective-permute-start.18 = (bf16[128,512]{1,0:T(8,128)(2,1)S(1)}, bf16[128,512]{1,0:T(8,128)(2,1)S(1)}, u32[]{:S(2)}, u32[]{:S(2)}) collective-permute-start(bf16[128,512]{1,0:T(8,128)(2,1)S(1)} %get-tuple-element.55), channel_id=1, source_target_pairs={{0,6},{1,7},{2,4},{3,5},{4,2},{5,3},{6,0},{7,1},{8,14},{9,15},{10,... | collective-permute-start | bytes 393224 | tf_op jit(solution)/shard_map/ppermute | solution.py:386
  45.1 10.2 %collective-permute-start.19 = (bf16[128,512]{1,0:T(8,128)(2,1)S(1)}, bf16[128,512]{1,0:T(8,128)(2,1)S(1)}, u32[]{:S(2)}, u32[]{:S(2)}) collective-permute-start(bf16[128,512]{1,0:T(8,128)(2,1)S(1)} %get-tuple-element.56), channel_id=1, source_target_pairs={{0,7},{1,6},{2,5},{3,4},{4,3},{5,2},{6,1},{7,0},{8,15},{9,14},{10,... | collective-permute-start | bytes 393224 | tf_op jit(solution)/shard_map/ppermute | solution.py:386
  47.2 10.3 %collective-permute-start.3 = (bf16[128,512]{1,0:T(8,128)(2,1)S(1)}, bf16[128,512]{1,0:T(8,128)(2,1)S(1)}, u32[]{:S(2)}, u32[]{:S(2)}) collective-permute-start(bf16[128,512]{1,0:T(8,128)(2,1)S(1)} %get-tuple-element.38), channel_id=1, source_target_pairs={{0,1},{1,0},{2,3},{3,2},{4,5},{5,4},{6,7},{7,6},{8,9},{9,8},{10,11... | collective-permute-start | bytes 393224 | tf_op jit(solution)/shard_map/ppermute | solution.py:386
  47.2 10.5 %collective-permute-start.4 = (bf16[128,512]{1,0:T(8,128)(2,1)S(1)}, bf16[128,512]{1,0:T(8,128)(2,1)S(1)}, u32[]{:S(2)}, u32[]{:S(2)}) collective-permute-start(bf16[128,512]{1,0:T(8,128)(2,1)S(1)} %get-tuple-element.39), channel_id=1, source_target_pairs={{0,2},{1,3},{2,0},{3,1},{4,6},{5,7},{6,4},{7,5},{8,10},{9,11},{10,... | collective-permute-start | bytes 393224 | tf_op jit(solution)/shard_map/ppermute | solution.py:386
  54.3 5.3 %collective-permute-start.5 = (bf16[128,512]{1,0:T(8,128)(2,1)S(1)}, bf16[128,512]{1,0:T(8,128)(2,1)S(1)}, u32[]{:S(2)}, u32[]{:S(2)}) collective-permute-start(bf16[128,512]{1,0:T(8,128)(2,1)S(1)} %get-tuple-element.40), channel_id=1, source_target_pairs={{0,3},{1,2},{2,1},{3,0},{4,7},{5,6},{6,5},{7,4},{8,11},{9,10},{10,... | collective-permute-start | bytes 393224 | tf_op jit(solution)/shard_map/ppermute | solution.py:386
  55.2 4.4 %collective-permute-start.6 = (bf16[128,512]{1,0:T(8,128)(2,1)S(1)}, bf16[128,512]{1,0:T(8,128)(2,1)S(1)}, u32[]{:S(2)}, u32[]{:S(2)}) collective-permute-start(bf16[128,512]{1,0:T(8,128)(2,1)S(1)} %get-tuple-element.41), channel_id=1, source_target_pairs={{0,4},{1,5},{2,6},{3,7},{4,0},{5,1},{6,2},{7,3},{8,12},{9,13},{10,... | collective-permute-start | bytes 393224 | tf_op jit(solution)/shard_map/ppermute | solution.py:386
  55.3 13.6 %collective-permute-start.7 = (bf16[128,512]{1,0:T(8,128)(2,1)S(1)}, bf16[128,512]{1,0:T(8,128)(2,1)S(1)}, u32[]{:S(2)}, u32[]{:S(2)}) collective-permute-start(bf16[128,512]{1,0:T(8,128)(2,1)S(1)} %get-tuple-element.42), channel_id=1, source_target_pairs={{0,5},{1,4},{2,7},{3,6},{4,1},{5,0},{6,3},{7,2},{8,13},{9,12},{10,... | collective-permute-start | bytes 393224 | tf_op jit(solution)/shard_map/ppermute | solution.py:386
  57.5 11.3 %collective-permute-start.8 = (bf16[128,512]{1,0:T(8,128)(2,1)S(1)}, bf16[128,512]{1,0:T(8,128)(2,1)S(1)}, u32[]{:S(2)}, u32[]{:S(2)}) collective-permute-start(bf16[128,512]{1,0:T(8,128)(2,1)S(1)} %get-tuple-element.43), channel_id=1, source_target_pairs={{0,6},{1,7},{2,4},{3,5},{4,2},{5,3},{6,0},{7,1},{8,14},{9,15},{10,... | collective-permute-start | bytes 393224 | tf_op jit(solution)/shard_map/ppermute | solution.py:386
  57.7 11.1 %collective-permute-start.9 = (bf16[128,512]{1,0:T(8,128)(2,1)S(1)}, bf16[128,512]{1,0:T(8,128)(2,1)S(1)}, u32[]{:S(2)}, u32[]{:S(2)}) collective-permute-start(bf16[128,512]{1,0:T(8,128)(2,1)S(1)} %get-tuple-element.44), channel_id=1, source_target_pairs={{0,7},{1,6},{2,5},{3,4},{4,3},{5,2},{6,1},{7,0},{8,15},{9,14},{10,... | collective-permute-start | bytes 393224 | tf_op jit(solution)/shard_map/ppermute | solution.py:386
  (4 other events, 7.6 us)

commit v2 on v1

--- a/solution.py
+++ b/solution.py
@@ -65,10 +65,30 @@
 
 
 def state_kernel(
-    head_dim, column, pieces, docs, decay, keys, values, state, message, through, inputs, arrived
+    head_dim,
+    chunk,
+    pieces,
+    docs_far,
+    decay_far,
+    keys,
+    values,
+    state,
+    message,
+    through,
+    docs,
+    decay,
+    inputs,
+    arrived,
 ):
     heads, tokens = decay.shape
     width = inputs.shape[1]
+    column = chunk * width
+    small = [
+        pltpu.make_async_copy(
+            decay_far.at[pl.ds(chunk * heads, heads), :], decay, arrived.at[pieces]
+        ),
+        pltpu.make_async_copy(docs_far, docs, arrived.at[pieces + 1]),
+    ]
     tiles = tokens // TILE
     rows = tokens // pieces
     copies = [
@@ -79,8 +99,10 @@
         )
         for i in range(pieces)
     ]
-    for copy in copies:
+    for copy in small + copies:
         copy.start()
+    for copy in small:
+        copy.wait()
     shut = resets(docs, tiles)
     lane = iota((heads, TILE), 1)
     later = jnp.where(iota((TILE, TILE), 0) > iota((TILE, TILE), 1), 1.0, 0.0)
@@ -123,17 +145,18 @@
 
 
 def local_kernel(
-    head_dim, column, far, docs, decay, weight, values, queries, keys, follow, out, coefs
+    head_dim, heads, chunk, far, docs, decay, weight, values, queries, keys, follow, out, coefs
 ):
     del follow
-    heads, tokens = decay.shape
-    width = out.shape[1]
+    tokens, width = out.shape
+    column = chunk * width
+    mine = slice(chunk * heads, (chunk + 1) * heads)
     tiles = tokens // TILE
     near = tiles.bit_length() - 1
     shut = resets(docs, tiles)
     lane = iota((heads, TILE), 1)
     upto = jnp.where(iota((TILE, TILE), 0) <= iota((TILE, TILE), 1), 1.0, 0.0)
-    all_sums = dot(tile_rows(decay[...]), upto, precision=HIGHEST)
+    all_sums = dot(tile_rows(decay[mine, :]), upto, precision=HIGHEST)
     causal = iota((TILE, TILE), 0) >= iota((TILE, TILE), 1)
     per_tile = LANES // head_dim
     lane_head = jnp.right_shift(iota((TILE, LANES), 1), head_dim.bit_length() - 1)
@@ -151,7 +174,7 @@
     for b in range(tiles):
         tokens_here = slice(b * TILE, (b + 1) * TILE)
         sums = all_sums[b * heads : (b + 1) * heads]
-        scale = [weight[level, :, tokens_here] for level in range(weight.shape[0])]
+        scale = [weight[level, mine, tokens_here] for level in range(weight.shape[0])]
         last = jnp.broadcast_to(sums[:, TILE - 1 :], sums.shape)
         opened = sums + jnp.where(lane < SPAN, shut[b][0], shut[b][0] + shut[b][1])
         own = sums + jnp.log(scale[0])
@@ -233,7 +256,7 @@
             outs[0][index] = rows_of(index)
 
 
-def norm_kernel(sources, me, gain, *rest):
+def norm_kernel(sources, before, me, gain, *rest):
     out = rest[-1]
     step = pl.program_id(0)
 
@@ -256,7 +279,11 @@
 
         @pl.when(step == index)
         def _(places=places):
-            write([rest[place][...] for place in places])
+            write([rest[before + place][...] for place in places])
+
+
+def partners(count):
+    return sorted(range(1, count), key=lambda apart: (-apart.bit_count(), -apart))
 
 
 def params(limit):
@@ -288,17 +315,16 @@
     part = width // chunks
     levels = weight.shape[0]
     smem = pl.BlockSpec(memory_space=pltpu.SMEM)
-    decays = [decay[c * heads : (c + 1) * heads] for c in range(chunks)]
-    weights = [weight[:, c * heads : (c + 1) * heads] for c in range(chunks)]
 
     whole = pl.BlockSpec(memory_space=pltpu.VMEM)
     anywhere = pl.BlockSpec(memory_space=pl.ANY)
+    far_away = pl.BlockSpec(memory_space=pltpu.HBM)
 
     def state_call(c):
         pieces = min(4, tiles)
         return pl.pallas_call(
-            functools.partial(state_kernel, head_dim, c * part, pieces),
-            in_specs=[smem, whole, whole, anywhere],
+            functools.partial(state_kernel, head_dim, c, pieces),
+            in_specs=[far_away, far_away, whole, far_away],
             out_specs=[whole, whole, whole],
             out_shape=[
                 jax.ShapeDtypeStruct((state_size, part), jnp.float32),
@@ -306,19 +332,21 @@
                 jax.ShapeDtypeStruct((SUBLANES, part), jnp.float32),
             ],
             scratch_shapes=[
+                pltpu.SMEM(doc_start.shape, doc_start.dtype),
+                pltpu.VMEM((heads, tokens), jnp.float32),
                 pltpu.VMEM((tokens, part), jnp.bfloat16),
-                pltpu.SemaphoreType.DMA((pieces,)),
+                pltpu.SemaphoreType.DMA((pieces + 2,)),
             ],
             compiler_params=params(16),
             cost_estimate=pl.CostEstimate(
                 flops=4 * tokens * state_size * part, bytes_accessed=3 * tokens * part, transcendentals=0
             ),
             name="block_state",
-        )(doc_start, decays[c], key_rows, values)
+        )(doc_start, decay, key_rows, values)
 
     def local_call(c, follow):
         return pl.pallas_call(
-            functools.partial(local_kernel, head_dim, c * part, far),
+            functools.partial(local_kernel, head_dim, heads, c, far),
             in_specs=[smem, whole, whole, whole, whole, whole, anywhere],
             out_specs=[whole, whole],
             out_shape=[
@@ -330,7 +358,7 @@
                 flops=16 * tokens * state_size * part, bytes_accessed=12 * tokens * part, transcendentals=0
             ),
             name="local_mixer",
-        )(doc_start, decays[c], weights[c], values, query_rows, key_rows, follow)
+        )(doc_start, decay, weight, values, query_rows, key_rows, follow)
 
     rows = tokens // head_count
     direct = head_count == GROUPS
@@ -356,13 +384,13 @@
     owns, throughs, messages = zip(*[(s, t[:1], m) for s, m, t in map(state_call, range(chunks))])
     owns = list(owns)
     carried = [[None] * far for _ in range(chunks)]
-    locals_ = [local_call(0, messages[-1])]
+    second = messages[0]
     for bit in range(far):
         size = 2**bit
         for c in range(chunks):
             moving = messages[c] if bit == 0 else owns[c].astype(jnp.bfloat16)
-            if bit == 1 and len(locals_) == c and c:
-                locals_.append(local_call(c, moving))
+            if bit == 1 and c == 0:
+                second = moving
             arrived = None
             for hop in range(1, size + 1):
                 source = [base + size + hop - 2 for base in range(0, seq_count, 2 * size)]
@@ -372,16 +400,16 @@
                 moving = passed.astype(jnp.bfloat16)
             carried[c][bit] = arrived
             owns[c] = owns[c] + passed
-    for c in range(len(locals_), chunks):
-        locals_.append(local_call(c, messages[-1]))
 
     pieces = []
+    follow = second
     for c in range(chunks):
-        local, coefs = locals_[c]
+        local, coefs = local_call(c, follow)
         out = gate_call(c, local, coefs, jnp.stack(carried[c]))
+        follow = out[0]
         if direct:
             got = [out[0]] + [None] * (head_count - 1)
-            for apart in sorted(range(1, head_count), key=lambda k: -k.bit_count() * 8 - k):
+            for apart in partners(head_count):
                 pairs = [(source, source ^ apart) for source in range(head_count)]
                 got[apart] = lax.ppermute(out[apart], "head", pairs)
             pieces.append(got)
@@ -390,32 +418,47 @@
 
     gain = jnp.reshape(norm_gain, (1, -1))
     group_width = width * head_count // GROUPS
-    if direct:
-        flat = [piece for got in pieces for piece in got]
-        sources = [[c * head_count + k for c in range(chunks)] for k in range(head_count)]
-        column = lambda i, s: (0, jnp.bitwise_xor(i, s[0]))
-        in_specs = [pl.BlockSpec((rows, part), lambda i, s: (0, 0))] * len(flat)
-    else:
-        flat = pieces
-        sources = None
+
+    def norm_call(kernel, steps, column, in_specs, operands, result=None):
+        given = [] if result is None else [result]
+        return pl.pallas_call(
+            kernel,
+            grid_spec=pltpu.PrefetchScalarGridSpec(
+                num_scalar_prefetch=1,
+                grid=(steps,),
+                in_specs=[pl.BlockSpec((1, group_width), column)] + [far_away] * len(given) + in_specs,
+                out_specs=pl.BlockSpec((rows, group_width), column),
+            ),
+            out_shape=jax.ShapeDtypeStruct((rows, width * head_count), jnp.bfloat16),
+            input_output_aliases={2: 0} if given else {},
+            compiler_params=params(16),
+            cost_estimate=pl.CostEstimate(
+                flops=8 * rows * group_width * steps,
+                bytes_accessed=4 * rows * group_width * steps,
+                transcendentals=0,
+            ),
+            name="norm_rows",
+        )(me, gain, *given, *operands)
+
+    if not direct:
         per_group = max(1, group_width // width)
-        column = lambda i, s: (0, i)
-        in_specs = [pl.BlockSpec((per_group, rows, part), lambda i, s: (i, 0, 0))] * len(flat)
-    return pl.pallas_call(
-        functools.partial(norm_kernel, sources),
-        grid_spec=pltpu.PrefetchScalarGridSpec(
-            num_scalar_prefetch=1,
-            grid=(GROUPS,),
-            in_specs=[pl.BlockSpec((1, group_width), column)] + in_specs,
-            out_specs=pl.BlockSpec((rows, group_width), column),
-        ),
-        out_shape=jax.ShapeDtypeStruct((rows, width * head_count), jnp.bfloat16),
-        compiler_params=params(16),
-        cost_estimate=pl.CostEstimate(
-            flops=8 * tokens * width, bytes_accessed=4 * tokens * width, transcendentals=0
-        ),
-        name="norm_rows",
-    )(me, gain, *flat)
+        spec = pl.BlockSpec((per_group, rows, part), lambda i, s: (i, 0, 0))
+        kernel = functools.partial(norm_kernel, None, 0)
+        return norm_call(kernel, GROUPS, lambda i, s: (0, i), [spec] * chunks, pieces)
+    order = [0] + partners(head_count)
+    early = order[: 3 * head_count // 4]
+    result = None
+    for some in (early, order[len(early) :]):
+        operands = [pieces[c][k] for k in some for c in range(chunks)]
+        sources = [[n * chunks + c for c in range(chunks)] for n in range(len(some))]
+
+        def column(i, s, some=some):
+            apart = sum(jnp.where(i == n, k, 0) for n, k in enumerate(some))
+            return 0, jnp.bitwise_xor(apart, s[0])
+
+        kernel = functools.partial(norm_kernel, sources, 0 if result is None else 1)
+        result = norm_call(kernel, len(some), column, [whole] * len(operands), operands, result)
+    return result
 
 
 def solution(mesh):

time: 72.9 us -> 66.6 us (0.914)
  the two profiles are of different devices: /device:TPU:29 before, /device:TPU:25 now
where the time goes in v2:
time: 66.6 us; the launch traced here: 66.2 us
  starting transfers between devices  23.4 us (35%)
  Pallas kernels  22.8 us (34%)
  waiting for transfers between devices  12.1 us (18%)
  local copies, waits for them, and re-layouts  7.47 us (11%)
    ppermute x14, starting transfers between devices, body(): got[apart] = lax.ppermute(out[apart], 'head', pairs)  16.5 us
    pallas_call x2, Pallas kernels, local_call(): pl.pallas_call(functools.partial(local_kernel, head_dim, heads, c, far),...  10.7 us
    ppermute x14, waiting for transfers between devices, body(): got[apart] = lax.ppermute(out[apart], 'head', pairs)  7.2 us
    ppermute x6, starting transfers between devices, body(): got = lax.ppermute(moving, 'seq', [(s, s + 1) for s in source])  6.82 us
    ppermute x6, waiting for transfers between devices, body(): got = lax.ppermute(moving, 'seq', [(s, s + 1) for s in source])  4.92 us
    unnamed x22, local copies, waits for them, and re-layouts  4.78 us
    pallas_call x2, Pallas kernels, state_call(): pl.pallas_call(functools.partial(state_kernel, head_dim, c, pieces), in_s...  4.69 us
    pallas_call x2, Pallas kernels, norm_call(): pl.pallas_call(kernel, grid_spec=pltpu.PrefetchScalarGridSpec(num_scalar_...  3.97 us
  transfers between devices with their start and end apart: 20, of which 6 were waited for; matrix products, arithmetic and copies ran while one was open for 4% of the time, Pallas kernels for 29%

profile of v2, /device:TPU:25, one launch (start us, length us, event | category | flops | bytes accessed | tf_op | source)
XLA Modules:
  0.0 66.2 jit_solution(14953943051009518086)
XLA Ops:
  0.0 1.6 %copy-done = bf16[1024,8,128]{2,1,0:T(8,128)(2,1)S(1)} copy-done((bf16[1024,8,128]{2,1,0:T(8,128)(2,1)S(1)}, bf16[1024,8,128]{2,1,0:T(8,128)(2,1)}, u32[]{:S(2)}) %copy-start) | copy-done | bytes 2097176
  2.2 1.6 %copy-done.1 = bf16[1024,1024]{1,0:T(8,128)(2,1)S(1)} copy-done((bf16[1024,1024]{1,0:T(8,128)(2,1)S(1)}, bf16[1024,1024]{1,0:T(8,128)(2,1)}, u32[]{:S(2)}) %copy-start.1) | copy-done | bytes 2097176
  5.3 2.3 %block_state.2 = (f32[128,512]{1,0:T(8,128)S(1)}, bf16[128,512]{1,0:T(8,128)(2,1)S(1)}, f32[8,512]{1,0:T(8,128)S(1)}) custom-call(s32[64]{0:T(128)S(1)} %copy-done.7, f32[16,1024]{1,0:T(8,128)S(1)} %bitcast.26, bf16[1024,128]{1,0:T(8,128)(2,1)S(1)} %bitcast.18, bf16[1024,1024]{1,0:T(8,128)(2,1)S(1)} %copy-done.1), custom_call_target="tpu_custom_call" | custom-call | flops 268435456 | bytes 1572864 | tf_op jit(solution)/shard_map/block_state/pallas_call | solution.py:325
  7.6 1.4 %collective-permute-start = (bf16[128,512]{1,0:T(8,128)(2,1)S(1)}, bf16[128,512]{1,0:T(8,128)(2,1)S(1)}, u32[]{:S(2)}, u32[]{:S(2)}) collective-permute-start(bf16[128,512]{1,0:T(8,128)(2,1)S(1)} %get-tuple-element.32), channel_id=1, source_target_pairs={{0,8},{16,24},{1,9},{17,25},{2,10},{18,26},{3,11},{19,27},{4,12},{... | collective-permute-start | bytes 393224 | tf_op jit(solution)/shard_map/ppermute | solution.py:397
  9.1 2.4 %block_state.3 = (f32[128,512]{1,0:T(8,128)S(1)}, bf16[128,512]{1,0:T(8,128)(2,1)S(1)}, f32[8,512]{1,0:T(8,128)S(1)}) custom-call(s32[64]{0:T(128)S(1)} %copy-done.8, f32[16,1024]{1,0:T(8,128)S(1)} %bitcast.27, bf16[1024,128]{1,0:T(8,128)(2,1)S(1)} %bitcast.19, bf16[1024,1024]{1,0:T(8,128)(2,1)S(1)} %copy-done.1), custom_call_target="tpu_custom_call" | custom-call | flops 268435456 | bytes 1572864 | tf_op jit(solution)/shard_map/block_state/pallas_call | solution.py:325
  11.5 1.3 %collective-permute-start.3 = (bf16[128,512]{1,0:T(8,128)(2,1)S(1)}, bf16[128,512]{1,0:T(8,128)(2,1)S(1)}, u32[]{:S(2)}, u32[]{:S(2)}) collective-permute-start(bf16[128,512]{1,0:T(8,128)(2,1)S(1)} %get-tuple-element.39), channel_id=1, source_target_pairs={{0,8},{16,24},{1,9},{17,25},{2,10},{18,26},{3,11},{19,27},{4,12},{... | collective-permute-start | bytes 393224 | tf_op jit(solution)/shard_map/ppermute | solution.py:397
  12.8 2.1 %constant_dynamic-slice_fusion.1 = bf16[1024,1,128]{2,1,0:T(2,128)(2,1)S(1)} fusion(bf16[1024,8,128]{2,1,0:T(8,128)(2,1)} %param.11, s32[]{:T(128)S(6)} %select_n.11), kind=kLoop, calls=%fused_computation.11 | loop fusion | bytes 524292 | tf_op jit(solution)/shard_map/jit(dynamic_index_in_dim)/dynamic_slice | solution.py:306
  15.7 2.0 %collective-permute-done.3 = bf16[128,512]{1,0:T(8,128)(2,1)S(1)} collective-permute-done((bf16[128,512]{1,0:T(8,128)(2,1)S(1)}, bf16[128,512]{1,0:T(8,128)(2,1)S(1)}, u32[]{:S(2)}, u32[]{:S(2)}) %collective-permute-start.3) | collective-permute-done | bytes 131104 | tf_op jit(solution)/shard_map/ppermute | solution.py:397
  18.5 5.4 %local_mixer.2 = (f32[1024,512]{1,0:T(8,128)S(1)}, bf16[1024,256]{1,0:T(8,128)(2,1)S(1)}) custom-call(s32[64]{0:T(128)S(1)} %copy-done.8, f32[16,1024]{1,0:T(8,128)S(1)} %bitcast.28, f32[7,16,1024]{2,1,0:T(8,128)S(1)} %bitcast.32, bf16[1024,1024]{1,0:T(8,128)(2,1)S(1)} %copy-done.2, bf16[1024,128]{1,0:T(8,128)(2,1)S(1)} %bitcast.22, ...), custom_call_target="tpu_custom_call" | custom-call | flops 1073741824 | bytes 6291456 | tf_op jit(solution)/shard_map/local_mixer/pallas_call | solution.py:348
  25.2 1.5 %collective-permute-start.5 = (bf16[128,512]{1,0:T(8,128)(2,1)S(1)}, bf16[128,512]{1,0:T(8,128)(2,1)S(1)}, u32[]{:S(2)}, u32[]{:S(2)}) collective-permute-start(bf16[128,512]{1,0:T(8,128)(2,1)S(1)} %multiply_convert_fusion), channel_id=1, source_target_pairs={{16,24},{17,25},{18,26},{19,27},{20,28},{21,29},{22,30},{23,31}} | collective-permute-start | bytes 393224 | tf_op jit(solution)/shard_map/ppermute | solution.py:397
  26.7 2.9 %collective-permute-done.2 = bf16[128,512]{1,0:T(8,128)(2,1)S(1)} collective-permute-done((bf16[128,512]{1,0:T(8,128)(2,1)S(1)}, bf16[128,512]{1,0:T(8,128)(2,1)S(1)}, u32[]{:S(2)}, u32[]{:S(2)}) %collective-permute-start.2) | collective-permute-done | bytes 131104 | tf_op jit(solution)/shard_map/ppermute | solution.py:397
  29.7 1.7 %far_and_gate.2 = (bf16[128,512]{1,0:T(8,128)(2,1)S(1)}, bf16[128,512]{1,0:T(8,128)(2,1)S(1)}, bf16[128,512]{1,0:T(8,128)(2,1)S(1)}, bf16[128,512]{1,0:T(8,128)(...) custom-call(s32[1]{0:T(128)} %bitcast.me, ...), custom_call_target="tpu_custom_call" | custom-call | flops 268435456 | bytes 4194304 | tf_op jit(solution)/shard_map/far_and_gate/pallas_call | solution.py:372
  31.4 5.6 %collective-permute-start.6 = (bf16[128,512]{1,0:T(8,128)(2,1)S(1)}, bf16[128,512]{1,0:T(8,128)(2,1)S(1)}, u32[]{:S(2)}, u32[]{:S(2)}) collective-permute-start(bf16[128,512]{1,0:T(8,128)(2,1)S(1)} %get-tuple-element.43), channel_id=1, source_target_pairs={{0,7},{1,6},{2,5},{3,4},{4,3},{5,2},{6,1},{7,0},{8,15},{9,14},{10,... | collective-permute-start | bytes 393224 | tf_op jit(solution)/shard_map/ppermute | solution.py:414
  37.6 2.3 %collective-permute-start.12 = (bf16[128,512]{1,0:T(8,128)(2,1)S(1)}, bf16[128,512]{1,0:T(8,128)(2,1)S(1)}, u32[]{:S(2)}, u32[]{:S(2)}) collective-permute-start(bf16[128,512]{1,0:T(8,128)(2,1)S(1)} %get-tuple-element.49), channel_id=1, source_target_pairs={{0,3},{1,2},{2,1},{3,0},{4,7},{5,6},{6,5},{7,4},{8,11},{9,10},{10,... | collective-permute-start | bytes 393224 | tf_op jit(solution)/shard_map/ppermute | solution.py:414
  40.2 5.4 %local_mixer.3 = (f32[1024,512]{1,0:T(8,128)S(1)}, bf16[1024,256]{1,0:T(8,128)(2,1)S(1)}) custom-call(s32[64]{0:T(128)S(1)} %copy-done.8, f32[16,1024]{1,0:T(8,128)S(1)} %bitcast.29, f32[7,16,1024]{2,1,0:T(8,128)S(1)} %bitcast.33, bf16[1024,1024]{1,0:T(8,128)(2,1)S(1)} %copy-done.2, bf16[1024,128]{1,0:T(8,128)(2,1)S(1)} %bitcast.24, ...), custom_call_target="tpu_custom_call" | custom-call | flops 1073741824 | bytes 6291456 | tf_op jit(solution)/shard_map/local_mixer/pallas_call | solution.py:348
  45.6 1.7 %far_and_gate.3 = (bf16[128,512]{1,0:T(8,128)(2,1)S(1)}, bf16[128,512]{1,0:T(8,128)(2,1)S(1)}, bf16[128,512]{1,0:T(8,128)(2,1)S(1)}, bf16[128,512]{1,0:T(8,128)(...) custom-call(s32[1]{0:T(128)} %bitcast.me, ...), custom_call_target="tpu_custom_call" | custom-call | flops 268435456 | bytes 4194304 | tf_op jit(solution)/shard_map/far_and_gate/pallas_call | solution.py:372
  47.3 1.3 %collective-permute-start.7 = (bf16[128,512]{1,0:T(8,128)(2,1)S(1)}, bf16[128,512]{1,0:T(8,128)(2,1)S(1)}, u32[]{:S(2)}, u32[]{:S(2)}) collective-permute-start(bf16[128,512]{1,0:T(8,128)(2,1)S(1)} %get-tuple-element.44), channel_id=1, source_target_pairs={{0,7},{1,6},{2,5},{3,4},{4,3},{5,2},{6,1},{7,0},{8,15},{9,14},{10,... | collective-permute-start | bytes 393224 | tf_op jit(solution)/shard_map/ppermute | solution.py:414
  49.8 1.7 %collective-permute-start.11 = (bf16[128,512]{1,0:T(8,128)(2,1)S(1)}, bf16[128,512]{1,0:T(8,128)(2,1)S(1)}, u32[]{:S(2)}, u32[]{:S(2)}) collective-permute-start(bf16[128,512]{1,0:T(8,128)(2,1)S(1)} %get-tuple-element.48), channel_id=1, source_target_pairs={{0,5},{1,4},{2,7},{3,6},{4,1},{5,0},{6,3},{7,2},{8,13},{9,12},{10,... | collective-permute-start | bytes 393224 | tf_op jit(solution)/shard_map/ppermute | solution.py:414
  52.2 1.9 %collective-permute-done.7.rest_3_ = bf16[128,512]{1,0:T(8,128)(2,1)S(1)} collective-permute-done((bf16[128,512]{1,0:T(8,128)(2,1)S(1)}, bf16[128,512]{1,0:T(8,128)(2,1)S(1)}, u32[]{:S(2)}, u32[]{:S(2)}) %collective-permute-start.7) | collective-permute-done | bytes 131104 | tf_op jit(solution)/shard_map/ppermute | solution.py:414
  54.4 1.8 %collective-permute-done.9.rest_5_ = bf16[128,512]{1,0:T(8,128)(2,1)S(1)} collective-permute-done((bf16[128,512]{1,0:T(8,128)(2,1)S(1)}, bf16[128,512]{1,0:T(8,128)(2,1)S(1)}, u32[]{:S(2)}, u32[]{:S(2)}) %collective-permute-start.9) | collective-permute-done | bytes 131104 | tf_op jit(solution)/shard_map/ppermute | solution.py:414
  56.2 1.3 %collective-permute-start.18 = (bf16[128,512]{1,0:T(8,128)(2,1)S(1)}, bf16[128,512]{1,0:T(8,128)(2,1)S(1)}, u32[]{:S(2)}, u32[]{:S(2)}) collective-permute-start(bf16[128,512]{1,0:T(8,128)(2,1)S(1)} %get-tuple-element.55), channel_id=1, source_target_pairs={{0,1},{1,0},{2,3},{3,2},{4,5},{5,4},{6,7},{7,6},{8,9},{9,8},{10,11... | collective-permute-start | bytes 393224 | tf_op jit(solution)/shard_map/ppermute | solution.py:414
  57.5 1.9 %collective-permute-done.11.rest_7_ = bf16[128,512]{1,0:T(8,128)(2,1)S(1)} collective-permute-done((bf16[128,512]{1,0:T(8,128)(2,1)S(1)}, bf16[128,512]{1,0:T(8,128)(2,1)S(1)}, u32[]{:S(2)}, u32[]{:S(2)}) %collective-permute-start.11) | collective-permute-done | bytes 131104 | tf_op jit(solution)/shard_map/ppermute | solution.py:414
  60.7 1.5 %collective-permute-done.15.rest_11_ = bf16[128,512]{1,0:T(8,128)(2,1)S(1)} collective-permute-done((bf16[128,512]{1,0:T(8,128)(2,1)S(1)}, bf16[128,512]{1,0:T(8,128)(2,1)S(1)}, u32[]{:S(2)}, u32[]{:S(2)}) %collective-permute-start.15) | collective-permute-done | bytes 131104 | tf_op jit(solution)/shard_map/ppermute | solution.py:414
  62.3 2.9 %norm_rows.2.rest_0_ = bf16[128,8192]{1,0:T(8,128)(2,1)} custom-call(s32[1]{0:T(128)} %bitcast.me, f32[1,8192]{1,0:T(1,128)S(1)} %bitcast.30, bf16[128,512]{1,0:T(8,128)(2,1)S(1)} %get-tuple-element.36.follow.rest_0_, bf16[128,512]{1,0:T(8,128)(2,1)S(1)} %get-tuple-element.42.rest_1_, bf16[128,512]{1,0:T(8,128)(2,1)S(1)} %collective-permute-done.6.rest_2_, ...), custom_call_target="tpu_custom_call" | custom-call | flops 6291456 | bytes 3145728 | tf_op jit(solution)/shard_map/norm_rows/pallas_call | solution.py:424
  (58 shorter events, 10.3 us)
Async XLA Ops:
  7.6 10.8 %copy-start.2 = (bf16[1024,1024]{1,0:T(8,128)(2,1)S(1)}, bf16[1024,1024]{1,0:T(8,128)(2,1)}, u32[]{:S(2)}) copy-start(bf16[1024,1024]{1,0:T(8,128)(2,1)} %values.7) | copy-start | bytes 6291460
  7.6 10.8 %copy-start.9 = (f32[1024,16,7]{0,1,2:T(8,128)S(1)}, f32[1024,16,7]{0,1,2:T(8,128)}, u32[]{:S(2)}) copy-start(f32[1024,16,7]{0,1,2:T(8,128)} %param.13) | copy-start | bytes 1376260
  7.6 7.3 %collective-permute-start = (bf16[128,512]{1,0:T(8,128)(2,1)S(1)}, bf16[128,512]{1,0:T(8,128)(2,1)S(1)}, u32[]{:S(2)}, u32[]{:S(2)}) collective-permute-start(bf16[128,512]{1,0:T(8,128)(2,1)S(1)} %get-tuple-element.32), channel_id=1, source_target_pairs={{0,8},{16,24},{1,9},{17,25},{2,10},{18,26},{3,11},{19,27},{4,12},{... | collective-permute-start | bytes 393224 | tf_op jit(solution)/shard_map/ppermute | solution.py:397
  11.5 6.3 %collective-permute-start.3 = (bf16[128,512]{1,0:T(8,128)(2,1)S(1)}, bf16[128,512]{1,0:T(8,128)(2,1)S(1)}, u32[]{:S(2)}, u32[]{:S(2)}) collective-permute-start(bf16[128,512]{1,0:T(8,128)(2,1)S(1)} %get-tuple-element.39), channel_id=1, source_target_pairs={{0,8},{16,24},{1,9},{17,25},{2,10},{18,26},{3,11},{19,27},{4,12},{... | collective-permute-start | bytes 393224 | tf_op jit(solution)/shard_map/ppermute | solution.py:397
  15.0 8.8 %collective-permute-start.1 = (bf16[128,512]{1,0:T(8,128)(2,1)S(1)}, bf16[128,512]{1,0:T(8,128)(2,1)S(1)}, u32[]{:S(2)}, u32[]{:S(2)}) collective-permute-start(bf16[128,512]{1,0:T(8,128)(2,1)S(1)} %add_convert_fusion.1.follow), channel_id=1, source_target_pairs={{8,16},{9,17},{10,18},{11,19},{12,20},{13,21},{14,22},{15,23}} | collective-permute-start | bytes 393224 | tf_op jit(solution)/shard_map/ppermute | solution.py:397
  17.8 7.4 %collective-permute-start.4 = (bf16[128,512]{1,0:T(8,128)(2,1)S(1)}, bf16[128,512]{1,0:T(8,128)(2,1)S(1)}, u32[]{:S(2)}, u32[]{:S(2)}) collective-permute-start(bf16[128,512]{1,0:T(8,128)(2,1)S(1)} %add_convert_fusion), channel_id=1, source_target_pairs={{8,16},{9,17},{10,18},{11,19},{12,20},{13,21},{14,22},{15,23}} | collective-permute-start | bytes 393224 | tf_op jit(solution)/shard_map/ppermute | solution.py:397
  18.5 11.2 %copy-start.3 = (bf16[1024,1024]{1,0:T(8,128)(2,1)S(1)}, bf16[1024,1024]{1,0:T(8,128)(2,1)}, u32[]{:S(2)}) copy-start(bf16[1024,1024]{1,0:T(8,128)(2,1)} %gate.3) | copy-start | bytes 6291460
  23.9 5.7 %collective-permute-start.2 = (bf16[128,512]{1,0:T(8,128)(2,1)S(1)}, bf16[128,512]{1,0:T(8,128)(2,1)S(1)}, u32[]{:S(2)}, u32[]{:S(2)}) collective-permute-start(bf16[128,512]{1,0:T(8,128)(2,1)S(1)} %multiply_convert_fusion.1), channel_id=1, source_target_pairs={{16,24},{17,25},{18,26},{19,27},{20,28},{21,29},{22,30},{23,31}} | collective-permute-start | bytes 393224 | tf_op jit(solution)/shard_map/ppermute | solution.py:397
  25.2 14.7 %collective-permute-start.5 = (bf16[128,512]{1,0:T(8,128)(2,1)S(1)}, bf16[128,512]{1,0:T(8,128)(2,1)S(1)}, u32[]{:S(2)}, u32[]{:S(2)}) collective-permute-start(bf16[128,512]{1,0:T(8,128)(2,1)S(1)} %multiply_convert_fusion), channel_id=1, source_target_pairs={{16,24},{17,25},{18,26},{19,27},{20,28},{21,29},{22,30},{23,31}} | collective-permute-start | bytes 393224 | tf_op jit(solution)/shard_map/ppermute | solution.py:397
  31.4 15.9 %collective-permute-start.6 = (bf16[128,512]{1,0:T(8,128)(2,1)S(1)}, bf16[128,512]{1,0:T(8,128)(2,1)S(1)}, u32[]{:S(2)}, u32[]{:S(2)}) collective-permute-start(bf16[128,512]{1,0:T(8,128)(2,1)S(1)} %get-tuple-element.43), channel_id=1, source_target_pairs={{0,7},{1,6},{2,5},{3,4},{4,3},{5,2},{6,1},{7,0},{8,15},{9,14},{10,... | collective-permute-start | bytes 393224 | tf_op jit(solution)/shard_map/ppermute | solution.py:414
  37.0 11.6 %collective-permute-start.8 = (bf16[128,512]{1,0:T(8,128)(2,1)S(1)}, bf16[128,512]{1,0:T(8,128)(2,1)S(1)}, u32[]{:S(2)}, u32[]{:S(2)}) collective-permute-start(bf16[128,512]{1,0:T(8,128)(2,1)S(1)} %get-tuple-element.45), channel_id=1, source_target_pairs={{0,6},{1,7},{2,4},{3,5},{4,2},{5,3},{6,0},{7,1},{8,14},{9,15},{10,... | collective-permute-start | bytes 393224 | tf_op jit(solution)/shard_map/ppermute | solution.py:414
  37.2 12.6 %collective-permute-start.10 = (bf16[128,512]{1,0:T(8,128)(2,1)S(1)}, bf16[128,512]{1,0:T(8,128)(2,1)S(1)}, u32[]{:S(2)}, u32[]{:S(2)}) collective-permute-start(bf16[128,512]{1,0:T(8,128)(2,1)S(1)} %get-tuple-element.47), channel_id=1, source_target_pairs={{0,5},{1,4},{2,7},{3,6},{4,1},{5,0},{6,3},{7,2},{8,13},{9,12},{10,... | collective-permute-start | bytes 393224 | tf_op jit(solution)/shard_map/ppermute | solution.py:414
  37.6 13.9 %collective-permute-start.12 = (bf16[128,512]{1,0:T(8,128)(2,1)S(1)}, bf16[128,512]{1,0:T(8,128)(2,1)S(1)}, u32[]{:S(2)}, u32[]{:S(2)}) collective-permute-start(bf16[128,512]{1,0:T(8,128)(2,1)S(1)} %get-tuple-element.49), channel_id=1, source_target_pairs={{0,3},{1,2},{2,1},{3,0},{4,7},{5,6},{6,5},{7,4},{8,11},{9,10},{10,... | collective-permute-start | bytes 393224 | tf_op jit(solution)/shard_map/ppermute | solution.py:414
  39.9 11.6 %collective-permute-start.14 = (bf16[128,512]{1,0:T(8,128)(2,1)S(1)}, bf16[128,512]{1,0:T(8,128)(2,1)S(1)}, u32[]{:S(2)}, u32[]{:S(2)}) collective-permute-start(bf16[128,512]{1,0:T(8,128)(2,1)S(1)} %get-tuple-element.51), channel_id=1, source_target_pairs={{0,4},{1,5},{2,6},{3,7},{4,0},{5,1},{6,2},{7,3},{8,12},{9,13},{10,... | collective-permute-start | bytes 393224 | tf_op jit(solution)/shard_map/ppermute | solution.py:414
  45.6 16.7 %copy-start.6 = (f32[8192]{0:T(1024)S(1)}, f32[8192]{0:T(1024)}, u32[]{:S(2)}) copy-start(f32[8192]{0:T(1024)} %param.15) | copy-start | bytes 98308
  47.3 6.8 %collective-permute-start.7 = (bf16[128,512]{1,0:T(8,128)(2,1)S(1)}, bf16[128,512]{1,0:T(8,128)(2,1)S(1)}, u32[]{:S(2)}, u32[]{:S(2)}) collective-permute-start(bf16[128,512]{1,0:T(8,128)(2,1)S(1)} %get-tuple-element.44), channel_id=1, source_target_pairs={{0,7},{1,6},{2,5},{3,4},{4,3},{5,2},{6,1},{7,0},{8,15},{9,14},{10,... | collective-permute-start | bytes 393224 | tf_op jit(solution)/shard_map/ppermute | solution.py:414
  48.6 7.6 %collective-permute-start.9 = (bf16[128,512]{1,0:T(8,128)(2,1)S(1)}, bf16[128,512]{1,0:T(8,128)(2,1)S(1)}, u32[]{:S(2)}, u32[]{:S(2)}) collective-permute-start(bf16[128,512]{1,0:T(8,128)(2,1)S(1)} %get-tuple-element.46), channel_id=1, source_target_pairs={{0,6},{1,7},{2,4},{3,5},{4,2},{5,3},{6,0},{7,1},{8,14},{9,15},{10,... | collective-permute-start | bytes 393224 | tf_op jit(solution)/shard_map/ppermute | solution.py:414
  49.8 9.7 %collective-permute-start.11 = (bf16[128,512]{1,0:T(8,128)(2,1)S(1)}, bf16[128,512]{1,0:T(8,128)(2,1)S(1)}, u32[]{:S(2)}, u32[]{:S(2)}) collective-permute-start(bf16[128,512]{1,0:T(8,128)(2,1)S(1)} %get-tuple-element.48), channel_id=1, source_target_pairs={{0,5},{1,4},{2,7},{3,6},{4,1},{5,0},{6,3},{7,2},{8,13},{9,12},{10,... | collective-permute-start | bytes 393224 | tf_op jit(solution)/shard_map/ppermute | solution.py:414
  51.5 8.5 %collective-permute-start.13 = (bf16[128,512]{1,0:T(8,128)(2,1)S(1)}, bf16[128,512]{1,0:T(8,128)(2,1)S(1)}, u32[]{:S(2)}, u32[]{:S(2)}) collective-permute-start(bf16[128,512]{1,0:T(8,128)(2,1)S(1)} %get-tuple-element.50), channel_id=1, source_target_pairs={{0,3},{1,2},{2,1},{3,0},{4,7},{5,6},{6,5},{7,4},{8,11},{9,10},{10,... | collective-permute-start | bytes 393224 | tf_op jit(solution)/shard_map/ppermute | solution.py:414
  51.6 10.7 %collective-permute-start.15 = (bf16[128,512]{1,0:T(8,128)(2,1)S(1)}, bf16[128,512]{1,0:T(8,128)(2,1)S(1)}, u32[]{:S(2)}, u32[]{:S(2)}) collective-permute-start(bf16[128,512]{1,0:T(8,128)(2,1)S(1)} %get-tuple-element.52), channel_id=1, source_target_pairs={{0,4},{1,5},{2,6},{3,7},{4,0},{5,1},{6,2},{7,3},{8,12},{9,13},{10,... | collective-permute-start | bytes 393224 | tf_op jit(solution)/shard_map/ppermute | solution.py:414
  54.1 11.0 %collective-permute-start.16 = (bf16[128,512]{1,0:T(8,128)(2,1)S(1)}, bf16[128,512]{1,0:T(8,128)(2,1)S(1)}, u32[]{:S(2)}, u32[]{:S(2)}) collective-permute-start(bf16[128,512]{1,0:T(8,128)(2,1)S(1)} %get-tuple-element.53), channel_id=1, source_target_pairs={{0,2},{1,3},{2,0},{3,1},{4,6},{5,7},{6,4},{7,5},{8,10},{9,11},{10,... | collective-permute-start | bytes 393224 | tf_op jit(solution)/shard_map/ppermute | solution.py:414
  56.2 8.9 %collective-permute-start.18 = (bf16[128,512]{1,0:T(8,128)(2,1)S(1)}, bf16[128,512]{1,0:T(8,128)(2,1)S(1)}, u32[]{:S(2)}, u32[]{:S(2)}) collective-permute-start(bf16[128,512]{1,0:T(8,128)(2,1)S(1)} %get-tuple-element.55), channel_id=1, source_target_pairs={{0,1},{1,0},{2,3},{3,2},{4,5},{5,4},{6,7},{7,6},{8,9},{9,8},{10,11... | collective-permute-start | bytes 393224 | tf_op jit(solution)/shard_map/ppermute | solution.py:414
  59.4 5.7 %collective-permute-start.17 = (bf16[128,512]{1,0:T(8,128)(2,1)S(1)}, bf16[128,512]{1,0:T(8,128)(2,1)S(1)}, u32[]{:S(2)}, u32[]{:S(2)}) collective-permute-start(bf16[128,512]{1,0:T(8,128)(2,1)S(1)} %get-tuple-element.54), channel_id=1, source_target_pairs={{0,2},{1,3},{2,0},{3,1},{4,6},{5,7},{6,4},{7,5},{8,10},{9,11},{10,... | collective-permute-start | bytes 393224 | tf_op jit(solution)/shard_map/ppermute | solution.py:414
  60.0 5.1 %collective-permute-start.19 = (bf16[128,512]{1,0:T(8,128)(2,1)S(1)}, bf16[128,512]{1,0:T(8,128)(2,1)S(1)}, u32[]{:S(2)}, u32[]{:S(2)}) collective-permute-start(bf16[128,512]{1,0:T(8,128)(2,1)S(1)} %get-tuple-element.56), channel_id=1, source_target_pairs={{0,1},{1,0},{2,3},{3,2},{4,5},{5,4},{6,7},{7,6},{8,9},{9,8},{10,11... | collective-permute-start | bytes 393224 | tf_op jit(solution)/shard_map/ppermute | solution.py:414
  (6 other events, 19.6 us)

commit v3 on v2

v3 whole, which is shorter than its diff:
```python
import functools

import jax
import jax.numpy as jnp
from jax import lax
from jax.experimental import pallas as pl
from jax.experimental.pallas import tpu as pltpu
from jax.sharding import PartitionSpec as P

MIXER_HEADS = 128
GROUPS = 8
SPAN = 64
TILE = 2 * SPAN
LANES = 128
WIDE = 2 * LANES
SUBLANES = 8
NEVER = -1e30
HIGHEST = lax.Precision.HIGHEST
MIB = 2**20


def dot(left, right, contract=((1,), (0,)), precision=None):
    return lax.dot_general(
        left, right, (contract, ((), ())), precision=precision, preferred_element_type=jnp.float32
    )


def iota(shape, axis):
    return lax.broadcasted_iota(jnp.int32, shape, axis)


def halves(coef):
    high = coef.astype(jnp.bfloat16)
    low = (coef - high.astype(jnp.float32)).astype(jnp.bfloat16)
    return jnp.concatenate([high, low], axis=1)


def spread(first, width, head_dim):
    row = jnp.bitwise_and(iota((2 * LANES, width), 0), LANES - 1)
    head = jnp.right_shift(iota((2 * LANES, width), 1), head_dim.bit_length() - 1)
    return jnp.where(row == head + first, 1.0, 0.0).astype(jnp.bfloat16)


def head_row(column, width, head_dim):
    shape = (column.shape[0], width)
    head = jnp.right_shift(iota(shape, 1), head_dim.bit_length() - 1)
    return jnp.sum(jnp.where(head == iota(shape, 0), column, 0.0), axis=0, keepdims=True)


def stack_rows(pieces):
    rows = sum(piece.shape[0] for piece in pieces)
    if rows < LANES:
        pieces = pieces + [jnp.zeros((LANES - rows, LANES), jnp.float32)]
    return jnp.transpose(jnp.concatenate(pieces, axis=0))


def tile_rows(decay):
    tiles = decay.shape[1] // TILE
    return jnp.concatenate([decay[:, b * TILE : (b + 1) * TILE] for b in range(tiles)], axis=0)


def resets(docs, tiles):
    first = lax.axis_index("seq") * (tiles * (TILE // SPAN))
    shut = [NEVER * docs[first + s].astype(jnp.float32) for s in range(tiles * (TILE // SPAN))]
    return [shut[2 * b : 2 * b + 2] for b in range(tiles)]


def pack(total, through):
    high = through.astype(jnp.bfloat16)
    low = (through - high.astype(jnp.float32)).astype(jnp.bfloat16)
    return jnp.concatenate([total.astype(jnp.bfloat16), high, low], axis=0)


def state_kernel(
    head_dim,
    chunk,
    pieces,
    docs_far,
    decay_far,
    keys,
    values,
    follow,
    state,
    message,
    through,
    docs,
    decay,
    inputs,
    arrived,
):
    del follow
    heads, tokens = decay.shape
    width = inputs.shape[1]
    column = chunk * width
    small = [
        pltpu.make_async_copy(
            decay_far.at[pl.ds(chunk * heads, heads), :], decay, arrived.at[pieces]
        ),
        pltpu.make_async_copy(docs_far, docs, arrived.at[pieces + 1]),
    ]
    tiles = tokens // TILE
    rows = tokens // pieces
    copies = [
        pltpu.make_async_copy(
            values.at[pl.ds(i * rows, rows), pl.ds(column, width)],
            inputs.at[pl.ds(i * rows, rows), :],
            arrived.at[i],
        )
        for i in range(pieces)
    ]
    for copy in small + copies:
        copy.start()
    for copy in small:
        copy.wait()
    shut = resets(docs, tiles)
    lane = iota((heads, TILE), 1)
    later = jnp.where(iota((TILE, TILE), 0) > iota((TILE, TILE), 1), 1.0, 0.0)
    stacked = tile_rows(decay)
    suffix = dot(stacked, later, precision=HIGHEST)
    totals = jnp.sum(stacked, axis=1, keepdims=True)
    after = jnp.zeros((heads, 1), jnp.float32)
    closed = jnp.float32(0.0)
    scales = [None] * tiles
    for b in reversed(range(tiles)):
        ends = jnp.where(lane < SPAN, closed + shut[b][1], closed)
        scales[b] = jnp.exp(suffix[b * heads : (b + 1) * heads] + after + ends)
        closed = closed + shut[b][1] + shut[b][0]
        after = after + totals[b * heads : (b + 1) * heads]
    terms = halves(stack_rows(scales))
    row = head_row(jnp.exp(after + closed), width, head_dim)
    through[...] = jnp.broadcast_to(row, through.shape)
    owner = jnp.right_shift(
        jnp.bitwise_and(iota((1, 2 * LANES), 1), LANES - 1), heads.bit_length() - 1
    )
    shape = (2 * LANES, width)
    same = jnp.bitwise_and(iota(shape, 0), heads - 1) == jnp.right_shift(
        iota(shape, 1), head_dim.bit_length() - 1
    )
    one_hot = jnp.where(same, 1.0, 0.0).astype(jnp.bfloat16)
    chosen = [
        terms * jnp.where(owner == b, 1.0, 0.0).astype(jnp.bfloat16) for b in range(tiles)
    ]
    total = jnp.zeros(state.shape, jnp.float32)
    for i in range(pieces):
        span = tiles // pieces
        scale = dot(jnp.concatenate(chosen[i * span : (i + 1) * span], axis=0), one_hot)
        copies[i].wait()
        scaled = inputs[i * rows : (i + 1) * rows, :].astype(jnp.float32) * scale
        total += dot(
            keys[i * rows : (i + 1) * rows, :], scaled.astype(jnp.bfloat16), ((0,), (0,))
        )
    state[...] = total
    message[...] = pack(total, through[...])


def merge_kernel(bit, arrivals, follow, *refs):
    del follow
    got, (own, through, before, new_own, new_through, new_before, message) = (
        refs[:arrivals],
        refs[arrivals:],
    )
    states = own.shape[0]
    total = sum(part[...].astype(jnp.float32) for part in got)
    decays = total[states : states + SUBLANES] + total[states + SUBLANES :]
    upper = jnp.bitwise_and(jnp.right_shift(lax.axis_index("seq"), bit), 1).astype(jnp.float32)
    new_before[...] = before[...] * (decays + (1.0 - upper))
    summed = own[...] + total[:states] * through[:1]
    passed = through[...] * (decays + (1.0 - upper))
    new_own[...] = summed
    new_through[...] = passed
    message[...] = pack(summed, passed)


def local_kernel(
    head_dim, heads, chunk, far, docs, decay, weight, values, queries, keys, *rest
):
    out, coefs = rest[-2:]
    tokens, width = out.shape
    column = chunk * width
    mine = slice(chunk * heads, (chunk + 1) * heads)
    tiles = tokens // TILE
    near = tiles.bit_length() - 1
    shut = resets(docs, tiles)
    lane = iota((heads, TILE), 1)
    upto = jnp.where(iota((TILE, TILE), 0) <= iota((TILE, TILE), 1), 1.0, 0.0)
    all_sums = dot(tile_rows(decay[mine, :]), upto, precision=HIGHEST)
    causal = iota((TILE, TILE), 0) >= iota((TILE, TILE), 1)
    early = iota((SPAN, TILE), 1) < SPAN
    per_tile = LANES // head_dim
    lane_head = jnp.right_shift(iota((TILE, LANES), 1), head_dim.bit_length() - 1)
    hot = [spread((2 + i) * heads, width, head_dim) for i in range(near + 1)]

    def here(b):
        return slice(b * TILE, (b + 1) * TILE)

    columns, totals = [], []
    for b in range(tiles):
        sums = all_sums[b * heads : (b + 1) * heads]
        scale = [weight[level, mine, here(b)] for level in range(weight.shape[0])]
        last = jnp.broadcast_to(sums[:, TILE - 1 :], sums.shape)
        opened = sums + jnp.where(lane < SPAN, shut[b][0], shut[b][0] + shut[b][1])
        rows = [sums + jnp.log(scale[0]), sums + jnp.log(scale[1]) + shut[b][1]]
        for k in range(near):
            if (b >> k) & 1:
                since = sum(totals[(b >> k) << k : b], jnp.zeros_like(sums))
                rows.append(jnp.exp(opened + since) * scale[2 + k])
            else:
                rows.append(jnp.zeros_like(sums))
        rows.append(jnp.exp(last - sums + jnp.where(lane < SPAN, shut[b][1], 0.0)))
        since = sum(totals, jnp.zeros_like(sums))
        rows += [jnp.exp(opened + since) * scale[2 + near + m] for m in range(far)]
        totals.append(last + (shut[b][0] + shut[b][1]))
        columns.append(stack_rows(rows))
        coefs[here(b), :] = halves(columns[b])

    whole = (tiles - 1) * TILE
    slots = {}
    if tiles > 1:
        scaled = values[:whole, column : column + width].astype(jnp.float32)
        scaled = (scaled * dot(coefs[:whole, :], hot[near])).astype(jnp.bfloat16)
    held = [None] * near
    for b in range(tiles - 1):
        now = dot(keys[here(b), :], scaled[here(b), :], ((0,), (0,)))
        for k in range(near):
            if not (b >> k) & 1:
                held[k] = now
                slots[k, b >> k] = now.astype(jnp.bfloat16)
                break
            since = sum(totals[(b >> k) << k : b + 1])
            now = now + held[k] * head_row(jnp.exp(since)[:, :1], width, head_dim)

    for b in range(tiles):
        sums = all_sums[b * heads : (b + 1) * heads]
        scores = dot(queries[here(b), :], keys[here(b), :], ((1,), (1,)))
        scores = jnp.where(causal, scores, 0.0)
        block = values[here(b), column : column + width]
        mixed = []
        for part in range(width // LANES):
            values_here = block[:, part * LANES : (part + 1) * LANES]
            left, right = [], []
            for inner in range(per_tile):
                head = part * per_tile + inner
                own = jnp.broadcast_to(columns[b][:, head : head + 1], (TILE, TILE))
                beside = columns[b][SPAN:, heads + head : heads + head + 1]
                below = jnp.where(early, jnp.broadcast_to(beside, (SPAN, TILE)), own[SPAN:])
                gap = jnp.concatenate([own[:SPAN], below], axis=0) - sums[head : head + 1, :]
                left.append((jnp.exp(jnp.minimum(gap, 80.0)) * scores).astype(jnp.bfloat16))
                right.append(jnp.where(lane_head == inner, values_here, jnp.zeros_like(values_here)))
            mixed.append(dot(jnp.concatenate(left, axis=1), jnp.concatenate(right, axis=0)))
        for at in range(0, width, WIDE):
            lanes = slice(at, min(at + WIDE, width))
            total = jnp.concatenate(mixed[at // LANES : (at + WIDE) // LANES], axis=1)
            for k in range(near):
                if (b >> k) & 1:
                    reached = dot(queries[here(b), :], slots[k, (b >> k) - 1][:, lanes])
                    total += dot(coefs[here(b), :], hot[k][:, lanes]) * reached
            out[here(b), lanes] = total


def gate_kernel(
    head_dim, heads, first, column, xor, far, four, arrivals, me, *refs
):
    local, coefs, queries, gate, *rest = refs
    got = [rest[sum(arrivals[:m]) : sum(arrivals[: m + 1])] for m in range(len(arrivals))]
    at = sum(arrivals)
    befores = 0 if four else far
    before, outs = rest[at : at + befores], rest[at + befores :]
    count = len(outs) if xor else outs[0].shape[0]
    rows = local.shape[0] // count
    width = local.shape[1]
    states = queries.shape[1]
    hot = [spread(first + m * heads, width, head_dim) for m in range(far)]
    arrived = []
    if four:
        near_by, next_by, over = (part[...].astype(jnp.float32) for (part,) in got)
        decays = next_by[states : states + SUBLANES] + next_by[states + SUBLANES :]
        last = jnp.where(lax.axis_index("seq") == 3, 1.0, 0.0)
        arrived.append(near_by[:states] + next_by[:states] * last)
        arrived.append(next_by[:states] * (1.0 - last) + over[:states] * decays[:1])
        arrived = [state.astype(jnp.bfloat16) for state in arrived]
    else:
        for m in range(far):
            state = sum(part[:states, :].astype(jnp.float32) for part in got[m])
            arrived.append((state * before[m][:1]).astype(jnp.bfloat16))

    def fill(place, out):
        here = pl.ds(pl.multiple_of(place * rows, rows), rows)
        for at in range(0, width, WIDE):
            end = min(at + WIDE, width)
            total = local[here, at:end]
            for m in range(far):
                reached = dot(queries[here, :], arrived[m][:, at:end])
                total += dot(coefs[here, :], hot[m][:, at:end]) * reached
            opened = 0.5 * gate[here, column + at : column + end].astype(jnp.float32)
            out[:, at:end] = (total * opened * (1.0 + jnp.tanh(opened))).astype(jnp.bfloat16)

    if xor:
        for index, out in enumerate(outs):
            fill(jnp.bitwise_xor(me[0], index), out)
    else:

        @pl.loop(0, count)
        def _(index):
            fill(index, outs[0].at[index])


def norm_kernel(sources, xor, me, gain, *rest):
    parts, (out, done, sent) = rest[:-3], rest[-3:]
    rows, group_width = done.shape[1:]
    some = min(rows, 4 * SUBLANES)
    copies = []
    for index, places in enumerate(sources):
        group = jnp.bitwise_xor(me[0], index) if xor else index
        columns = pl.ds(pl.multiple_of(group * group_width, group_width), group_width)
        for top in range(0, rows, some):
            here = slice(top, top + some)
            blocks = [parts[n][here, :] if at is None else parts[n][at, here, :] for n, at in places]
            blocks = [block.astype(jnp.float32) for block in blocks]
            square = sum(jnp.sum(block * block, axis=1, keepdims=True) for block in blocks)
            scale = lax.rsqrt(square / group_width + 1e-05)
            normed = jnp.concatenate([block * scale for block in blocks], axis=1)
            done[index, here, :] = (normed * gain[:, columns]).astype(out.dtype)
        copies.append(pltpu.make_async_copy(done.at[index], out.at[:, columns], sent.at[index]))
        copies[-1].start()
    for copy in copies:
        copy.wait()


def partners(count):
    return sorted(range(1, count), key=lambda apart: (-apart.bit_count(), -apart))


def params(limit):
    return pltpu.CompilerParams(vmem_limit_bytes=limit * MIB)


def body(values, gate_z, b_keys, c_queries, log_decay, level_weight, doc_start, norm_gain):
    tokens, width = values.shape
    heads_here = log_decay.shape[1]
    head_dim = width // heads_here
    state_size = b_keys.shape[2]
    tiles = tokens // TILE
    near = tiles.bit_length() - 1
    seq_count = lax.axis_size("seq")
    far = seq_count.bit_length() - 1
    head_count = lax.axis_size("head")
    head_index = lax.axis_index("head")
    group_index = head_index * heads_here // (MIXER_HEADS // GROUPS)
    key_rows = lax.dynamic_index_in_dim(b_keys, group_index, 1, keepdims=False)
    query_rows = lax.dynamic_index_in_dim(c_queries, group_index, 1, keepdims=False)
    decay = jnp.transpose(log_decay)
    weight = jnp.transpose(level_weight, (2, 1, 0))
    heads = SUBLANES
    if heads_here < heads:
        short = heads - heads_here
        decay = jnp.pad(decay, ((0, short), (0, 0)))
        weight = jnp.pad(weight, ((0, 0), (0, short), (0, 0)), constant_values=1.0)
    chunks = max(1, heads_here // heads)
    part = width // chunks
    levels = weight.shape[0]
    smem = pl.BlockSpec(memory_space=pltpu.SMEM)

    whole = pl.BlockSpec(memory_space=pltpu.VMEM)
    anywhere = pl.BlockSpec(memory_space=pl.ANY)
    far_away = pl.BlockSpec(memory_space=pltpu.HBM)

    def state_call(c):
        pieces = min(4, tiles)
        return pl.pallas_call(
            functools.partial(state_kernel, head_dim, c, pieces),
            in_specs=[far_away, far_away, whole, far_away, anywhere],
            out_specs=[whole, whole, whole],
            out_shape=[
                jax.ShapeDtypeStruct((state_size, part), jnp.float32),
                jax.ShapeDtypeStruct((state_size + 2 * SUBLANES, part), jnp.bfloat16),
                jax.ShapeDtypeStruct((SUBLANES, part), jnp.float32),
            ],
            scratch_shapes=[
                pltpu.SMEM(doc_start.shape, doc_start.dtype),
                pltpu.VMEM((heads, tokens), jnp.float32),
                pltpu.VMEM((tokens, part), jnp.bfloat16),
                pltpu.SemaphoreType.DMA((pieces + 2,)),
            ],
            compiler_params=params(16),
            cost_estimate=pl.CostEstimate(
                flops=4 * tokens * state_size * part, bytes_accessed=3 * tokens * part, transcendentals=0
            ),
            name="block_state",
        )(doc_start, decay, key_rows, values, key_rows if c == 0 else query_rows)

    def local_call(c, follow):
        return pl.pallas_call(
            functools.partial(local_kernel, head_dim, heads, c, far),
            in_specs=[smem] + [whole] * 5 + [anywhere] * len(follow),
            out_specs=[whole] * 2,
            out_shape=[
                jax.ShapeDtypeStruct((tokens, part), jnp.float32),
                jax.ShapeDtypeStruct((tokens, 2 * LANES), jnp.bfloat16),
            ],
            compiler_params=params(16),
            cost_estimate=pl.CostEstimate(
                flops=16 * tokens * state_size * part, bytes_accessed=12 * tokens * part, transcendentals=0
            ),
            name="local_mixer",
        )(doc_start, decay, weight, values, query_rows, key_rows, *follow)

    rows = tokens // head_count
    direct = head_count == GROUPS
    me = jnp.reshape(head_index, (1,)).astype(jnp.int32)

    def gate_call(c, local, coefs, chain):
        if direct:
            out_shape = [jax.ShapeDtypeStruct((rows, part), jnp.bfloat16)] * head_count
        else:
            out_shape = [jax.ShapeDtypeStruct((head_count, rows, part), jnp.bfloat16)]
        states = [one for got, _ in chain.arrived for one in got]
        if not four:
            states += [before for _, before in chain.arrived]
        arrivals = [len(got) for got, _ in chain.arrived]
        return pl.pallas_call(
            functools.partial(
                gate_kernel,
                head_dim,
                heads,
                (near + 3) * heads,
                c * part,
                direct,
                far,
                four,
                arrivals,
            ),
            in_specs=[smem] + [whole] * (4 + len(states)),
            out_specs=[whole] * len(out_shape),
            out_shape=out_shape,
            compiler_params=params(16),
            cost_estimate=pl.CostEstimate(
                flops=4 * tokens * state_size * part, bytes_accessed=8 * tokens * part, transcendentals=0
            ),
            name="far_and_gate",
        )(me, local, coefs, query_rows, gate_z, *states)

    def merge_call(bit, got, own, through, before, follow):
        return pl.pallas_call(
            functools.partial(merge_kernel, bit, len(got)),
            in_specs=[anywhere] + [whole] * (len(got) + 3),
            out_specs=[whole] * 4,
            out_shape=[
                jax.ShapeDtypeStruct(own.shape, jnp.float32),
                jax.ShapeDtypeStruct(through.shape, jnp.float32),
                jax.ShapeDtypeStruct(through.shape, jnp.float32),
                jax.ShapeDtypeStruct(got[0].shape, jnp.bfloat16),
            ],
            compiler_params=params(4),
            cost_estimate=pl.CostEstimate(
                flops=8 * state_size * part, bytes_accessed=16 * state_size * part, transcendentals=0
            ),
            name="merge_blocks",
        )(follow, *got, own, through, before)

    four = seq_count == 4
    if four:
        phases = [[[(0, 1)]], [[(1, 2), (2, 3)], [(1, 3)]]]
    else:
        phases = []
        for size in (2**bit for bit in range(far)):
            source = range(size - 1, seq_count, 2 * size)
            phases.append([[(s, s + up) for s in source] for up in range(1, size + 1)])

    class Chain:
        def __init__(self, c):
            self.own, self.moving, self.through = state_call(c)
            self.before = jnp.ones_like(self.through)
            self.arrived = []

        def post(self):
            got = [lax.ppermute(self.moving, "seq", p) for p in phases[len(self.arrived)]]
            self.arrived.append((got, self.before))

        def finish(self, follow):
            while self.arrived and len(self.arrived) < far:
                got = self.arrived[-1][0]
                bit = len(self.arrived) - 1
                self.own, self.through, self.before, self.moving = merge_call(
                    bit, got, self.own, self.through, self.before, follow
                )
                self.post()
            if four and len(self.arrived) == far:
                self.arrived = [([one], None) for got, _ in self.arrived for one in got]

    chains = [Chain(c) for c in range(chunks)]
    if far:
        for chain in chains:
            chain.post()
    for chain in chains:
        chain.finish(key_rows)
    pieces = []
    follow = [chains[-1].moving]
    for c in range(chunks):
        if c:
            follow = follow + [one for got, _ in chains[c].arrived for one in got]
        local, coefs = local_call(c, follow)
        out = gate_call(c, local, coefs, chains[c])
        follow = [out[0]]
        if direct:
            got = [out[0]] + [None] * (head_count - 1)
            for apart in partners(head_count):
                pairs = [(source, source ^ apart) for source in range(head_count)]
                got[apart] = lax.ppermute(out[apart], "head", pairs)
            pieces.append(got)
        else:
            pieces.append(lax.all_to_all(out[0], "head", split_axis=0, concat_axis=0))

    gain = jnp.reshape(norm_gain, (1, -1))
    group_width = width * head_count // GROUPS

    if direct:
        operands = [piece for got in pieces for piece in got]
        sources = [[(c * head_count + k, None) for c in range(chunks)] for k in range(head_count)]
    else:
        operands = pieces
        per_group = group_width // width
        sources = [
            [(c, g * per_group + n) for n in range(per_group) for c in range(chunks)]
            for g in range(GROUPS)
        ]
    return pl.pallas_call(
        functools.partial(norm_kernel, sources, direct),
        in_specs=[smem, whole] + [whole] * len(operands),
        out_specs=far_away,
        out_shape=jax.ShapeDtypeStruct((rows, width * head_count), jnp.bfloat16),
        scratch_shapes=[
            pltpu.VMEM((GROUPS, rows, group_width), jnp.bfloat16),
            pltpu.SemaphoreType.DMA((GROUPS,)),
        ],
        compiler_params=params(16),
        cost_estimate=pl.CostEstimate(
            flops=8 * tokens * width, bytes_accessed=4 * tokens * width, transcendentals=0
        ),
        name="norm_rows",
    )(me, gain, *operands)


def solution(mesh):
    in_specs = (
        P("seq", "head"),
        P("seq", "head"),
        P("seq", None, None),
        P("seq", None, None),
        P("seq", "head"),
        P("seq", "head", None),
        P(),
        P(),
    )
    out_specs = P(("seq", "head"), None)
    return jax.shard_map(body, mesh=mesh, in_specs=in_specs, out_specs=out_specs, check_vma=False)
```

time: 66.6 us -> 63.4 us (0.952)
  the two profiles are of different devices: /device:TPU:25 before, /device:TPU:9 now
where the time goes in v3:
time: 63.4 us; the launch traced here: 63.1 us
  starting transfers between devices  25.5 us (40%)
  Pallas kernels  19.9 us (31%)
  waiting for transfers between devices  9.83 us (16%)
  local copies, waits for them, and re-layouts  7.46 us (12%)
    ppermute x14, starting transfers between devices, body(): got[apart] = lax.ppermute(out[apart], 'head', pairs)  15.8 us
    ppermute x6, starting transfers between devices, post(): lax.ppermute(self.moving, 'seq', p)  9.74 us
    ppermute x14, waiting for transfers between devices, body(): got[apart] = lax.ppermute(out[apart], 'head', pairs)  9.54 us
    pallas_call x2, Pallas kernels, local_call(): pl.pallas_call(functools.partial(local_kernel, head_dim, heads, c, far),...  8.99 us
    unnamed x22, local copies, waits for them, and re-layouts  4.77 us
    pallas_call x2, Pallas kernels, state_call(): pl.pallas_call(functools.partial(state_kernel, head_dim, c, pieces), in_s...  4.72 us
    pallas_call x2, Pallas kernels, gate_call(): pl.pallas_call(functools.partial(gate_kernel, head_dim, heads, (near + 3)...  3 us
    dynamic_slice x1, local copies, waits for them, and re-layouts, body(): lax.dynamic_index_in_dim(c_queries, group_index, 1, keepdims=False)  2.14 us
  transfers between devices with their start and end apart: 20, of which 7 were waited for; matrix products, arithmetic and copies ran while one was open for 3% of the time, Pallas kernels for 25%

profile of v3, /device:TPU:9, one launch (start us, length us, event | category | flops | bytes accessed | tf_op | source)
XLA Modules:
  0.0 63.1 jit_solution(13506301810391355423)
XLA Ops:
  0.0 1.6 %copy-done = bf16[1024,8,128]{2,1,0:T(8,128)(2,1)S(1)} copy-done((bf16[1024,8,128]{2,1,0:T(8,128)(2,1)S(1)}, bf16[1024,8,128]{2,1,0:T(8,128)(2,1)}, u32[]{:S(2)}) %copy-start) | copy-done | bytes 2097176
  2.2 1.6 %copy-done.1 = bf16[1024,1024]{1,0:T(8,128)(2,1)S(1)} copy-done((bf16[1024,1024]{1,0:T(8,128)(2,1)S(1)}, bf16[1024,1024]{1,0:T(8,128)(2,1)}, u32[]{:S(2)}) %copy-start.1) | copy-done | bytes 2097176
  5.3 2.4 %block_state.3 = (f32[128,512]{1,0:T(8,128)S(1)}, bf16[144,512]{1,0:T(8,128)(2,1)S(1)}, f32[8,512]{1,0:T(8,128)S(1)}) custom-call(s32[64]{0:T(128)S(1)} %copy-done.7, f32[16,1024]{1,0:T(8,128)S(1)} %bitcast.22, bf16[1024,128]{1,0:T(8,128)(2,1)S(1)} %bitcast.10, bf16[1024,1024]{1,0:T(8,128)(2,1)S(1)} %copy-done.1, bf16[1024,128]{1,0:T(8,128)(2,1)S(1)} %bitcast.11), custom_call_target="tpu_custom_call" | custom-call | flops 268435456 | bytes 1572864 | tf_op jit(solution)/shard_map/block_state/pallas_call | solution.py:369
  7.6 1.3 %collective-permute-start.1 = (bf16[144,512]{1,0:T(8,128)(2,1)S(1)}, bf16[144,512]{1,0:T(8,128)(2,1)S(1)}, u32[]{:S(2)}, u32[]{:S(2)}) collective-permute-start(bf16[144,512]{1,0:T(8,128)(2,1)S(1)} %get-tuple-element.39), channel_id=1, source_target_pairs={{0,8},{1,9},{2,10},{3,11},{4,12},{5,13},{6,14},{7,15}} | collective-permute-start | bytes 442376 | tf_op jit(solution)/shard_map/ppermute | solution.py:476
  8.9 2.1 %constant_dynamic-slice_fusion.1 = bf16[1024,1,128]{2,1,0:T(2,128)(2,1)S(1)} fusion(bf16[1024,8,128]{2,1,0:T(8,128)(2,1)} %param.11, s32[]{:T(128)S(6)} %select_n.11), kind=kLoop, calls=%fused_computation.3 | loop fusion | bytes 524292 | tf_op jit(solution)/shard_map/jit(dynamic_index_in_dim)/dynamic_slice | solution.py:350
  11.2 2.4 %block_state.2 = (f32[128,512]{1,0:T(8,128)S(1)}, bf16[144,512]{1,0:T(8,128)(2,1)S(1)}, f32[8,512]{1,0:T(8,128)S(1)}) custom-call(s32[64]{0:T(128)S(1)} %copy-done.8, f32[16,1024]{1,0:T(8,128)S(1)} %bitcast.23, bf16[1024,128]{1,0:T(8,128)(2,1)S(1)} %bitcast.12, bf16[1024,1024]{1,0:T(8,128)(2,1)S(1)} %copy-done.2, bf16[1024,128]{1,0:T(8,128)(2,1)S(1)} %bitcast.17), custom_call_target="tpu_custom_call" | custom-call | flops 268435456 | bytes 1572864 | tf_op jit(solution)/shard_map/block_state/pallas_call | solution.py:369
  13.5 1.3 %collective-permute-start = (bf16[144,512]{1,0:T(8,128)(2,1)S(1)}, bf16[144,512]{1,0:T(8,128)(2,1)S(1)}, u32[]{:S(2)}, u32[]{:S(2)}) collective-permute-start(bf16[144,512]{1,0:T(8,128)(2,1)S(1)} %get-tuple-element.33), channel_id=1, source_target_pairs={{0,8},{1,9},{2,10},{3,11},{4,12},{5,13},{6,14},{7,15}} | collective-permute-start | bytes 442376 | tf_op jit(solution)/shard_map/ppermute | solution.py:476
  15.6 3.0 %collective-permute-start.3 = (bf16[144,512]{1,0:T(8,128)(2,1)S(1)}, bf16[144,512]{1,0:T(8,128)(2,1)S(1)}, u32[]{:S(2)}, u32[]{:S(2)}) collective-permute-start(bf16[144,512]{1,0:T(8,128)(2,1)S(1)} %get-tuple-element.42), channel_id=1, source_target_pairs={{8,24},{9,25},{10,26},{11,27},{12,28},{13,29},{14,30},{15,31}} | collective-permute-start | bytes 442376 | tf_op jit(solution)/shard_map/ppermute | solution.py:476
  18.6 1.3 %collective-permute-start.2 = (bf16[144,512]{1,0:T(8,128)(2,1)S(1)}, bf16[144,512]{1,0:T(8,128)(2,1)S(1)}, u32[]{:S(2)}, u32[]{:S(2)}) collective-permute-start(bf16[144,512]{1,0:T(8,128)(2,1)S(1)} %get-tuple-element.42), channel_id=1, source_target_pairs={{8,16},{16,24},{9,17},{17,25},{10,18},{18,26},{11,19},{19,27},{12,... | collective-permute-start | bytes 442376 | tf_op jit(solution)/shard_map/ppermute | solution.py:476
  20.9 1.4 %collective-permute-start.12 = (bf16[144,512]{1,0:T(8,128)(2,1)S(1)}, bf16[144,512]{1,0:T(8,128)(2,1)S(1)}, u32[]{:S(2)}, u32[]{:S(2)}) collective-permute-start(bf16[144,512]{1,0:T(8,128)(2,1)S(1)} %get-tuple-element.36.rest_0_), channel_id=1, source_target_pairs={{8,24},{9,25},{10,26},{11,27},{12,28},{13,29},{14,30},{15,31}} | collective-permute-start | bytes 442376 | tf_op jit(solution)/shard_map/ppermute | solution.py:476
  22.3 1.5 %collective-permute-start.11 = (bf16[144,512]{1,0:T(8,128)(2,1)S(1)}, bf16[144,512]{1,0:T(8,128)(2,1)S(1)}, u32[]{:S(2)}, u32[]{:S(2)}) collective-permute-start(bf16[144,512]{1,0:T(8,128)(2,1)S(1)} %get-tuple-element.36.rest_0_), channel_id=1, source_target_pairs={{8,16},{16,24},{9,17},{17,25},{10,18},{18,26},{11,19},{19,27},{12,... | collective-permute-start | bytes 442376 | tf_op jit(solution)/shard_map/ppermute | solution.py:476
  23.8 4.5 %local_mixer.2 = (f32[1024,512]{1,0:T(8,128)S(1)}, bf16[1024,256]{1,0:T(8,128)(2,1)S(1)}) custom-call(s32[64]{0:T(128)S(1)} %copy-done.8, f32[16,1024]{1,0:T(8,128)S(1)} %bitcast.24, f32[7,16,1024]{2,1,0:T(8,128)S(1)} %bitcast.27, bf16[1024,1024]{1,0:T(8,128)(2,1)S(1)} %copy-done.2, bf16[1024,128]{1,0:T(8,128)(2,1)S(1)} %bitcast.18, ...), custom_call_target="tpu_custom_call" | custom-call | flops 1073741824 | bytes 6291456 | tf_op jit(solution)/shard_map/local_mixer/pallas_call | solution.py:392
  28.4 1.5 %far_and_gate.2 = (bf16[128,512]{1,0:T(8,128)(2,1)S(1)}, bf16[128,512]{1,0:T(8,128)(2,1)S(1)}, bf16[128,512]{1,0:T(8,128)(2,1)S(1)}, bf16[128,512]{1,0:T(8,128)(...) custom-call(s32[1]{0:T(128)} %bitcast.me, ...), custom_call_target="tpu_custom_call" | custom-call | flops 268435456 | bytes 4194304 | tf_op jit(solution)/shard_map/far_and_gate/pallas_call | solution.py:420
  29.9 1.6 %collective-permute-start.4 = (bf16[128,512]{1,0:T(8,128)(2,1)S(1)}, bf16[128,512]{1,0:T(8,128)(2,1)S(1)}, u32[]{:S(2)}, u32[]{:S(2)}) collective-permute-start(bf16[128,512]{1,0:T(8,128)(2,1)S(1)} %get-tuple-element.44), channel_id=1, source_target_pairs={{0,1},{1,0},{2,3},{3,2},{4,5},{5,4},{6,7},{7,6},{8,9},{9,8},{10,11... | collective-permute-start | bytes 393224 | tf_op jit(solution)/shard_map/ppermute | solution.py:508
  35.0 4.5 %local_mixer.3 = (f32[1024,512]{1,0:T(8,128)S(1)}, bf16[1024,256]{1,0:T(8,128)(2,1)S(1)}) custom-call(s32[64]{0:T(128)S(1)} %copy-done.8, f32[16,1024]{1,0:T(8,128)S(1)} %bitcast.25, f32[7,16,1024]{2,1,0:T(8,128)S(1)} %bitcast.28, bf16[1024,1024]{1,0:T(8,128)(2,1)S(1)} %copy-done.2, bf16[1024,128]{1,0:T(8,128)(2,1)S(1)} %bitcast.20, ...), custom_call_target="tpu_custom_call" | custom-call | flops 1073741824 | bytes 6291456 | tf_op jit(solution)/shard_map/local_mixer/pallas_call | solution.py:392
  39.5 1.5 %far_and_gate.3 = (bf16[128,512]{1,0:T(8,128)(2,1)S(1)}, bf16[128,512]{1,0:T(8,128)(2,1)S(1)}, bf16[128,512]{1,0:T(8,128)(2,1)S(1)}, bf16[128,512]{1,0:T(8,128)(...) custom-call(s32[1]{0:T(128)} %bitcast.me, ...), custom_call_target="tpu_custom_call" | custom-call | flops 268435456 | bytes 4194304 | tf_op jit(solution)/shard_map/far_and_gate/pallas_call | solution.py:420
  41.0 2.2 %collective-permute-start.9 = (bf16[128,512]{1,0:T(8,128)(2,1)S(1)}, bf16[128,512]{1,0:T(8,128)(2,1)S(1)}, u32[]{:S(2)}, u32[]{:S(2)}) collective-permute-start(bf16[128,512]{1,0:T(8,128)(2,1)S(1)} %get-tuple-element.49), channel_id=1, source_target_pairs={{0,6},{1,7},{2,4},{3,5},{4,2},{5,3},{6,0},{7,1},{8,14},{9,15},{10,... | collective-permute-start | bytes 393224 | tf_op jit(solution)/shard_map/ppermute | solution.py:508
  48.3 2.1 %collective-permute-done.10.rest_7_ = bf16[128,512]{1,0:T(8,128)(2,1)S(1)} collective-permute-done((bf16[128,512]{1,0:T(8,128)(2,1)S(1)}, bf16[128,512]{1,0:T(8,128)(2,1)S(1)}, u32[]{:S(2)}, u32[]{:S(2)}) %collective-permute-start.10) | collective-permute-done | bytes 131104 | tf_op jit(solution)/shard_map/ppermute | solution.py:508
  51.4 1.3 %collective-permute-start.18 = (bf16[128,512]{1,0:T(8,128)(2,1)S(1)}, bf16[128,512]{1,0:T(8,128)(2,1)S(1)}, u32[]{:S(2)}, u32[]{:S(2)}) collective-permute-start(bf16[128,512]{1,0:T(8,128)(2,1)S(1)} %get-tuple-element.59), channel_id=1, source_target_pairs={{0,6},{1,7},{2,4},{3,5},{4,2},{5,3},{6,0},{7,1},{8,14},{9,15},{10,... | collective-permute-start | bytes 393224 | tf_op jit(solution)/shard_map/ppermute | solution.py:508
  52.7 2.3 %collective-permute-start.19 = (bf16[128,512]{1,0:T(8,128)(2,1)S(1)}, bf16[128,512]{1,0:T(8,128)(2,1)S(1)}, u32[]{:S(2)}, u32[]{:S(2)}) collective-permute-start(bf16[128,512]{1,0:T(8,128)(2,1)S(1)} %get-tuple-element.60), channel_id=1, source_target_pairs={{0,7},{1,6},{2,5},{3,4},{4,3},{5,2},{6,1},{7,0},{8,15},{9,14},{10,... | collective-permute-start | bytes 393224 | tf_op jit(solution)/shard_map/ppermute | solution.py:508
  55.1 1.4 %collective-permute-done.15.rest_11_ = bf16[128,512]{1,0:T(8,128)(2,1)S(1)} collective-permute-done((bf16[128,512]{1,0:T(8,128)(2,1)S(1)}, bf16[128,512]{1,0:T(8,128)(2,1)S(1)}, u32[]{:S(2)}, u32[]{:S(2)}) %collective-permute-start.15) | collective-permute-done | bytes 131104 | tf_op jit(solution)/shard_map/ppermute | solution.py:508
  56.5 2.0 %collective-permute-done.18.rest_14_ = bf16[128,512]{1,0:T(8,128)(2,1)S(1)} collective-permute-done((bf16[128,512]{1,0:T(8,128)(2,1)S(1)}, bf16[128,512]{1,0:T(8,128)(2,1)S(1)}, u32[]{:S(2)}, u32[]{:S(2)}) %collective-permute-start.18) | collective-permute-done | bytes 131104 | tf_op jit(solution)/shard_map/ppermute | solution.py:508
  58.4 2.9 %collective-permute-done.19.rest_15_ = bf16[128,512]{1,0:T(8,128)(2,1)S(1)} collective-permute-done((bf16[128,512]{1,0:T(8,128)(2,1)S(1)}, bf16[128,512]{1,0:T(8,128)(2,1)S(1)}, u32[]{:S(2)}, u32[]{:S(2)}) %collective-permute-start.19) | collective-permute-done | bytes 131104 | tf_op jit(solution)/shard_map/ppermute | solution.py:508
  61.3 1.7 %norm_rows.1 = bf16[128,8192]{1,0:T(8,128)(2,1)} custom-call(s32[1]{0:T(128)} %bitcast.me, f32[1,8192]{1,0:T(1,128)S(1)} %bitcast.26, bf16[128,512]{1,0:T(8,128)(2,1)S(1)} %get-tuple-element.43.rest_0_, bf16[128,512]{1,0:T(8,128)(2,1)S(1)} %collective-permute-done.4.rest_1_, bf16[128,512]{1,0:T(8,128)(2,1)S(1)} %collective-permute-done.5.rest_2_, ...), custom_call_target="tpu_custom_call" | custom-call | flops 8388608 | bytes 4194304 | tf_op jit(solution)/shard_map/norm_rows/pallas_call | solution.py:526
  (50 shorter events, 13.5 us)
Async XLA Ops:
  5.3 5.9 %copy-start.8 = (s32[64]{0:T(128)S(1)}, s32[64]{0:T(128)}, u32[]{:S(2)}) copy-start(s32[64]{0:T(128)} %docs.3) | copy-start | bytes 772
  7.6 7.2 %collective-permute-start.1 = (bf16[144,512]{1,0:T(8,128)(2,1)S(1)}, bf16[144,512]{1,0:T(8,128)(2,1)S(1)}, u32[]{:S(2)}, u32[]{:S(2)}) collective-permute-start(bf16[144,512]{1,0:T(8,128)(2,1)S(1)} %get-tuple-element.39), channel_id=1, source_target_pairs={{0,8},{1,9},{2,10},{3,11},{4,12},{5,13},{6,14},{7,15}} | collective-permute-start | bytes 442376 | tf_op jit(solution)/shard_map/ppermute | solution.py:476
  11.1 12.7 %copy-start.9 = (f32[1024,16,7]{0,1,2:T(8,128)S(1)}, f32[1024,16,7]{0,1,2:T(8,128)}, u32[]{:S(2)}) copy-start(f32[1024,16,7]{0,1,2:T(8,128)} %param.13) | copy-start | bytes 1376260
  13.5 6.6 %collective-permute-start = (bf16[144,512]{1,0:T(8,128)(2,1)S(1)}, bf16[144,512]{1,0:T(8,128)(2,1)S(1)}, u32[]{:S(2)}, u32[]{:S(2)}) collective-permute-start(bf16[144,512]{1,0:T(8,128)(2,1)S(1)} %get-tuple-element.33), channel_id=1, source_target_pairs={{0,8},{1,9},{2,10},{3,11},{4,12},{5,13},{6,14},{7,15}} | collective-permute-start | bytes 442376 | tf_op jit(solution)/shard_map/ppermute | solution.py:476
  15.6 12.7 %collective-permute-start.3 = (bf16[144,512]{1,0:T(8,128)(2,1)S(1)}, bf16[144,512]{1,0:T(8,128)(2,1)S(1)}, u32[]{:S(2)}, u32[]{:S(2)}) collective-permute-start(bf16[144,512]{1,0:T(8,128)(2,1)S(1)} %get-tuple-element.42), channel_id=1, source_target_pairs={{8,24},{9,25},{10,26},{11,27},{12,28},{13,29},{14,30},{15,31}} | collective-permute-start | bytes 442376 | tf_op jit(solution)/shard_map/ppermute | solution.py:476
  18.6 9.8 %collective-permute-start.2 = (bf16[144,512]{1,0:T(8,128)(2,1)S(1)}, bf16[144,512]{1,0:T(8,128)(2,1)S(1)}, u32[]{:S(2)}, u32[]{:S(2)}) collective-permute-start(bf16[144,512]{1,0:T(8,128)(2,1)S(1)} %get-tuple-element.42), channel_id=1, source_target_pairs={{8,16},{16,24},{9,17},{17,25},{10,18},{18,26},{11,19},{19,27},{12,... | collective-permute-start | bytes 442376 | tf_op jit(solution)/shard_map/ppermute | solution.py:476
  20.9 7.5 %copy-start.3 = (bf16[1024,1024]{1,0:T(8,128)(2,1)S(1)}, bf16[1024,1024]{1,0:T(8,128)(2,1)}, u32[]{:S(2)}) copy-start(bf16[1024,1024]{1,0:T(8,128)(2,1)} %refs_3_.3) | copy-start | bytes 6291460
  20.9 12.3 %collective-permute-start.12 = (bf16[144,512]{1,0:T(8,128)(2,1)S(1)}, bf16[144,512]{1,0:T(8,128)(2,1)S(1)}, u32[]{:S(2)}, u32[]{:S(2)}) collective-permute-start(bf16[144,512]{1,0:T(8,128)(2,1)S(1)} %get-tuple-element.36.rest_0_), channel_id=1, source_target_pairs={{8,24},{9,25},{10,26},{11,27},{12,28},{13,29},{14,30},{15,31}} | collective-permute-start | bytes 442376 | tf_op jit(solution)/shard_map/ppermute | solution.py:476
  22.3 12.1 %collective-permute-start.11 = (bf16[144,512]{1,0:T(8,128)(2,1)S(1)}, bf16[144,512]{1,0:T(8,128)(2,1)S(1)}, u32[]{:S(2)}, u32[]{:S(2)}) collective-permute-start(bf16[144,512]{1,0:T(8,128)(2,1)S(1)} %get-tuple-element.36.rest_0_), channel_id=1, source_target_pairs={{8,16},{16,24},{9,17},{17,25},{10,18},{18,26},{11,19},{19,27},{12,... | collective-permute-start | bytes 442376 | tf_op jit(solution)/shard_map/ppermute | solution.py:476
  29.9 11.2 %collective-permute-start.4 = (bf16[128,512]{1,0:T(8,128)(2,1)S(1)}, bf16[128,512]{1,0:T(8,128)(2,1)S(1)}, u32[]{:S(2)}, u32[]{:S(2)}) collective-permute-start(bf16[128,512]{1,0:T(8,128)(2,1)S(1)} %get-tuple-element.44), channel_id=1, source_target_pairs={{0,1},{1,0},{2,3},{3,2},{4,5},{5,4},{6,7},{7,6},{8,9},{9,8},{10,11... | collective-permute-start | bytes 393224 | tf_op jit(solution)/shard_map/ppermute | solution.py:508
  31.5 11.8 %collective-permute-start.5 = (bf16[128,512]{1,0:T(8,128)(2,1)S(1)}, bf16[128,512]{1,0:T(8,128)(2,1)S(1)}, u32[]{:S(2)}, u32[]{:S(2)}) collective-permute-start(bf16[128,512]{1,0:T(8,128)(2,1)S(1)} %get-tuple-element.45), channel_id=1, source_target_pairs={{0,2},{1,3},{2,0},{3,1},{4,6},{5,7},{6,4},{7,5},{8,10},{9,11},{10,... | collective-permute-start | bytes 393224 | tf_op jit(solution)/shard_map/ppermute | solution.py:508
  32.7 11.0 %collective-permute-start.6 = (bf16[128,512]{1,0:T(8,128)(2,1)S(1)}, bf16[128,512]{1,0:T(8,128)(2,1)S(1)}, u32[]{:S(2)}, u32[]{:S(2)}) collective-permute-start(bf16[128,512]{1,0:T(8,128)(2,1)S(1)} %get-tuple-element.46), channel_id=1, source_target_pairs={{0,3},{1,2},{2,1},{3,0},{4,7},{5,6},{6,5},{7,4},{8,11},{9,10},{10,... | collective-permute-start | bytes 393224 | tf_op jit(solution)/shard_map/ppermute | solution.py:508
  33.2 10.7 %collective-permute-start.7 = (bf16[128,512]{1,0:T(8,128)(2,1)S(1)}, bf16[128,512]{1,0:T(8,128)(2,1)S(1)}, u32[]{:S(2)}, u32[]{:S(2)}) collective-permute-start(bf16[128,512]{1,0:T(8,128)(2,1)S(1)} %get-tuple-element.47), channel_id=1, source_target_pairs={{0,4},{1,5},{2,6},{3,7},{4,0},{5,1},{6,2},{7,3},{8,12},{9,13},{10,... | collective-permute-start | bytes 393224 | tf_op jit(solution)/shard_map/ppermute | solution.py:508
  34.4 10.7 %collective-permute-start.8 = (bf16[128,512]{1,0:T(8,128)(2,1)S(1)}, bf16[128,512]{1,0:T(8,128)(2,1)S(1)}, u32[]{:S(2)}, u32[]{:S(2)}) collective-permute-start(bf16[128,512]{1,0:T(8,128)(2,1)S(1)} %get-tuple-element.48), channel_id=1, source_target_pairs={{0,5},{1,4},{2,7},{3,6},{4,1},{5,0},{6,3},{7,2},{8,13},{9,12},{10,... | collective-permute-start | bytes 393224 | tf_op jit(solution)/shard_map/ppermute | solution.py:508
  39.5 21.8 %copy-start.6 = (f32[8192]{0:T(1024)S(1)}, f32[8192]{0:T(1024)}, u32[]{:S(2)}) copy-start(f32[8192]{0:T(1024)} %param.15) | copy-start | bytes 98308
  41.0 6.0 %collective-permute-start.9 = (bf16[128,512]{1,0:T(8,128)(2,1)S(1)}, bf16[128,512]{1,0:T(8,128)(2,1)S(1)}, u32[]{:S(2)}, u32[]{:S(2)}) collective-permute-start(bf16[128,512]{1,0:T(8,128)(2,1)S(1)} %get-tuple-element.49), channel_id=1, source_target_pairs={{0,6},{1,7},{2,4},{3,5},{4,2},{5,3},{6,0},{7,1},{8,14},{9,15},{10,... | collective-permute-start | bytes 393224 | tf_op jit(solution)/shard_map/ppermute | solution.py:508
  43.3 7.1 %collective-permute-start.10 = (bf16[128,512]{1,0:T(8,128)(2,1)S(1)}, bf16[128,512]{1,0:T(8,128)(2,1)S(1)}, u32[]{:S(2)}, u32[]{:S(2)}) collective-permute-start(bf16[128,512]{1,0:T(8,128)(2,1)S(1)} %get-tuple-element.50), channel_id=1, source_target_pairs={{0,7},{1,6},{2,5},{3,4},{4,3},{5,2},{6,1},{7,0},{8,15},{9,14},{10,... | collective-permute-start | bytes 393224 | tf_op jit(solution)/shard_map/ppermute | solution.py:508
  43.7 7.7 %collective-permute-start.13 = (bf16[128,512]{1,0:T(8,128)(2,1)S(1)}, bf16[128,512]{1,0:T(8,128)(2,1)S(1)}, u32[]{:S(2)}, u32[]{:S(2)}) collective-permute-start(bf16[128,512]{1,0:T(8,128)(2,1)S(1)} %get-tuple-element.54), channel_id=1, source_target_pairs={{0,1},{1,0},{2,3},{3,2},{4,5},{5,4},{6,7},{7,6},{8,9},{9,8},{10,11... | collective-permute-start | bytes 393224 | tf_op jit(solution)/shard_map/ppermute | solution.py:508
  43.9 8.8 %collective-permute-start.14 = (bf16[128,512]{1,0:T(8,128)(2,1)S(1)}, bf16[128,512]{1,0:T(8,128)(2,1)S(1)}, u32[]{:S(2)}, u32[]{:S(2)}) collective-permute-start(bf16[128,512]{1,0:T(8,128)(2,1)S(1)} %get-tuple-element.55), channel_id=1, source_target_pairs={{0,2},{1,3},{2,0},{3,1},{4,6},{5,7},{6,4},{7,5},{8,10},{9,11},{10,... | collective-permute-start | bytes 393224 | tf_op jit(solution)/shard_map/ppermute | solution.py:508
  45.1 11.4 %collective-permute-start.15 = (bf16[128,512]{1,0:T(8,128)(2,1)S(1)}, bf16[128,512]{1,0:T(8,128)(2,1)S(1)}, u32[]{:S(2)}, u32[]{:S(2)}) collective-permute-start(bf16[128,512]{1,0:T(8,128)(2,1)S(1)} %get-tuple-element.56), channel_id=1, source_target_pairs={{0,3},{1,2},{2,1},{3,0},{4,7},{5,6},{6,5},{7,4},{8,11},{9,10},{10,... | collective-permute-start | bytes 393224 | tf_op jit(solution)/shard_map/ppermute | solution.py:508
  47.1 9.4 %collective-permute-start.16 = (bf16[128,512]{1,0:T(8,128)(2,1)S(1)}, bf16[128,512]{1,0:T(8,128)(2,1)S(1)}, u32[]{:S(2)}, u32[]{:S(2)}) collective-permute-start(bf16[128,512]{1,0:T(8,128)(2,1)S(1)} %get-tuple-element.57), channel_id=1, source_target_pairs={{0,4},{1,5},{2,6},{3,7},{4,0},{5,1},{6,2},{7,3},{8,12},{9,13},{10,... | collective-permute-start | bytes 393224 | tf_op jit(solution)/shard_map/ppermute | solution.py:508
  50.4 6.1 %collective-permute-start.17 = (bf16[128,512]{1,0:T(8,128)(2,1)S(1)}, bf16[128,512]{1,0:T(8,128)(2,1)S(1)}, u32[]{:S(2)}, u32[]{:S(2)}) collective-permute-start(bf16[128,512]{1,0:T(8,128)(2,1)S(1)} %get-tuple-element.58), channel_id=1, source_target_pairs={{0,5},{1,4},{2,7},{3,6},{4,1},{5,0},{6,3},{7,2},{8,13},{9,12},{10,... | collective-permute-start | bytes 393224 | tf_op jit(solution)/shard_map/ppermute | solution.py:508
  51.4 7.0 %collective-permute-start.18 = (bf16[128,512]{1,0:T(8,128)(2,1)S(1)}, bf16[128,512]{1,0:T(8,128)(2,1)S(1)}, u32[]{:S(2)}, u32[]{:S(2)}) collective-permute-start(bf16[128,512]{1,0:T(8,128)(2,1)S(1)} %get-tuple-element.59), channel_id=1, source_target_pairs={{0,6},{1,7},{2,4},{3,5},{4,2},{5,3},{6,0},{7,1},{8,14},{9,15},{10,... | collective-permute-start | bytes 393224 | tf_op jit(solution)/shard_map/ppermute | solution.py:508
  52.7 8.5 %collective-permute-start.19 = (bf16[128,512]{1,0:T(8,128)(2,1)S(1)}, bf16[128,512]{1,0:T(8,128)(2,1)S(1)}, u32[]{:S(2)}, u32[]{:S(2)}) collective-permute-start(bf16[128,512]{1,0:T(8,128)(2,1)S(1)} %get-tuple-element.60), channel_id=1, source_target_pairs={{0,7},{1,6},{2,5},{3,4},{4,3},{5,2},{6,1},{7,0},{8,15},{9,14},{10,... | collective-permute-start | bytes 393224 | tf_op jit(solution)/shard_map/ppermute | solution.py:508
  (6 other events, 16.4 us)

commit v4 on v3

--- a/solution.py
+++ b/solution.py
@@ -71,64 +71,38 @@
     return jnp.concatenate([total.astype(jnp.bfloat16), high, low], axis=0)
 
 
-def state_kernel(
-    head_dim,
-    chunk,
-    pieces,
-    docs_far,
-    decay_far,
-    keys,
-    values,
-    follow,
-    state,
-    message,
-    through,
-    docs,
-    decay,
-    inputs,
-    arrived,
-):
-    del follow
-    heads, tokens = decay.shape
-    width = inputs.shape[1]
-    column = chunk * width
-    small = [
-        pltpu.make_async_copy(
-            decay_far.at[pl.ds(chunk * heads, heads), :], decay, arrived.at[pieces]
-        ),
-        pltpu.make_async_copy(docs_far, docs, arrived.at[pieces + 1]),
-    ]
-    tiles = tokens // TILE
-    rows = tokens // pieces
-    copies = [
-        pltpu.make_async_copy(
-            values.at[pl.ds(i * rows, rows), pl.ds(column, width)],
-            inputs.at[pl.ds(i * rows, rows), :],
-            arrived.at[i],
-        )
-        for i in range(pieces)
-    ]
-    for copy in small + copies:
-        copy.start()
-    for copy in small:
-        copy.wait()
+def decay_kernel(head_dim, heads, docs, decay, *outs):
+    chunks = len(outs) // 2
+    tiles = decay.shape[1] // TILE
     shut = resets(docs, tiles)
     lane = iota((heads, TILE), 1)
     later = jnp.where(iota((TILE, TILE), 0) > iota((TILE, TILE), 1), 1.0, 0.0)
-    stacked = tile_rows(decay)
-    suffix = dot(stacked, later, precision=HIGHEST)
-    totals = jnp.sum(stacked, axis=1, keepdims=True)
-    after = jnp.zeros((heads, 1), jnp.float32)
-    closed = jnp.float32(0.0)
-    scales = [None] * tiles
-    for b in reversed(range(tiles)):
-        ends = jnp.where(lane < SPAN, closed + shut[b][1], closed)
-        scales[b] = jnp.exp(suffix[b * heads : (b + 1) * heads] + after + ends)
-        closed = closed + shut[b][1] + shut[b][0]
-        after = after + totals[b * heads : (b + 1) * heads]
-    terms = halves(stack_rows(scales))
-    row = head_row(jnp.exp(after + closed), width, head_dim)
-    through[...] = jnp.broadcast_to(row, through.shape)
+    for c in range(chunks):
+        terms, through = outs[2 * c : 2 * c + 2]
+        stacked = tile_rows(decay[c * heads : (c + 1) * heads, :])
+        suffix = dot(stacked, later, precision=HIGHEST)
+        totals = jnp.sum(stacked, axis=1, keepdims=True)
+        after = jnp.zeros((heads, 1), jnp.float32)
+        closed = jnp.float32(0.0)
+        scales = [None] * tiles
+        for b in reversed(range(tiles)):
+            ends = jnp.where(lane < SPAN, closed + shut[b][1], closed)
+            scales[b] = jnp.exp(suffix[b * heads : (b + 1) * heads] + after + ends)
+            closed = closed + shut[b][1] + shut[b][0]
+            after = after + totals[b * heads : (b + 1) * heads]
+        terms[...] = halves(stack_rows(scales))
+        row = head_row(jnp.exp(after + closed), through.shape[1], head_dim)
+        through[...] = jnp.broadcast_to(row, through.shape)
+
+
+def state_kernel(
+    head_dim, heads, column, pieces, terms, through, keys, values, follow, state, message
+):
+    del follow
+    width = state.shape[1]
+    tokens = keys.shape[0]
+    tiles = tokens // TILE
+    rows = tokens // pieces
     owner = jnp.right_shift(
         jnp.bitwise_and(iota((1, 2 * LANES), 1), LANES - 1), heads.bit_length() - 1
     )
@@ -138,17 +112,15 @@
     )
     one_hot = jnp.where(same, 1.0, 0.0).astype(jnp.bfloat16)
     chosen = [
-        terms * jnp.where(owner == b, 1.0, 0.0).astype(jnp.bfloat16) for b in range(tiles)
+        terms[...] * jnp.where(owner == b, 1.0, 0.0).astype(jnp.bfloat16) for b in range(tiles)
     ]
     total = jnp.zeros(state.shape, jnp.float32)
     for i in range(pieces):
         span = tiles // pieces
+        here = slice(i * rows, (i + 1) * rows)
         scale = dot(jnp.concatenate(chosen[i * span : (i + 1) * span], axis=0), one_hot)
-        copies[i].wait()
-        scaled = inputs[i * rows : (i + 1) * rows, :].astype(jnp.float32) * scale
-        total += dot(
-            keys[i * rows : (i + 1) * rows, :], scaled.astype(jnp.bfloat16), ((0,), (0,))
-        )
+        scaled = values[here, column : column + width].astype(jnp.float32) * scale
+        total += dot(keys[here, :], scaled.astype(jnp.bfloat16), ((0,), (0,)))
     state[...] = total
     message[...] = pack(total, through[...])
 
@@ -258,13 +230,14 @@
 
 
 def gate_kernel(
-    head_dim, heads, first, column, xor, far, four, arrivals, me, *refs
+    head_dim, heads, first, column, xor, far, four, arrivals, joined, me, *refs
 ):
     local, coefs, queries, gate, *rest = refs
     got = [rest[sum(arrivals[:m]) : sum(arrivals[: m + 1])] for m in range(len(arrivals))]
     at = sum(arrivals)
     befores = 0 if four else far
-    before, outs = rest[at : at + befores], rest[at + befores :]
+    before, rest = rest[at : at + befores], rest[at + befores :]
+    earlier, outs = rest[: sum(joined.values())], rest[sum(joined.values()) :]
     count = len(outs) if xor else outs[0].shape[0]
     rows = local.shape[0] // count
     width = local.shape[1]
@@ -295,8 +268,13 @@
             out[:, at:end] = (total * opened * (1.0 + jnp.tanh(opened))).astype(jnp.bfloat16)
 
     if xor:
+        at = 0
         for index, out in enumerate(outs):
-            fill(jnp.bitwise_xor(me[0], index), out)
+            prior = joined.get(index, 0) * width
+            for start in range(0, prior, width):
+                out[:, start : start + width] = earlier[at][...]
+                at += 1
+            fill(jnp.bitwise_xor(me[0], index), out.at[:, prior : prior + width])
     else:
 
         @pl.loop(0, count)
@@ -326,7 +304,9 @@
         copy.wait()
 
 
-def partners(count):
+def partners(count, final):
+    if final:
+        return sorted(range(1, count), key=lambda apart: (apart in (1, 4), apart != 5, -apart))
     return sorted(range(1, count), key=lambda apart: (-apart.bit_count(), -apart))
 
 
@@ -364,29 +344,40 @@
     anywhere = pl.BlockSpec(memory_space=pl.ANY)
     far_away = pl.BlockSpec(memory_space=pltpu.HBM)
 
+    decays = pl.pallas_call(
+        functools.partial(decay_kernel, head_dim, heads),
+        in_specs=[smem, whole],
+        out_specs=[whole] * (2 * chunks),
+        out_shape=[
+            jax.ShapeDtypeStruct((LANES, 2 * LANES), jnp.bfloat16),
+            jax.ShapeDtypeStruct((SUBLANES, part), jnp.float32),
+        ]
+        * chunks,
+        compiler_params=params(8),
+        cost_estimate=pl.CostEstimate(
+            flops=tokens * width, bytes_accessed=4 * tokens * part, transcendentals=0
+        ),
+        name="token_decays",
+    )(doc_start, decay)
+
     def state_call(c):
+        terms, through = decays[2 * c : 2 * c + 2]
         pieces = min(4, tiles)
-        return pl.pallas_call(
-            functools.partial(state_kernel, head_dim, c, pieces),
-            in_specs=[far_away, far_away, whole, far_away, anywhere],
-            out_specs=[whole, whole, whole],
+        state, message = pl.pallas_call(
+            functools.partial(state_kernel, head_dim, heads, c * part, pieces),
+            in_specs=[whole, whole, whole, whole, anywhere],
+            out_specs=[whole, whole],
             out_shape=[
                 jax.ShapeDtypeStruct((state_size, part), jnp.float32),
                 jax.ShapeDtypeStruct((state_size + 2 * SUBLANES, part), jnp.bfloat16),
-                jax.ShapeDtypeStruct((SUBLANES, part), jnp.float32),
-            ],
-            scratch_shapes=[
-                pltpu.SMEM(doc_start.shape, doc_start.dtype),
-                pltpu.VMEM((heads, tokens), jnp.float32),
-                pltpu.VMEM((tokens, part), jnp.bfloat16),
-                pltpu.SemaphoreType.DMA((pieces + 2,)),
             ],
             compiler_params=params(16),
             cost_estimate=pl.CostEstimate(
                 flops=4 * tokens * state_size * part, bytes_accessed=3 * tokens * part, transcendentals=0
             ),
             name="block_state",
-        )(doc_start, decay, key_rows, values, key_rows if c == 0 else query_rows)
+        )(terms, through, key_rows, values, key_rows if c == 0 else query_rows)
+        return state, message, through
 
     def local_call(c, follow):
         return pl.pallas_call(
@@ -408,15 +399,20 @@
     direct = head_count == GROUPS
     me = jnp.reshape(head_index, (1,)).astype(jnp.int32)
 
-    def gate_call(c, local, coefs, chain):
+    def gate_call(c, local, coefs, chain, earlier):
+        joined = {apart: len(kept) for apart, kept in earlier.items()}
         if direct:
-            out_shape = [jax.ShapeDtypeStruct((rows, part), jnp.bfloat16)] * head_count
+            out_shape = [
+                jax.ShapeDtypeStruct((rows, part * (1 + joined.get(k, 0))), jnp.bfloat16)
+                for k in range(head_count)
+            ]
         else:
             out_shape = [jax.ShapeDtypeStruct((head_count, rows, part), jnp.bfloat16)]
         states = [one for got, _ in chain.arrived for one in got]
         if not four:
             states += [before for _, before in chain.arrived]
         arrivals = [len(got) for got, _ in chain.arrived]
+        states += [one for apart in sorted(earlier) for one in earlier[apart]]
         return pl.pallas_call(
             functools.partial(
                 gate_kernel,
@@ -428,6 +424,7 @@
                 far,
                 four,
                 arrivals,
+                joined,
             ),
             in_specs=[smem] + [whole] * (4 + len(states)),
             out_specs=[whole] * len(out_shape),
@@ -493,17 +490,23 @@
             chain.post()
     for chain in chains:
         chain.finish(key_rows)
+    held = (1, 2)
+    kept = {}
     pieces = []
     follow = [chains[-1].moving]
     for c in range(chunks):
         if c:
             follow = follow + [one for got, _ in chains[c].arrived for one in got]
         local, coefs = local_call(c, follow)
-        out = gate_call(c, local, coefs, chains[c])
+        final = c + 1 == chunks
+        out = gate_call(c, local, coefs, chains[c], kept if final else {})
         follow = [out[0]]
         if direct:
             got = [out[0]] + [None] * (head_count - 1)
-            for apart in partners(head_count):
+            for apart in partners(head_count, final):
+                if not final and apart in held:
+                    kept.setdefault(apart, []).append(out[apart])
+                    continue
                 pairs = [(source, source ^ apart) for source in range(head_count)]
                 got[apart] = lax.ppermute(out[apart], "head", pairs)
             pieces.append(got)
@@ -514,8 +517,11 @@
     group_width = width * head_count // GROUPS
 
     if direct:
-        operands = [piece for got in pieces for piece in got]
-        sources = [[(c * head_count + k, None) for c in range(chunks)] for k in range(head_count)]
+        operands, sources = [], []
+        for k in range(head_count):
+            mine = [got[k] for got in pieces if got[k] is not None]
+            sources.append([(len(operands) + n, None) for n in range(len(mine))])
+            operands += mine
     else:
         operands = pieces
         per_group = group_width // width

time: 63.4 us -> 61.3 us (0.967)
  starting transfers between devices: 25.5 us -> 23.3 us
  waiting for transfers between devices: 9.83 us -> 11.8 us
  Pallas kernels: 19.9 us -> 18 us
    pallas_call x2 -> x3, Pallas kernels: 4.72 us -> 2.84 us  [the longest x2 1.97 us: state_call(): pl.pallas_call(functools.partial(state_kernel, head_dim, heads, c * part,...]
    ppermute x14 -> x12, starting transfers between devices: 15.8 us -> 14.3 us  [body(): got[apart] = lax.ppermute(out[apart], 'head', pairs)]
    ppermute x14 -> x12, waiting for transfers between devices: 9.54 us -> 10.7 us  [body(): got[apart] = lax.ppermute(out[apart], 'head', pairs)]
    ppermute x6, waiting for transfers between devices: 0.29 us -> 1.06 us  [post(): lax.ppermute(self.moving, 'seq', p)]
    ppermute x6, starting transfers between devices: 9.74 us -> 9 us  [post(): lax.ppermute(self.moving, 'seq', p)]
  transfers between devices with their start and end apart: 20 -> 18, of which waited for: 7 -> 6; matrix products, arithmetic and copies ran while one was open for 3% -> 4% of each run, Pallas kernels for 25% -> 24%
where the time goes in v4:
time: 61.3 us; the launch traced here: 61 us
  starting transfers between devices  23.3 us (38%)
  Pallas kernels  18 us (29%)
  waiting for transfers between devices  11.8 us (19%)
  local copies, waits for them, and re-layouts  7.46 us (12%)
    ppermute x12, starting transfers between devices, body(): got[apart] = lax.ppermute(out[apart], 'head', pairs)  14.3 us
    ppermute x12, waiting for transfers between devices, body(): got[apart] = lax.ppermute(out[apart], 'head', pairs)  10.7 us
    pallas_call x2, Pallas kernels, local_call(): pl.pallas_call(functools.partial(local_kernel, head_dim, heads, c, far),...  9.01 us
    ppermute x6, starting transfers between devices, post(): lax.ppermute(self.moving, 'seq', p)  9 us
    unnamed x22, local copies, waits for them, and re-layouts  4.77 us
    pallas_call x2, Pallas kernels, gate_call(): pl.pallas_call(functools.partial(gate_kernel, head_dim, heads, (near + 3)...  2.98 us
    dynamic_slice x1, local copies, waits for them, and re-layouts, body(): lax.dynamic_index_in_dim(c_queries, group_index, 1, keepdims=False)  2.14 us
    pallas_call x2, Pallas kernels, state_call(): pl.pallas_call(functools.partial(state_kernel, head_dim, heads, c * part,...  1.97 us
  transfers between devices with their start and end apart: 18, of which 6 were waited for; matrix products, arithmetic and copies ran while one was open for 4% of the time, Pallas kernels for 24%

profile of v4, /device:TPU:9, one launch (start us, length us, event | category | flops | bytes accessed | tf_op | source)
XLA Modules:
  0.0 61.0 jit_solution(12682082029888326567)
XLA Ops:
  0.0 1.6 %copy-done = bf16[1024,8,128]{2,1,0:T(8,128)(2,1)S(1)} copy-done((bf16[1024,8,128]{2,1,0:T(8,128)(2,1)S(1)}, bf16[1024,8,128]{2,1,0:T(8,128)(2,1)}, u32[]{:S(2)}) %copy-start) | copy-done | bytes 2097176
  4.6 1.6 %copy-done.2 = bf16[1024,1024]{1,0:T(8,128)(2,1)S(1)} copy-done((bf16[1024,1024]{1,0:T(8,128)(2,1)S(1)}, bf16[1024,1024]{1,0:T(8,128)(2,1)}, u32[]{:S(2)}) %copy-start.2) | copy-done | bytes 2097176
  7.2 1.3 %collective-permute-start.1 = (bf16[144,512]{1,0:T(8,128)(2,1)S(1)}, bf16[144,512]{1,0:T(8,128)(2,1)S(1)}, u32[]{:S(2)}, u32[]{:S(2)}) collective-permute-start(bf16[144,512]{1,0:T(8,128)(2,1)S(1)} %get-tuple-element.44), channel_id=1, source_target_pairs={{0,8},{1,9},{2,10},{3,11},{4,12},{5,13},{6,14},{7,15}} | collective-permute-start | bytes 442376 | tf_op jit(solution)/shard_map/ppermute | solution.py:473
  8.5 2.1 %constant_dynamic-slice_fusion.1 = bf16[1024,1,128]{2,1,0:T(2,128)(2,1)S(1)} fusion(bf16[1024,8,128]{2,1,0:T(8,128)(2,1)} %param.11, s32[]{:T(128)S(6)} %select_n.11), kind=kLoop, calls=%fused_computation.3 | loop fusion | bytes 524292 | tf_op jit(solution)/shard_map/jit(dynamic_index_in_dim)/dynamic_slice | solution.py:330
  11.7 1.3 %collective-permute-start = (bf16[144,512]{1,0:T(8,128)(2,1)S(1)}, bf16[144,512]{1,0:T(8,128)(2,1)S(1)}, u32[]{:S(2)}, u32[]{:S(2)}) collective-permute-start(bf16[144,512]{1,0:T(8,128)(2,1)S(1)} %get-tuple-element.37), channel_id=1, source_target_pairs={{0,8},{1,9},{2,10},{3,11},{4,12},{5,13},{6,14},{7,15}} | collective-permute-start | bytes 442376 | tf_op jit(solution)/shard_map/ppermute | solution.py:473
  14.5 2.2 %collective-permute-start.3 = (bf16[144,512]{1,0:T(8,128)(2,1)S(1)}, bf16[144,512]{1,0:T(8,128)(2,1)S(1)}, u32[]{:S(2)}, u32[]{:S(2)}) collective-permute-start(bf16[144,512]{1,0:T(8,128)(2,1)S(1)} %get-tuple-element.46), channel_id=1, source_target_pairs={{8,24},{9,25},{10,26},{11,27},{12,28},{13,29},{14,30},{15,31}} | collective-permute-start | bytes 442376 | tf_op jit(solution)/shard_map/ppermute | solution.py:473
  16.7 1.3 %collective-permute-start.2 = (bf16[144,512]{1,0:T(8,128)(2,1)S(1)}, bf16[144,512]{1,0:T(8,128)(2,1)S(1)}, u32[]{:S(2)}, u32[]{:S(2)}) collective-permute-start(bf16[144,512]{1,0:T(8,128)(2,1)S(1)} %get-tuple-element.46), channel_id=1, source_target_pairs={{8,16},{16,24},{9,17},{17,25},{10,18},{18,26},{11,19},{19,27},{12,... | collective-permute-start | bytes 442376 | tf_op jit(solution)/shard_map/ppermute | solution.py:473
  19.0 1.4 %collective-permute-start.5 = (bf16[144,512]{1,0:T(8,128)(2,1)S(1)}, bf16[144,512]{1,0:T(8,128)(2,1)S(1)}, u32[]{:S(2)}, u32[]{:S(2)}) collective-permute-start(bf16[144,512]{1,0:T(8,128)(2,1)S(1)} %get-tuple-element.39.rest_0_), channel_id=1, source_target_pairs={{8,24},{9,25},{10,26},{11,27},{12,28},{13,29},{14,30},{15,31}} | collective-permute-start | bytes 442376 | tf_op jit(solution)/shard_map/ppermute | solution.py:473
  20.5 1.5 %collective-permute-start.4 = (bf16[144,512]{1,0:T(8,128)(2,1)S(1)}, bf16[144,512]{1,0:T(8,128)(2,1)S(1)}, u32[]{:S(2)}, u32[]{:S(2)}) collective-permute-start(bf16[144,512]{1,0:T(8,128)(2,1)S(1)} %get-tuple-element.39.rest_0_), channel_id=1, source_target_pairs={{8,16},{16,24},{9,17},{17,25},{10,18},{18,26},{11,19},{19,27},{12,... | collective-permute-start | bytes 442376 | tf_op jit(solution)/shard_map/ppermute | solution.py:473
  22.0 4.5 %local_mixer.2 = (f32[1024,512]{1,0:T(8,128)S(1)}, bf16[1024,256]{1,0:T(8,128)(2,1)S(1)}) custom-call(s32[64]{0:T(128)S(1)} %copy-done.8, f32[16,1024]{1,0:T(8,128)S(1)} %bitcast.23, f32[7,16,1024]{2,1,0:T(8,128)S(1)} %bitcast.26, bf16[1024,1024]{1,0:T(8,128)(2,1)S(1)} %copy-done.3, bf16[1024,128]{1,0:T(8,128)(2,1)S(1)} %bitcast.18, ...), custom_call_target="tpu_custom_call" | custom-call | flops 1073741824 | bytes 6291456 | tf_op jit(solution)/shard_map/local_mixer/pallas_call | solution.py:383
  26.5 1.5 %far_and_gate.2 = (bf16[128,512]{1,0:T(8,128)(2,1)S(1)}, bf16[128,512]{1,0:T(8,128)(2,1)S(1)}, bf16[128,512]{1,0:T(8,128)(2,1)S(1)}, bf16[128,512]{1,0:T(8,128)(...) custom-call(s32[1]{0:T(128)} %bitcast.me, ...), custom_call_target="tpu_custom_call" | custom-call | flops 268435456 | bytes 4194304 | tf_op jit(solution)/shard_map/far_and_gate/pallas_call | solution.py:416
  28.0 2.7 %collective-permute-start.8 = (bf16[128,512]{1,0:T(8,128)(2,1)S(1)}, bf16[128,512]{1,0:T(8,128)(2,1)S(1)}, u32[]{:S(2)}, u32[]{:S(2)}) collective-permute-start(bf16[128,512]{1,0:T(8,128)(2,1)S(1)} %get-tuple-element.55), channel_id=1, source_target_pairs={{0,3},{1,2},{2,1},{3,0},{4,7},{5,6},{6,5},{7,4},{8,11},{9,10},{10,... | collective-permute-start | bytes 393224 | tf_op jit(solution)/shard_map/ppermute | solution.py:511
  30.7 1.2 %collective-permute-start.10 = (bf16[128,512]{1,0:T(8,128)(2,1)S(1)}, bf16[128,512]{1,0:T(8,128)(2,1)S(1)}, u32[]{:S(2)}, u32[]{:S(2)}) collective-permute-start(bf16[128,512]{1,0:T(8,128)(2,1)S(1)} %get-tuple-element.57), channel_id=1, source_target_pairs={{0,4},{1,5},{2,6},{3,7},{4,0},{5,1},{6,2},{7,3},{8,12},{9,13},{10,... | collective-permute-start | bytes 393224 | tf_op jit(solution)/shard_map/ppermute | solution.py:511
  32.0 1.5 %collective-permute-start.14 = (bf16[128,512]{1,0:T(8,128)(2,1)S(1)}, bf16[128,512]{1,0:T(8,128)(2,1)S(1)}, u32[]{:S(2)}, u32[]{:S(2)}) collective-permute-start(bf16[128,512]{1,0:T(8,128)(2,1)S(1)} %get-tuple-element.61), channel_id=1, source_target_pairs={{0,6},{1,7},{2,4},{3,5},{4,2},{5,3},{6,0},{7,1},{8,14},{9,15},{10,... | collective-permute-start | bytes 393224 | tf_op jit(solution)/shard_map/ppermute | solution.py:511
  33.5 1.6 %collective-permute-start.16 = (bf16[128,512]{1,0:T(8,128)(2,1)S(1)}, bf16[128,512]{1,0:T(8,128)(2,1)S(1)}, u32[]{:S(2)}, u32[]{:S(2)}) collective-permute-start(bf16[128,512]{1,0:T(8,128)(2,1)S(1)} %get-tuple-element.63), channel_id=1, source_target_pairs={{0,7},{1,6},{2,5},{3,4},{4,3},{5,2},{6,1},{7,0},{8,15},{9,14},{10,... | collective-permute-start | bytes 393224 | tf_op jit(solution)/shard_map/ppermute | solution.py:511
  35.1 4.5 %local_mixer.3 = (f32[1024,512]{1,0:T(8,128)S(1)}, bf16[1024,256]{1,0:T(8,128)(2,1)S(1)}) custom-call(s32[64]{0:T(128)S(1)} %copy-done.8, f32[16,1024]{1,0:T(8,128)S(1)} %bitcast.24, f32[7,16,1024]{2,1,0:T(8,128)S(1)} %bitcast.27, bf16[1024,1024]{1,0:T(8,128)(2,1)S(1)} %copy-done.3, bf16[1024,128]{1,0:T(8,128)(2,1)S(1)} %bitcast.20, ...), custom_call_target="tpu_custom_call" | custom-call | flops 1073741824 | bytes 6291456 | tf_op jit(solution)/shard_map/local_mixer/pallas_call | solution.py:383
  39.7 1.5 %far_and_gate.3 = (bf16[128,512]{1,0:T(8,128)(2,1)S(1)}, bf16[128,1024]{1,0:T(8,128)(2,1)S(1)}, bf16[128,1024]{1,0:T(8,128)(2,1)S(1)}, bf16[128,512]{1,0:T(8,128...) custom-call(s32[1]{0:T(128)} %bitcast.me, ...), custom_call_target="tpu_custom_call" | custom-call | flops 268435456 | bytes 4194304 | tf_op jit(solution)/shard_map/far_and_gate/pallas_call | solution.py:416
  41.3 1.4 %collective-permute-start.11 = (bf16[128,512]{1,0:T(8,128)(2,1)S(1)}, bf16[128,512]{1,0:T(8,128)(2,1)S(1)}, u32[]{:S(2)}, u32[]{:S(2)}) collective-permute-start(bf16[128,512]{1,0:T(8,128)(2,1)S(1)} %get-tuple-element.58), channel_id=1, source_target_pairs={{0,4},{1,5},{2,6},{3,7},{4,0},{5,1},{6,2},{7,3},{8,12},{9,13},{10,... | collective-permute-start | bytes 393224 | tf_op jit(solution)/shard_map/ppermute | solution.py:511
  45.0 2.1 %collective-permute-start.13 = (bf16[128,512]{1,0:T(8,128)(2,1)S(1)}, bf16[128,512]{1,0:T(8,128)(2,1)S(1)}, u32[]{:S(2)}, u32[]{:S(2)}) collective-permute-start(bf16[128,512]{1,0:T(8,128)(2,1)S(1)} %get-tuple-element.60), channel_id=1, source_target_pairs={{0,5},{1,4},{2,7},{3,6},{4,1},{5,0},{6,3},{7,2},{8,13},{9,12},{10,... | collective-permute-start | bytes 393224 | tf_op jit(solution)/shard_map/ppermute | solution.py:511
  47.8 1.6 %collective-permute-start.17 = (bf16[128,512]{1,0:T(8,128)(2,1)S(1)}, bf16[128,512]{1,0:T(8,128)(2,1)S(1)}, u32[]{:S(2)}, u32[]{:S(2)}) collective-permute-start(bf16[128,512]{1,0:T(8,128)(2,1)S(1)} %get-tuple-element.64), channel_id=1, source_target_pairs={{0,7},{1,6},{2,5},{3,4},{4,3},{5,2},{6,1},{7,0},{8,15},{9,14},{10,... | collective-permute-start | bytes 393224 | tf_op jit(solution)/shard_map/ppermute | solution.py:511
  49.4 1.7 %collective-permute-done.13.rest_9_ = bf16[128,512]{1,0:T(8,128)(2,1)S(1)} collective-permute-done((bf16[128,512]{1,0:T(8,128)(2,1)S(1)}, bf16[128,512]{1,0:T(8,128)(2,1)S(1)}, u32[]{:S(2)}, u32[]{:S(2)}) %collective-permute-start.13) | collective-permute-done | bytes 131104 | tf_op jit(solution)/shard_map/ppermute | solution.py:511
  51.1 5.1 %collective-permute-done.15.rest_11_ = bf16[128,512]{1,0:T(8,128)(2,1)S(1)} collective-permute-done((bf16[128,512]{1,0:T(8,128)(2,1)S(1)}, bf16[128,512]{1,0:T(8,128)(2,1)S(1)}, u32[]{:S(2)}, u32[]{:S(2)}) %collective-permute-start.15) | collective-permute-done | bytes 131104 | tf_op jit(solution)/shard_map/ppermute | solution.py:511
  56.2 2.9 %collective-permute-done.17.rest_13_ = bf16[128,512]{1,0:T(8,128)(2,1)S(1)} collective-permute-done((bf16[128,512]{1,0:T(8,128)(2,1)S(1)}, bf16[128,512]{1,0:T(8,128)(2,1)S(1)}, u32[]{:S(2)}, u32[]{:S(2)}) %collective-permute-start.17) | collective-permute-done | bytes 131104 | tf_op jit(solution)/shard_map/ppermute | solution.py:511
  59.1 1.7 %norm_rows.1 = bf16[128,8192]{1,0:T(8,128)(2,1)} custom-call(s32[1]{0:T(128)} %bitcast.me, f32[1,8192]{1,0:T(1,128)S(1)} %bitcast.25, bf16[128,512]{1,0:T(8,128)(2,1)S(1)} %get-tuple-element.47.rest_0_, bf16[128,512]{1,0:T(8,128)(2,1)S(1)} %get-tuple-element.52.rest_1_, bf16[128,1024]{1,0:T(8,128)(2,1)S(1)} %collective-permute-done.6.rest_2_, ...), custom_call_target="tpu_custom_call" | custom-call | flops 8388608 | bytes 4194304 | tf_op jit(solution)/shard_map/norm_rows/pallas_call | solution.py:532
  (47 shorter events, 10.6 us)
Async XLA Ops:
  6.2 4.5 %copy-start.3 = (bf16[1024,1024]{1,0:T(8,128)(2,1)S(1)}, bf16[1024,1024]{1,0:T(8,128)(2,1)}, u32[]{:S(2)}) copy-start(bf16[1024,1024]{1,0:T(8,128)(2,1)} %values.7) | copy-start | bytes 6291460
  7.2 6.6 %collective-permute-start.1 = (bf16[144,512]{1,0:T(8,128)(2,1)S(1)}, bf16[144,512]{1,0:T(8,128)(2,1)S(1)}, u32[]{:S(2)}, u32[]{:S(2)}) collective-permute-start(bf16[144,512]{1,0:T(8,128)(2,1)S(1)} %get-tuple-element.44), channel_id=1, source_target_pairs={{0,8},{1,9},{2,10},{3,11},{4,12},{5,13},{6,14},{7,15}} | collective-permute-start | bytes 442376 | tf_op jit(solution)/shard_map/ppermute | solution.py:473
  10.6 11.3 %copy-start.5 = (f32[1024,16]{0,1:T(8,128)S(1)}, f32[1024,16]{0,1:T(8,128)}, u32[]{:S(2)}) copy-start(f32[1024,16]{0,1:T(8,128)} %param.12) | copy-start | bytes 196612
  10.7 11.3 %copy-start.8 = (s32[64]{0:T(128)S(1)}, s32[64]{0:T(128)}, u32[]{:S(2)}) copy-start(s32[64]{0:T(128)} %docs.5) | copy-start | bytes 772
  10.7 11.3 %copy-start.9 = (f32[1024,16,7]{0,1,2:T(8,128)S(1)}, f32[1024,16,7]{0,1,2:T(8,128)}, u32[]{:S(2)}) copy-start(f32[1024,16,7]{0,1,2:T(8,128)} %param.13) | copy-start | bytes 1376260
  11.7 6.6 %collective-permute-start = (bf16[144,512]{1,0:T(8,128)(2,1)S(1)}, bf16[144,512]{1,0:T(8,128)(2,1)S(1)}, u32[]{:S(2)}, u32[]{:S(2)}) collective-permute-start(bf16[144,512]{1,0:T(8,128)(2,1)S(1)} %get-tuple-element.37), channel_id=1, source_target_pairs={{0,8},{1,9},{2,10},{3,11},{4,12},{5,13},{6,14},{7,15}} | collective-permute-start | bytes 442376 | tf_op jit(solution)/shard_map/ppermute | solution.py:473
  14.5 12.0 %collective-permute-start.3 = (bf16[144,512]{1,0:T(8,128)(2,1)S(1)}, bf16[144,512]{1,0:T(8,128)(2,1)S(1)}, u32[]{:S(2)}, u32[]{:S(2)}) collective-permute-start(bf16[144,512]{1,0:T(8,128)(2,1)S(1)} %get-tuple-element.46), channel_id=1, source_target_pairs={{8,24},{9,25},{10,26},{11,27},{12,28},{13,29},{14,30},{15,31}} | collective-permute-start | bytes 442376 | tf_op jit(solution)/shard_map/ppermute | solution.py:473
  16.7 9.8 %collective-permute-start.2 = (bf16[144,512]{1,0:T(8,128)(2,1)S(1)}, bf16[144,512]{1,0:T(8,128)(2,1)S(1)}, u32[]{:S(2)}, u32[]{:S(2)}) collective-permute-start(bf16[144,512]{1,0:T(8,128)(2,1)S(1)} %get-tuple-element.46), channel_id=1, source_target_pairs={{8,16},{16,24},{9,17},{17,25},{10,18},{18,26},{11,19},{19,27},{12,... | collective-permute-start | bytes 442376 | tf_op jit(solution)/shard_map/ppermute | solution.py:473
  19.0 7.5 %copy-start.1 = (bf16[1024,1024]{1,0:T(8,128)(2,1)S(1)}, bf16[1024,1024]{1,0:T(8,128)(2,1)}, u32[]{:S(2)}) copy-start(bf16[1024,1024]{1,0:T(8,128)(2,1)} %refs_3_.3) | copy-start | bytes 6291460
  19.0 12.9 %collective-permute-start.5 = (bf16[144,512]{1,0:T(8,128)(2,1)S(1)}, bf16[144,512]{1,0:T(8,128)(2,1)S(1)}, u32[]{:S(2)}, u32[]{:S(2)}) collective-permute-start(bf16[144,512]{1,0:T(8,128)(2,1)S(1)} %get-tuple-element.39.rest_0_), channel_id=1, source_target_pairs={{8,24},{9,25},{10,26},{11,27},{12,28},{13,29},{14,30},{15,31}} | collective-permute-start | bytes 442376 | tf_op jit(solution)/shard_map/ppermute | solution.py:473
  20.5 13.0 %collective-permute-start.4 = (bf16[144,512]{1,0:T(8,128)(2,1)S(1)}, bf16[144,512]{1,0:T(8,128)(2,1)S(1)}, u32[]{:S(2)}, u32[]{:S(2)}) collective-permute-start(bf16[144,512]{1,0:T(8,128)(2,1)S(1)} %get-tuple-element.39.rest_0_), channel_id=1, source_target_pairs={{8,16},{16,24},{9,17},{17,25},{10,18},{18,26},{11,19},{19,27},{12,... | collective-permute-start | bytes 442376 | tf_op jit(solution)/shard_map/ppermute | solution.py:473
  28.0 13.1 %collective-permute-start.8 = (bf16[128,512]{1,0:T(8,128)(2,1)S(1)}, bf16[128,512]{1,0:T(8,128)(2,1)S(1)}, u32[]{:S(2)}, u32[]{:S(2)}) collective-permute-start(bf16[128,512]{1,0:T(8,128)(2,1)S(1)} %get-tuple-element.55), channel_id=1, source_target_pairs={{0,3},{1,2},{2,1},{3,0},{4,7},{5,6},{6,5},{7,4},{8,11},{9,10},{10,... | collective-permute-start | bytes 393224 | tf_op jit(solution)/shard_map/ppermute | solution.py:511
  30.7 10.6 %collective-permute-start.10 = (bf16[128,512]{1,0:T(8,128)(2,1)S(1)}, bf16[128,512]{1,0:T(8,128)(2,1)S(1)}, u32[]{:S(2)}, u32[]{:S(2)}) collective-permute-start(bf16[128,512]{1,0:T(8,128)(2,1)S(1)} %get-tuple-element.57), channel_id=1, source_target_pairs={{0,4},{1,5},{2,6},{3,7},{4,0},{5,1},{6,2},{7,3},{8,12},{9,13},{10,... | collective-permute-start | bytes 393224 | tf_op jit(solution)/shard_map/ppermute | solution.py:511
  32.0 11.8 %collective-permute-start.12 = (bf16[128,512]{1,0:T(8,128)(2,1)S(1)}, bf16[128,512]{1,0:T(8,128)(2,1)S(1)}, u32[]{:S(2)}, u32[]{:S(2)}) collective-permute-start(bf16[128,512]{1,0:T(8,128)(2,1)S(1)} %get-tuple-element.59), channel_id=1, source_target_pairs={{0,5},{1,4},{2,7},{3,6},{4,1},{5,0},{6,3},{7,2},{8,13},{9,12},{10,... | collective-permute-start | bytes 393224 | tf_op jit(solution)/shard_map/ppermute | solution.py:511
  32.0 12.5 %collective-permute-start.14 = (bf16[128,512]{1,0:T(8,128)(2,1)S(1)}, bf16[128,512]{1,0:T(8,128)(2,1)S(1)}, u32[]{:S(2)}, u32[]{:S(2)}) collective-permute-start(bf16[128,512]{1,0:T(8,128)(2,1)S(1)} %get-tuple-element.61), channel_id=1, source_target_pairs={{0,6},{1,7},{2,4},{3,5},{4,2},{5,3},{6,0},{7,1},{8,14},{9,15},{10,... | collective-permute-start | bytes 393224 | tf_op jit(solution)/shard_map/ppermute | solution.py:511
  33.5 11.5 %collective-permute-start.16 = (bf16[128,512]{1,0:T(8,128)(2,1)S(1)}, bf16[128,512]{1,0:T(8,128)(2,1)S(1)}, u32[]{:S(2)}, u32[]{:S(2)}) collective-permute-start(bf16[128,512]{1,0:T(8,128)(2,1)S(1)} %get-tuple-element.63), channel_id=1, source_target_pairs={{0,7},{1,6},{2,5},{3,4},{4,3},{5,2},{6,1},{7,0},{8,15},{9,14},{10,... | collective-permute-start | bytes 393224 | tf_op jit(solution)/shard_map/ppermute | solution.py:511
  39.7 19.5 %copy-start.6 = (f32[8192]{0:T(1024)S(1)}, f32[8192]{0:T(1024)}, u32[]{:S(2)}) copy-start(f32[8192]{0:T(1024)} %param.15) | copy-start | bytes 98308
  41.2 6.0 %collective-permute-start.9 = (bf16[128,512]{1,0:T(8,128)(2,1)S(1)}, bf16[128,512]{1,0:T(8,128)(2,1)S(1)}, u32[]{:S(2)}, u32[]{:S(2)}) collective-permute-start(bf16[128,512]{1,0:T(8,128)(2,1)S(1)} %get-tuple-element.56), channel_id=1, source_target_pairs={{0,3},{1,2},{2,1},{3,0},{4,7},{5,6},{6,5},{7,4},{8,11},{9,10},{10,... | collective-permute-start | bytes 393224 | tf_op jit(solution)/shard_map/ppermute | solution.py:511
  41.3 6.4 %collective-permute-start.11 = (bf16[128,512]{1,0:T(8,128)(2,1)S(1)}, bf16[128,512]{1,0:T(8,128)(2,1)S(1)}, u32[]{:S(2)}, u32[]{:S(2)}) collective-permute-start(bf16[128,512]{1,0:T(8,128)(2,1)S(1)} %get-tuple-element.58), channel_id=1, source_target_pairs={{0,4},{1,5},{2,6},{3,7},{4,0},{5,1},{6,2},{7,3},{8,12},{9,13},{10,... | collective-permute-start | bytes 393224 | tf_op jit(solution)/shard_map/ppermute | solution.py:511
  43.7 15.4 %collective-permute-start.6 = (bf16[128,1024]{1,0:T(8,128)(2,1)S(1)}, bf16[128,1024]{1,0:T(8,128)(2,1)S(1)}, u32[]{:S(2)}, u32[]{:S(2)}) collective-permute-start(bf16[128,1024]{1,0:T(8,128)(2,1)S(1)} %get-tuple-element.53), channel_id=1, source_target_pairs={{0,1},{1,0},{2,3},{3,2},{4,5},{5,4},{6,7},{7,6},{8,9},{9,8},{10,11... | collective-permute-start | bytes 786440 | tf_op jit(solution)/shard_map/ppermute | solution.py:511
  44.5 14.6 %collective-permute-start.7 = (bf16[128,1024]{1,0:T(8,128)(2,1)S(1)}, bf16[128,1024]{1,0:T(8,128)(2,1)S(1)}, u32[]{:S(2)}, u32[]{:S(2)}) collective-permute-start(bf16[128,1024]{1,0:T(8,128)(2,1)S(1)} %get-tuple-element.54), channel_id=1, source_target_pairs={{0,2},{1,3},{2,0},{3,1},{4,6},{5,7},{6,4},{7,5},{8,10},{9,11},{10,... | collective-permute-start | bytes 786440 | tf_op jit(solution)/shard_map/ppermute | solution.py:511
  45.0 6.1 %collective-permute-start.13 = (bf16[128,512]{1,0:T(8,128)(2,1)S(1)}, bf16[128,512]{1,0:T(8,128)(2,1)S(1)}, u32[]{:S(2)}, u32[]{:S(2)}) collective-permute-start(bf16[128,512]{1,0:T(8,128)(2,1)S(1)} %get-tuple-element.60), channel_id=1, source_target_pairs={{0,5},{1,4},{2,7},{3,6},{4,1},{5,0},{6,3},{7,2},{8,13},{9,12},{10,... | collective-permute-start | bytes 393224 | tf_op jit(solution)/shard_map/ppermute | solution.py:511
  47.2 9.1 %collective-permute-start.15 = (bf16[128,512]{1,0:T(8,128)(2,1)S(1)}, bf16[128,512]{1,0:T(8,128)(2,1)S(1)}, u32[]{:S(2)}, u32[]{:S(2)}) collective-permute-start(bf16[128,512]{1,0:T(8,128)(2,1)S(1)} %get-tuple-element.62), channel_id=1, source_target_pairs={{0,6},{1,7},{2,4},{3,5},{4,2},{5,3},{6,0},{7,1},{8,14},{9,15},{10,... | collective-permute-start | bytes 393224 | tf_op jit(solution)/shard_map/ppermute | solution.py:511
  47.8 11.3 %collective-permute-start.17 = (bf16[128,512]{1,0:T(8,128)(2,1)S(1)}, bf16[128,512]{1,0:T(8,128)(2,1)S(1)}, u32[]{:S(2)}, u32[]{:S(2)}) collective-permute-start(bf16[128,512]{1,0:T(8,128)(2,1)S(1)} %get-tuple-element.64), channel_id=1, source_target_pairs={{0,7},{1,6},{2,5},{3,4},{4,3},{5,2},{6,1},{7,0},{8,15},{9,14},{10,... | collective-permute-start | bytes 393224 | tf_op jit(solution)/shard_map/ppermute | solution.py:511
  (4 other events, 4.7 us)

commit v5 on v4

--- a/solution.py
+++ b/solution.py
@@ -326,8 +326,6 @@
     head_count = lax.axis_size("head")
     head_index = lax.axis_index("head")
     group_index = head_index * heads_here // (MIXER_HEADS // GROUPS)
-    key_rows = lax.dynamic_index_in_dim(b_keys, group_index, 1, keepdims=False)
-    query_rows = lax.dynamic_index_in_dim(c_queries, group_index, 1, keepdims=False)
     decay = jnp.transpose(log_decay)
     weight = jnp.transpose(level_weight, (2, 1, 0))
     heads = SUBLANES
@@ -359,6 +357,10 @@
         ),
         name="token_decays",
     )(doc_start, decay)
+
+    group_index, _ = lax.optimization_barrier((group_index, decays[1]))
+    key_rows = lax.dynamic_index_in_dim(b_keys, group_index, 1, keepdims=False)
+    query_rows = lax.dynamic_index_in_dim(c_queries, group_index, 1, keepdims=False)
 
     def state_call(c):
         terms, through = decays[2 * c : 2 * c + 2]

time: 61.3 us -> 59.8 us (0.976)
  local copies, waits for them, and re-layouts: 7.46 us -> 6.03 us
    unnamed x22, local copies, waits for them, and re-layouts: 4.77 us -> 3.34 us
where the time goes in v5:
time: 59.8 us; the launch traced here: 59.5 us
  starting transfers between devices  23.3 us (39%)
  Pallas kernels  18 us (30%)
  waiting for transfers between devices  11.8 us (20%)
  local copies, waits for them, and re-layouts  6.03 us (10%)
    ppermute x12, starting transfers between devices, body(): got[apart] = lax.ppermute(out[apart], 'head', pairs)  14.3 us
    ppermute x12, waiting for transfers between devices, body(): got[apart] = lax.ppermute(out[apart], 'head', pairs)  10.7 us
    pallas_call x2, Pallas kernels, local_call(): pl.pallas_call(functools.partial(local_kernel, head_dim, heads, c, far),...  9.01 us
    ppermute x6, starting transfers between devices, post(): lax.ppermute(self.moving, 'seq', p)  8.99 us
    unnamed x22, local copies, waits for them, and re-layouts  3.34 us
    pallas_call x2, Pallas kernels, gate_call(): pl.pallas_call(functools.partial(gate_kernel, head_dim, heads, (near + 3)...  2.98 us
    dynamic_slice x1, local copies, waits for them, and re-layouts, body(): lax.dynamic_index_in_dim(c_queries, group_index, 1, keepdims=False)  2.14 us
    pallas_call x2, Pallas kernels, state_call(): pl.pallas_call(functools.partial(state_kernel, head_dim, heads, c * part,...  1.96 us
  transfers between devices with their start and end apart: 18, of which 6 were waited for; matrix products, arithmetic and copies ran while one was open for 4% of the time, Pallas kernels for 24%

profile of v5, /device:TPU:9, one launch (start us, length us, event | category | flops | bytes accessed | tf_op | source)
XLA Modules:
  0.0 59.5 jit_solution(6899489033833584349)
XLA Ops:
  3.2 1.6 %copy-done.2 = bf16[1024,1024]{1,0:T(8,128)(2,1)S(1)} copy-done((bf16[1024,1024]{1,0:T(8,128)(2,1)S(1)}, bf16[1024,1024]{1,0:T(8,128)(2,1)}, u32[]{:S(2)}) %copy-start.2) | copy-done | bytes 2097176
  5.7 1.3 %collective-permute-start.1 = (bf16[144,512]{1,0:T(8,128)(2,1)S(1)}, bf16[144,512]{1,0:T(8,128)(2,1)S(1)}, u32[]{:S(2)}, u32[]{:S(2)}) collective-permute-start(bf16[144,512]{1,0:T(8,128)(2,1)S(1)} %get-tuple-element.46), channel_id=1, source_target_pairs={{0,8},{1,9},{2,10},{3,11},{4,12},{5,13},{6,14},{7,15}} | collective-permute-start | bytes 442376 | tf_op jit(solution)/shard_map/ppermute | solution.py:475
  7.0 2.1 %constant_dynamic-slice_fusion.1 = bf16[1024,1,128]{2,1,0:T(2,128)(2,1)S(1)} fusion(bf16[1024,8,128]{2,1,0:T(8,128)(2,1)} %param.11, s32[]{:T(128)S(6)} %select_n.11), kind=kLoop, calls=%fused_computation.3 | loop fusion | bytes 524292 | tf_op jit(solution)/shard_map/jit(dynamic_index_in_dim)/dynamic_slice | solution.py:363
  10.3 1.3 %collective-permute-start = (bf16[144,512]{1,0:T(8,128)(2,1)S(1)}, bf16[144,512]{1,0:T(8,128)(2,1)S(1)}, u32[]{:S(2)}, u32[]{:S(2)}) collective-permute-start(bf16[144,512]{1,0:T(8,128)(2,1)S(1)} %get-tuple-element.40), channel_id=1, source_target_pairs={{0,8},{1,9},{2,10},{3,11},{4,12},{5,13},{6,14},{7,15}} | collective-permute-start | bytes 442376 | tf_op jit(solution)/shard_map/ppermute | solution.py:475
  13.1 2.2 %collective-permute-start.3 = (bf16[144,512]{1,0:T(8,128)(2,1)S(1)}, bf16[144,512]{1,0:T(8,128)(2,1)S(1)}, u32[]{:S(2)}, u32[]{:S(2)}) collective-permute-start(bf16[144,512]{1,0:T(8,128)(2,1)S(1)} %get-tuple-element.48), channel_id=1, source_target_pairs={{8,24},{9,25},{10,26},{11,27},{12,28},{13,29},{14,30},{15,31}} | collective-permute-start | bytes 442376 | tf_op jit(solution)/shard_map/ppermute | solution.py:475
  15.3 1.3 %collective-permute-start.2 = (bf16[144,512]{1,0:T(8,128)(2,1)S(1)}, bf16[144,512]{1,0:T(8,128)(2,1)S(1)}, u32[]{:S(2)}, u32[]{:S(2)}) collective-permute-start(bf16[144,512]{1,0:T(8,128)(2,1)S(1)} %get-tuple-element.48), channel_id=1, source_target_pairs={{8,16},{16,24},{9,17},{17,25},{10,18},{18,26},{11,19},{19,27},{12,... | collective-permute-start | bytes 442376 | tf_op jit(solution)/shard_map/ppermute | solution.py:475
  17.6 1.4 %collective-permute-start.5 = (bf16[144,512]{1,0:T(8,128)(2,1)S(1)}, bf16[144,512]{1,0:T(8,128)(2,1)S(1)}, u32[]{:S(2)}, u32[]{:S(2)}) collective-permute-start(bf16[144,512]{1,0:T(8,128)(2,1)S(1)} %get-tuple-element.42.rest_0_), channel_id=1, source_target_pairs={{8,24},{9,25},{10,26},{11,27},{12,28},{13,29},{14,30},{15,31}} | collective-permute-start | bytes 442376 | tf_op jit(solution)/shard_map/ppermute | solution.py:475
  19.1 1.5 %collective-permute-start.4 = (bf16[144,512]{1,0:T(8,128)(2,1)S(1)}, bf16[144,512]{1,0:T(8,128)(2,1)S(1)}, u32[]{:S(2)}, u32[]{:S(2)}) collective-permute-start(bf16[144,512]{1,0:T(8,128)(2,1)S(1)} %get-tuple-element.42.rest_0_), channel_id=1, source_target_pairs={{8,16},{16,24},{9,17},{17,25},{10,18},{18,26},{11,19},{19,27},{12,... | collective-permute-start | bytes 442376 | tf_op jit(solution)/shard_map/ppermute | solution.py:475
  20.6 4.5 %local_mixer.2 = (f32[1024,512]{1,0:T(8,128)S(1)}, bf16[1024,256]{1,0:T(8,128)(2,1)S(1)}) custom-call(s32[64]{0:T(128)S(1)} %copy-done.8, f32[16,1024]{1,0:T(8,128)S(1)} %bitcast.23, f32[7,16,1024]{2,1,0:T(8,128)S(1)} %bitcast.26, bf16[1024,1024]{1,0:T(8,128)(2,1)S(1)} %copy-done.3, bf16[1024,128]{1,0:T(8,128)(2,1)S(1)} %bitcast.18, ...), custom_call_target="tpu_custom_call" | custom-call | flops 1073741824 | bytes 6291456 | tf_op jit(solution)/shard_map/local_mixer/pallas_call | solution.py:385
  25.1 1.5 %far_and_gate.2 = (bf16[128,512]{1,0:T(8,128)(2,1)S(1)}, bf16[128,512]{1,0:T(8,128)(2,1)S(1)}, bf16[128,512]{1,0:T(8,128)(2,1)S(1)}, bf16[128,512]{1,0:T(8,128)(...) custom-call(s32[1]{0:T(128)} %bitcast.me, ...), custom_call_target="tpu_custom_call" | custom-call | flops 268435456 | bytes 4194304 | tf_op jit(solution)/shard_map/far_and_gate/pallas_call | solution.py:418
  26.6 2.7 %collective-permute-start.8 = (bf16[128,512]{1,0:T(8,128)(2,1)S(1)}, bf16[128,512]{1,0:T(8,128)(2,1)S(1)}, u32[]{:S(2)}, u32[]{:S(2)}) collective-permute-start(bf16[128,512]{1,0:T(8,128)(2,1)S(1)} %get-tuple-element.57), channel_id=1, source_target_pairs={{0,3},{1,2},{2,1},{3,0},{4,7},{5,6},{6,5},{7,4},{8,11},{9,10},{10,... | collective-permute-start | bytes 393224 | tf_op jit(solution)/shard_map/ppermute | solution.py:513
  29.3 1.2 %collective-permute-start.10 = (bf16[128,512]{1,0:T(8,128)(2,1)S(1)}, bf16[128,512]{1,0:T(8,128)(2,1)S(1)}, u32[]{:S(2)}, u32[]{:S(2)}) collective-permute-start(bf16[128,512]{1,0:T(8,128)(2,1)S(1)} %get-tuple-element.59), channel_id=1, source_target_pairs={{0,4},{1,5},{2,6},{3,7},{4,0},{5,1},{6,2},{7,3},{8,12},{9,13},{10,... | collective-permute-start | bytes 393224 | tf_op jit(solution)/shard_map/ppermute | solution.py:513
  30.6 1.5 %collective-permute-start.14 = (bf16[128,512]{1,0:T(8,128)(2,1)S(1)}, bf16[128,512]{1,0:T(8,128)(2,1)S(1)}, u32[]{:S(2)}, u32[]{:S(2)}) collective-permute-start(bf16[128,512]{1,0:T(8,128)(2,1)S(1)} %get-tuple-element.63), channel_id=1, source_target_pairs={{0,6},{1,7},{2,4},{3,5},{4,2},{5,3},{6,0},{7,1},{8,14},{9,15},{10,... | collective-permute-start | bytes 393224 | tf_op jit(solution)/shard_map/ppermute | solution.py:513
  32.1 1.6 %collective-permute-start.16 = (bf16[128,512]{1,0:T(8,128)(2,1)S(1)}, bf16[128,512]{1,0:T(8,128)(2,1)S(1)}, u32[]{:S(2)}, u32[]{:S(2)}) collective-permute-start(bf16[128,512]{1,0:T(8,128)(2,1)S(1)} %get-tuple-element.65), channel_id=1, source_target_pairs={{0,7},{1,6},{2,5},{3,4},{4,3},{5,2},{6,1},{7,0},{8,15},{9,14},{10,... | collective-permute-start | bytes 393224 | tf_op jit(solution)/shard_map/ppermute | solution.py:513
  33.7 4.5 %local_mixer.3 = (f32[1024,512]{1,0:T(8,128)S(1)}, bf16[1024,256]{1,0:T(8,128)(2,1)S(1)}) custom-call(s32[64]{0:T(128)S(1)} %copy-done.8, f32[16,1024]{1,0:T(8,128)S(1)} %bitcast.24, f32[7,16,1024]{2,1,0:T(8,128)S(1)} %bitcast.27, bf16[1024,1024]{1,0:T(8,128)(2,1)S(1)} %copy-done.3, bf16[1024,128]{1,0:T(8,128)(2,1)S(1)} %bitcast.20, ...), custom_call_target="tpu_custom_call" | custom-call | flops 1073741824 | bytes 6291456 | tf_op jit(solution)/shard_map/local_mixer/pallas_call | solution.py:385
  38.2 1.5 %far_and_gate.3 = (bf16[128,512]{1,0:T(8,128)(2,1)S(1)}, bf16[128,1024]{1,0:T(8,128)(2,1)S(1)}, bf16[128,1024]{1,0:T(8,128)(2,1)S(1)}, bf16[128,512]{1,0:T(8,128...) custom-call(s32[1]{0:T(128)} %bitcast.me, ...), custom_call_target="tpu_custom_call" | custom-call | flops 268435456 | bytes 4194304 | tf_op jit(solution)/shard_map/far_and_gate/pallas_call | solution.py:418
  39.9 1.4 %collective-permute-start.11 = (bf16[128,512]{1,0:T(8,128)(2,1)S(1)}, bf16[128,512]{1,0:T(8,128)(2,1)S(1)}, u32[]{:S(2)}, u32[]{:S(2)}) collective-permute-start(bf16[128,512]{1,0:T(8,128)(2,1)S(1)} %get-tuple-element.60), channel_id=1, source_target_pairs={{0,4},{1,5},{2,6},{3,7},{4,0},{5,1},{6,2},{7,3},{8,12},{9,13},{10,... | collective-permute-start | bytes 393224 | tf_op jit(solution)/shard_map/ppermute | solution.py:513
  41.3 1.0 %collective-permute-done.12.rest_8_ = bf16[128,512]{1,0:T(8,128)(2,1)S(1)} collective-permute-done((bf16[128,512]{1,0:T(8,128)(2,1)S(1)}, bf16[128,512]{1,0:T(8,128)(2,1)S(1)}, u32[]{:S(2)}, u32[]{:S(2)}) %collective-permute-start.12) | collective-permute-done | bytes 131104 | tf_op jit(solution)/shard_map/ppermute | solution.py:513
  43.6 2.1 %collective-permute-start.13 = (bf16[128,512]{1,0:T(8,128)(2,1)S(1)}, bf16[128,512]{1,0:T(8,128)(2,1)S(1)}, u32[]{:S(2)}, u32[]{:S(2)}) collective-permute-start(bf16[128,512]{1,0:T(8,128)(2,1)S(1)} %get-tuple-element.62), channel_id=1, source_target_pairs={{0,5},{1,4},{2,7},{3,6},{4,1},{5,0},{6,3},{7,2},{8,13},{9,12},{10,... | collective-permute-start | bytes 393224 | tf_op jit(solution)/shard_map/ppermute | solution.py:513
  46.4 1.6 %collective-permute-start.17 = (bf16[128,512]{1,0:T(8,128)(2,1)S(1)}, bf16[128,512]{1,0:T(8,128)(2,1)S(1)}, u32[]{:S(2)}, u32[]{:S(2)}) collective-permute-start(bf16[128,512]{1,0:T(8,128)(2,1)S(1)} %get-tuple-element.66), channel_id=1, source_target_pairs={{0,7},{1,6},{2,5},{3,4},{4,3},{5,2},{6,1},{7,0},{8,15},{9,14},{10,... | collective-permute-start | bytes 393224 | tf_op jit(solution)/shard_map/ppermute | solution.py:513
  48.0 1.7 %collective-permute-done.13.rest_9_ = bf16[128,512]{1,0:T(8,128)(2,1)S(1)} collective-permute-done((bf16[128,512]{1,0:T(8,128)(2,1)S(1)}, bf16[128,512]{1,0:T(8,128)(2,1)S(1)}, u32[]{:S(2)}, u32[]{:S(2)}) %collective-permute-start.13) | collective-permute-done | bytes 131104 | tf_op jit(solution)/shard_map/ppermute | solution.py:513
  49.7 5.1 %collective-permute-done.15.rest_11_ = bf16[128,512]{1,0:T(8,128)(2,1)S(1)} collective-permute-done((bf16[128,512]{1,0:T(8,128)(2,1)S(1)}, bf16[128,512]{1,0:T(8,128)(2,1)S(1)}, u32[]{:S(2)}, u32[]{:S(2)}) %collective-permute-start.15) | collective-permute-done | bytes 131104 | tf_op jit(solution)/shard_map/ppermute | solution.py:513
  54.8 2.9 %collective-permute-done.17.rest_13_ = bf16[128,512]{1,0:T(8,128)(2,1)S(1)} collective-permute-done((bf16[128,512]{1,0:T(8,128)(2,1)S(1)}, bf16[128,512]{1,0:T(8,128)(2,1)S(1)}, u32[]{:S(2)}, u32[]{:S(2)}) %collective-permute-start.17) | collective-permute-done | bytes 131104 | tf_op jit(solution)/shard_map/ppermute | solution.py:513
  57.7 1.7 %norm_rows.1 = bf16[128,8192]{1,0:T(8,128)(2,1)} custom-call(s32[1]{0:T(128)} %bitcast.me, f32[1,8192]{1,0:T(1,128)S(1)} %bitcast.25, bf16[128,512]{1,0:T(8,128)(2,1)S(1)} %get-tuple-element.49.rest_0_, bf16[128,512]{1,0:T(8,128)(2,1)S(1)} %get-tuple-element.54.rest_1_, bf16[128,1024]{1,0:T(8,128)(2,1)S(1)} %collective-permute-done.6.rest_2_, ...), custom_call_target="tpu_custom_call" | custom-call | flops 8388608 | bytes 4194304 | tf_op jit(solution)/shard_map/norm_rows/pallas_call | solution.py:534
  (47 shorter events, 9.8 us)
Async XLA Ops:
  4.7 4.5 %copy-start.3 = (bf16[1024,1024]{1,0:T(8,128)(2,1)S(1)}, bf16[1024,1024]{1,0:T(8,128)(2,1)}, u32[]{:S(2)}) copy-start(bf16[1024,1024]{1,0:T(8,128)(2,1)} %values.7) | copy-start | bytes 6291460
  5.7 6.6 %collective-permute-start.1 = (bf16[144,512]{1,0:T(8,128)(2,1)S(1)}, bf16[144,512]{1,0:T(8,128)(2,1)S(1)}, u32[]{:S(2)}, u32[]{:S(2)}) collective-permute-start(bf16[144,512]{1,0:T(8,128)(2,1)S(1)} %get-tuple-element.46), channel_id=1, source_target_pairs={{0,8},{1,9},{2,10},{3,11},{4,12},{5,13},{6,14},{7,15}} | collective-permute-start | bytes 442376 | tf_op jit(solution)/shard_map/ppermute | solution.py:475
  9.2 11.3 %copy-start.5 = (f32[1024,16]{0,1:T(8,128)S(1)}, f32[1024,16]{0,1:T(8,128)}, u32[]{:S(2)}) copy-start(f32[1024,16]{0,1:T(8,128)} %param.12) | copy-start | bytes 196612
  9.2 11.3 %copy-start.8 = (s32[64]{0:T(128)S(1)}, s32[64]{0:T(128)}, u32[]{:S(2)}) copy-start(s32[64]{0:T(128)} %docs.5) | copy-start | bytes 772
  9.2 11.3 %copy-start.9 = (f32[1024,16,7]{0,1,2:T(8,128)S(1)}, f32[1024,16,7]{0,1,2:T(8,128)}, u32[]{:S(2)}) copy-start(f32[1024,16,7]{0,1,2:T(8,128)} %param.13) | copy-start | bytes 1376260
  10.3 6.6 %collective-permute-start = (bf16[144,512]{1,0:T(8,128)(2,1)S(1)}, bf16[144,512]{1,0:T(8,128)(2,1)S(1)}, u32[]{:S(2)}, u32[]{:S(2)}) collective-permute-start(bf16[144,512]{1,0:T(8,128)(2,1)S(1)} %get-tuple-element.40), channel_id=1, source_target_pairs={{0,8},{1,9},{2,10},{3,11},{4,12},{5,13},{6,14},{7,15}} | collective-permute-start | bytes 442376 | tf_op jit(solution)/shard_map/ppermute | solution.py:475
  13.1 12.0 %collective-permute-start.3 = (bf16[144,512]{1,0:T(8,128)(2,1)S(1)}, bf16[144,512]{1,0:T(8,128)(2,1)S(1)}, u32[]{:S(2)}, u32[]{:S(2)}) collective-permute-start(bf16[144,512]{1,0:T(8,128)(2,1)S(1)} %get-tuple-element.48), channel_id=1, source_target_pairs={{8,24},{9,25},{10,26},{11,27},{12,28},{13,29},{14,30},{15,31}} | collective-permute-start | bytes 442376 | tf_op jit(solution)/shard_map/ppermute | solution.py:475
  15.3 9.8 %collective-permute-start.2 = (bf16[144,512]{1,0:T(8,128)(2,1)S(1)}, bf16[144,512]{1,0:T(8,128)(2,1)S(1)}, u32[]{:S(2)}, u32[]{:S(2)}) collective-permute-start(bf16[144,512]{1,0:T(8,128)(2,1)S(1)} %get-tuple-element.48), channel_id=1, source_target_pairs={{8,16},{16,24},{9,17},{17,25},{10,18},{18,26},{11,19},{19,27},{12,... | collective-permute-start | bytes 442376 | tf_op jit(solution)/shard_map/ppermute | solution.py:475
  17.6 7.5 %copy-start.1 = (bf16[1024,1024]{1,0:T(8,128)(2,1)S(1)}, bf16[1024,1024]{1,0:T(8,128)(2,1)}, u32[]{:S(2)}) copy-start(bf16[1024,1024]{1,0:T(8,128)(2,1)} %refs_3_.3) | copy-start | bytes 6291460
  17.6 12.9 %collective-permute-start.5 = (bf16[144,512]{1,0:T(8,128)(2,1)S(1)}, bf16[144,512]{1,0:T(8,128)(2,1)S(1)}, u32[]{:S(2)}, u32[]{:S(2)}) collective-permute-start(bf16[144,512]{1,0:T(8,128)(2,1)S(1)} %get-tuple-element.42.rest_0_), channel_id=1, source_target_pairs={{8,24},{9,25},{10,26},{11,27},{12,28},{13,29},{14,30},{15,31}} | collective-permute-start | bytes 442376 | tf_op jit(solution)/shard_map/ppermute | solution.py:475
  19.1 13.0 %collective-permute-start.4 = (bf16[144,512]{1,0:T(8,128)(2,1)S(1)}, bf16[144,512]{1,0:T(8,128)(2,1)S(1)}, u32[]{:S(2)}, u32[]{:S(2)}) collective-permute-start(bf16[144,512]{1,0:T(8,128)(2,1)S(1)} %get-tuple-element.42.rest_0_), channel_id=1, source_target_pairs={{8,16},{16,24},{9,17},{17,25},{10,18},{18,26},{11,19},{19,27},{12,... | collective-permute-start | bytes 442376 | tf_op jit(solution)/shard_map/ppermute | solution.py:475
  26.6 13.1 %collective-permute-start.8 = (bf16[128,512]{1,0:T(8,128)(2,1)S(1)}, bf16[128,512]{1,0:T(8,128)(2,1)S(1)}, u32[]{:S(2)}, u32[]{:S(2)}) collective-permute-start(bf16[128,512]{1,0:T(8,128)(2,1)S(1)} %get-tuple-element.57), channel_id=1, source_target_pairs={{0,3},{1,2},{2,1},{3,0},{4,7},{5,6},{6,5},{7,4},{8,11},{9,10},{10,... | collective-permute-start | bytes 393224 | tf_op jit(solution)/shard_map/ppermute | solution.py:513
  29.3 10.6 %collective-permute-start.10 = (bf16[128,512]{1,0:T(8,128)(2,1)S(1)}, bf16[128,512]{1,0:T(8,128)(2,1)S(1)}, u32[]{:S(2)}, u32[]{:S(2)}) collective-permute-start(bf16[128,512]{1,0:T(8,128)(2,1)S(1)} %get-tuple-element.59), channel_id=1, source_target_pairs={{0,4},{1,5},{2,6},{3,7},{4,0},{5,1},{6,2},{7,3},{8,12},{9,13},{10,... | collective-permute-start | bytes 393224 | tf_op jit(solution)/shard_map/ppermute | solution.py:513
  30.5 11.8 %collective-permute-start.12 = (bf16[128,512]{1,0:T(8,128)(2,1)S(1)}, bf16[128,512]{1,0:T(8,128)(2,1)S(1)}, u32[]{:S(2)}, u32[]{:S(2)}) collective-permute-start(bf16[128,512]{1,0:T(8,128)(2,1)S(1)} %get-tuple-element.61), channel_id=1, source_target_pairs={{0,5},{1,4},{2,7},{3,6},{4,1},{5,0},{6,3},{7,2},{8,13},{9,12},{10,... | collective-permute-start | bytes 393224 | tf_op jit(solution)/shard_map/ppermute | solution.py:513
  30.6 12.5 %collective-permute-start.14 = (bf16[128,512]{1,0:T(8,128)(2,1)S(1)}, bf16[128,512]{1,0:T(8,128)(2,1)S(1)}, u32[]{:S(2)}, u32[]{:S(2)}) collective-permute-start(bf16[128,512]{1,0:T(8,128)(2,1)S(1)} %get-tuple-element.63), channel_id=1, source_target_pairs={{0,6},{1,7},{2,4},{3,5},{4,2},{5,3},{6,0},{7,1},{8,14},{9,15},{10,... | collective-permute-start | bytes 393224 | tf_op jit(solution)/shard_map/ppermute | solution.py:513
  32.1 11.5 %collective-permute-start.16 = (bf16[128,512]{1,0:T(8,128)(2,1)S(1)}, bf16[128,512]{1,0:T(8,128)(2,1)S(1)}, u32[]{:S(2)}, u32[]{:S(2)}) collective-permute-start(bf16[128,512]{1,0:T(8,128)(2,1)S(1)} %get-tuple-element.65), channel_id=1, source_target_pairs={{0,7},{1,6},{2,5},{3,4},{4,3},{5,2},{6,1},{7,0},{8,15},{9,14},{10,... | collective-permute-start | bytes 393224 | tf_op jit(solution)/shard_map/ppermute | solution.py:513
  38.2 19.5 %copy-start.6 = (f32[8192]{0:T(1024)S(1)}, f32[8192]{0:T(1024)}, u32[]{:S(2)}) copy-start(f32[8192]{0:T(1024)} %param.15) | copy-start | bytes 98308
  39.7 6.0 %collective-permute-start.9 = (bf16[128,512]{1,0:T(8,128)(2,1)S(1)}, bf16[128,512]{1,0:T(8,128)(2,1)S(1)}, u32[]{:S(2)}, u32[]{:S(2)}) collective-permute-start(bf16[128,512]{1,0:T(8,128)(2,1)S(1)} %get-tuple-element.58), channel_id=1, source_target_pairs={{0,3},{1,2},{2,1},{3,0},{4,7},{5,6},{6,5},{7,4},{8,11},{9,10},{10,... | collective-permute-start | bytes 393224 | tf_op jit(solution)/shard_map/ppermute | solution.py:513
  39.9 6.4 %collective-permute-start.11 = (bf16[128,512]{1,0:T(8,128)(2,1)S(1)}, bf16[128,512]{1,0:T(8,128)(2,1)S(1)}, u32[]{:S(2)}, u32[]{:S(2)}) collective-permute-start(bf16[128,512]{1,0:T(8,128)(2,1)S(1)} %get-tuple-element.60), channel_id=1, source_target_pairs={{0,4},{1,5},{2,6},{3,7},{4,0},{5,1},{6,2},{7,3},{8,12},{9,13},{10,... | collective-permute-start | bytes 393224 | tf_op jit(solution)/shard_map/ppermute | solution.py:513
  42.3 15.4 %collective-permute-start.6 = (bf16[128,1024]{1,0:T(8,128)(2,1)S(1)}, bf16[128,1024]{1,0:T(8,128)(2,1)S(1)}, u32[]{:S(2)}, u32[]{:S(2)}) collective-permute-start(bf16[128,1024]{1,0:T(8,128)(2,1)S(1)} %get-tuple-element.55), channel_id=1, source_target_pairs={{0,1},{1,0},{2,3},{3,2},{4,5},{5,4},{6,7},{7,6},{8,9},{9,8},{10,11... | collective-permute-start | bytes 786440 | tf_op jit(solution)/shard_map/ppermute | solution.py:513
  43.1 14.6 %collective-permute-start.7 = (bf16[128,1024]{1,0:T(8,128)(2,1)S(1)}, bf16[128,1024]{1,0:T(8,128)(2,1)S(1)}, u32[]{:S(2)}, u32[]{:S(2)}) collective-permute-start(bf16[128,1024]{1,0:T(8,128)(2,1)S(1)} %get-tuple-element.56), channel_id=1, source_target_pairs={{0,2},{1,3},{2,0},{3,1},{4,6},{5,7},{6,4},{7,5},{8,10},{9,11},{10,... | collective-permute-start | bytes 786440 | tf_op jit(solution)/shard_map/ppermute | solution.py:513
  43.6 6.1 %collective-permute-start.13 = (bf16[128,512]{1,0:T(8,128)(2,1)S(1)}, bf16[128,512]{1,0:T(8,128)(2,1)S(1)}, u32[]{:S(2)}, u32[]{:S(2)}) collective-permute-start(bf16[128,512]{1,0:T(8,128)(2,1)S(1)} %get-tuple-element.62), channel_id=1, source_target_pairs={{0,5},{1,4},{2,7},{3,6},{4,1},{5,0},{6,3},{7,2},{8,13},{9,12},{10,... | collective-permute-start | bytes 393224 | tf_op jit(solution)/shard_map/ppermute | solution.py:513
  45.7 9.0 %collective-permute-start.15 = (bf16[128,512]{1,0:T(8,128)(2,1)S(1)}, bf16[128,512]{1,0:T(8,128)(2,1)S(1)}, u32[]{:S(2)}, u32[]{:S(2)}) collective-permute-start(bf16[128,512]{1,0:T(8,128)(2,1)S(1)} %get-tuple-element.64), channel_id=1, source_target_pairs={{0,6},{1,7},{2,4},{3,5},{4,2},{5,3},{6,0},{7,1},{8,14},{9,15},{10,... | collective-permute-start | bytes 393224 | tf_op jit(solution)/shard_map/ppermute | solution.py:513
  46.4 11.3 %collective-permute-start.17 = (bf16[128,512]{1,0:T(8,128)(2,1)S(1)}, bf16[128,512]{1,0:T(8,128)(2,1)S(1)}, u32[]{:S(2)}, u32[]{:S(2)}) collective-permute-start(bf16[128,512]{1,0:T(8,128)(2,1)S(1)} %get-tuple-element.66), channel_id=1, source_target_pairs={{0,7},{1,6},{2,5},{3,4},{4,3},{5,2},{6,1},{7,0},{8,15},{9,14},{10,... | collective-permute-start | bytes 393224 | tf_op jit(solution)/shard_map/ppermute | solution.py:513
  (4 other events, 5.8 us)

commit v6 on v5

--- a/solution.py
+++ b/solution.py
@@ -125,22 +125,20 @@
     message[...] = pack(total, through[...])
 
 
-def merge_kernel(bit, arrivals, follow, *refs):
-    del follow
-    got, (own, through, before, new_own, new_through, new_before, message) = (
-        refs[:arrivals],
-        refs[arrivals:],
-    )
+def merge_kernel(bit, arrivals, *refs):
+    got, (own, through, before, message, *new) = refs[:arrivals], refs[arrivals:]
     states = own.shape[0]
     total = sum(part[...].astype(jnp.float32) for part in got)
     decays = total[states : states + SUBLANES] + total[states + SUBLANES :]
     upper = jnp.bitwise_and(jnp.right_shift(lax.axis_index("seq"), bit), 1).astype(jnp.float32)
-    new_before[...] = before[...] * (decays + (1.0 - upper))
     summed = own[...] + total[:states] * through[:1]
     passed = through[...] * (decays + (1.0 - upper))
-    new_own[...] = summed
-    new_through[...] = passed
     message[...] = pack(summed, passed)
+    if new:
+        new_own, new_through, new_before = new
+        new_before[...] = before[...] * (decays + (1.0 - upper))
+        new_own[...] = summed
+        new_through[...] = passed
 
 
 def local_kernel(
@@ -438,23 +436,25 @@
             name="far_and_gate",
         )(me, local, coefs, query_rows, gate_z, *states)
 
-    def merge_call(bit, got, own, through, before, follow):
-        return pl.pallas_call(
-            functools.partial(merge_kernel, bit, len(got)),
-            in_specs=[anywhere] + [whole] * (len(got) + 3),
-            out_specs=[whole] * 4,
-            out_shape=[
+    def merge_call(bit, got, own, through, before, last):
+        out_shape = [jax.ShapeDtypeStruct(got[0].shape, jnp.bfloat16)]
+        if not last:
+            out_shape += [
                 jax.ShapeDtypeStruct(own.shape, jnp.float32),
                 jax.ShapeDtypeStruct(through.shape, jnp.float32),
                 jax.ShapeDtypeStruct(through.shape, jnp.float32),
-                jax.ShapeDtypeStruct(got[0].shape, jnp.bfloat16),
-            ],
+            ]
+        return pl.pallas_call(
+            functools.partial(merge_kernel, bit, len(got)),
+            in_specs=[whole] * (len(got) + 3),
+            out_specs=[whole] * len(out_shape),
+            out_shape=out_shape,
             compiler_params=params(4),
             cost_estimate=pl.CostEstimate(
                 flops=8 * state_size * part, bytes_accessed=16 * state_size * part, transcendentals=0
             ),
             name="merge_blocks",
-        )(follow, *got, own, through, before)
+        )(*got, own, through, before)
 
     four = seq_count == 4
     if four:
@@ -475,13 +475,15 @@
             got = [lax.ppermute(self.moving, "seq", p) for p in phases[len(self.arrived)]]
             self.arrived.append((got, self.before))
 
-        def finish(self, follow):
+        def finish(self):
             while self.arrived and len(self.arrived) < far:
                 got = self.arrived[-1][0]
                 bit = len(self.arrived) - 1
-                self.own, self.through, self.before, self.moving = merge_call(
-                    bit, got, self.own, self.through, self.before, follow
+                self.moving, *new = merge_call(
+                    bit, got, self.own, self.through, self.before, four
                 )
+                if new:
+                    self.own, self.through, self.before = new
                 self.post()
             if four and len(self.arrived) == far:
                 self.arrived = [([one], None) for got, _ in self.arrived for one in got]
@@ -491,7 +493,7 @@
         for chain in chains:
             chain.post()
     for chain in chains:
-        chain.finish(key_rows)
+        chain.finish()
     held = (1, 2)
     kept = {}
     pieces = []

time: 59.8 us -> 59.2 us (0.990)
  Pallas kernels: 18 us -> 16.6 us
  waiting for transfers between devices: 11.8 us -> 12.5 us
    pallas_call x2, Pallas kernels: 1.49 us -> 0.1 us  [merge_call(): pl.pallas_call(functools.partial(merge_kernel, bit, len(got)), in_specs=[...]
    ppermute x6, waiting for transfers between devices: 1.08 us -> 1.76 us  [post(): lax.ppermute(self.moving, 'seq', p)]
  transfers between devices with their start and end apart: 18 -> 18, of which waited for: 6 -> 6; matrix products, arithmetic and copies ran while one was open for 4% -> 4% of each run, Pallas kernels for 24% -> 22%
where the time goes in v6:
time: 59.2 us; the launch traced here: 58.9 us
  starting transfers between devices  23.4 us (40%)
  Pallas kernels  16.6 us (28%)
  waiting for transfers between devices  12.5 us (21%)
  local copies, waits for them, and re-layouts  6.03 us (10%)
    ppermute x12, starting transfers between devices, body(): got[apart] = lax.ppermute(out[apart], 'head', pairs)  14.4 us
    ppermute x12, waiting for transfers between devices, body(): got[apart] = lax.ppermute(out[apart], 'head', pairs)  10.7 us
    ppermute x6, starting transfers between devices, post(): lax.ppermute(self.moving, 'seq', p)  9.01 us
    pallas_call x2, Pallas kernels, local_call(): pl.pallas_call(functools.partial(local_kernel, head_dim, heads, c, far),...  9 us
    unnamed x22, local copies, waits for them, and re-layouts  3.34 us
    pallas_call x2, Pallas kernels, gate_call(): pl.pallas_call(functools.partial(gate_kernel, head_dim, heads, (near + 3)...  2.98 us
    dynamic_slice x1, local copies, waits for them, and re-layouts, body(): lax.dynamic_index_in_dim(c_queries, group_index, 1, keepdims=False)  2.14 us
    pallas_call x2, Pallas kernels, state_call(): pl.pallas_call(functools.partial(state_kernel, head_dim, heads, c * part,...  1.96 us
  transfers between devices with their start and end apart: 18, of which 6 were waited for; matrix products, arithmetic and copies ran while one was open for 4% of the time, Pallas kernels for 22%

profile of v6, /device:TPU:9, one launch (start us, length us, event | category | flops | bytes accessed | tf_op | source)
XLA Modules:
  0.0 58.9 jit_solution(4299495288728474395)
XLA Ops:
  3.2 1.6 %copy-done.2 = bf16[1024,1024]{1,0:T(8,128)(2,1)S(1)} copy-done((bf16[1024,1024]{1,0:T(8,128)(2,1)S(1)}, bf16[1024,1024]{1,0:T(8,128)(2,1)}, u32[]{:S(2)}) %copy-start.2) | copy-done | bytes 2097176
  5.7 1.3 %collective-permute-start.1 = (bf16[144,512]{1,0:T(8,128)(2,1)S(1)}, bf16[144,512]{1,0:T(8,128)(2,1)S(1)}, u32[]{:S(2)}, u32[]{:S(2)}) collective-permute-start(bf16[144,512]{1,0:T(8,128)(2,1)S(1)} %get-tuple-element.43), channel_id=1, source_target_pairs={{0,8},{1,9},{2,10},{3,11},{4,12},{5,13},{6,14},{7,15}} | collective-permute-start | bytes 442376 | tf_op jit(solution)/shard_map/ppermute | solution.py:475
  7.0 2.1 %constant_dynamic-slice_fusion.1 = bf16[1024,1,128]{2,1,0:T(2,128)(2,1)S(1)} fusion(bf16[1024,8,128]{2,1,0:T(8,128)(2,1)} %param.11, s32[]{:T(128)S(6)} %select_n.11), kind=kLoop, calls=%fused_computation.3 | loop fusion | bytes 524292 | tf_op jit(solution)/shard_map/jit(dynamic_index_in_dim)/dynamic_slice | solution.py:361
  10.3 1.3 %collective-permute-start = (bf16[144,512]{1,0:T(8,128)(2,1)S(1)}, bf16[144,512]{1,0:T(8,128)(2,1)S(1)}, u32[]{:S(2)}, u32[]{:S(2)}) collective-permute-start(bf16[144,512]{1,0:T(8,128)(2,1)S(1)} %get-tuple-element.38), channel_id=1, source_target_pairs={{0,8},{1,9},{2,10},{3,11},{4,12},{5,13},{6,14},{7,15}} | collective-permute-start | bytes 442376 | tf_op jit(solution)/shard_map/ppermute | solution.py:475
  12.4 2.2 %collective-permute-start.3 = (bf16[144,512]{1,0:T(8,128)(2,1)S(1)}, bf16[144,512]{1,0:T(8,128)(2,1)S(1)}, u32[]{:S(2)}, u32[]{:S(2)}) collective-permute-start(bf16[144,512]{1,0:T(8,128)(2,1)S(1)} %merge_blocks.3), channel_id=1, source_target_pairs={{8,24},{9,25},{10,26},{11,27},{12,28},{13,29},{14,30},{15,31}} | collective-permute-start | bytes 442376 | tf_op jit(solution)/shard_map/ppermute | solution.py:475
  14.6 1.3 %collective-permute-start.2 = (bf16[144,512]{1,0:T(8,128)(2,1)S(1)}, bf16[144,512]{1,0:T(8,128)(2,1)S(1)}, u32[]{:S(2)}, u32[]{:S(2)}) collective-permute-start(bf16[144,512]{1,0:T(8,128)(2,1)S(1)} %merge_blocks.3), channel_id=1, source_target_pairs={{8,16},{16,24},{9,17},{17,25},{10,18},{18,26},{11,19},{19,27},{12,... | collective-permute-start | bytes 442376 | tf_op jit(solution)/shard_map/ppermute | solution.py:475
  17.0 1.4 %collective-permute-start.5 = (bf16[144,512]{1,0:T(8,128)(2,1)S(1)}, bf16[144,512]{1,0:T(8,128)(2,1)S(1)}, u32[]{:S(2)}, u32[]{:S(2)}) collective-permute-start(bf16[144,512]{1,0:T(8,128)(2,1)S(1)} %merge_blocks.2.rest_0_), channel_id=1, source_target_pairs={{8,24},{9,25},{10,26},{11,27},{12,28},{13,29},{14,30},{15,31}} | collective-permute-start | bytes 442376 | tf_op jit(solution)/shard_map/ppermute | solution.py:475
  18.4 1.5 %collective-permute-start.4 = (bf16[144,512]{1,0:T(8,128)(2,1)S(1)}, bf16[144,512]{1,0:T(8,128)(2,1)S(1)}, u32[]{:S(2)}, u32[]{:S(2)}) collective-permute-start(bf16[144,512]{1,0:T(8,128)(2,1)S(1)} %merge_blocks.2.rest_0_), channel_id=1, source_target_pairs={{8,16},{16,24},{9,17},{17,25},{10,18},{18,26},{11,19},{19,27},{12,... | collective-permute-start | bytes 442376 | tf_op jit(solution)/shard_map/ppermute | solution.py:475
  19.9 4.5 %local_mixer.2 = (f32[1024,512]{1,0:T(8,128)S(1)}, bf16[1024,256]{1,0:T(8,128)(2,1)S(1)}) custom-call(s32[64]{0:T(128)S(1)} %copy-done.8, f32[16,1024]{1,0:T(8,128)S(1)} %bitcast.21, f32[7,16,1024]{2,1,0:T(8,128)S(1)} %bitcast.24, bf16[1024,1024]{1,0:T(8,128)(2,1)S(1)} %copy-done.3, bf16[1024,128]{1,0:T(8,128)(2,1)S(1)} %bitcast.11, ...), custom_call_target="tpu_custom_call" | custom-call | flops 1073741824 | bytes 6291456 | tf_op jit(solution)/shard_map/local_mixer/pallas_call | solution.py:383
  24.4 1.5 %far_and_gate.2 = (bf16[128,512]{1,0:T(8,128)(2,1)S(1)}, bf16[128,512]{1,0:T(8,128)(2,1)S(1)}, bf16[128,512]{1,0:T(8,128)(2,1)S(1)}, bf16[128,512]{1,0:T(8,128)(...) custom-call(s32[1]{0:T(128)} %bitcast.me, ...), custom_call_target="tpu_custom_call" | custom-call | flops 268435456 | bytes 4194304 | tf_op jit(solution)/shard_map/far_and_gate/pallas_call | solution.py:416
  25.9 2.7 %collective-permute-start.8 = (bf16[128,512]{1,0:T(8,128)(2,1)S(1)}, bf16[128,512]{1,0:T(8,128)(2,1)S(1)}, u32[]{:S(2)}, u32[]{:S(2)}) collective-permute-start(bf16[128,512]{1,0:T(8,128)(2,1)S(1)} %get-tuple-element.53), channel_id=1, source_target_pairs={{0,3},{1,2},{2,1},{3,0},{4,7},{5,6},{6,5},{7,4},{8,11},{9,10},{10,... | collective-permute-start | bytes 393224 | tf_op jit(solution)/shard_map/ppermute | solution.py:515
  28.6 1.3 %collective-permute-start.10 = (bf16[128,512]{1,0:T(8,128)(2,1)S(1)}, bf16[128,512]{1,0:T(8,128)(2,1)S(1)}, u32[]{:S(2)}, u32[]{:S(2)}) collective-permute-start(bf16[128,512]{1,0:T(8,128)(2,1)S(1)} %get-tuple-element.55), channel_id=1, source_target_pairs={{0,4},{1,5},{2,6},{3,7},{4,0},{5,1},{6,2},{7,3},{8,12},{9,13},{10,... | collective-permute-start | bytes 393224 | tf_op jit(solution)/shard_map/ppermute | solution.py:515
  29.9 1.5 %collective-permute-start.14 = (bf16[128,512]{1,0:T(8,128)(2,1)S(1)}, bf16[128,512]{1,0:T(8,128)(2,1)S(1)}, u32[]{:S(2)}, u32[]{:S(2)}) collective-permute-start(bf16[128,512]{1,0:T(8,128)(2,1)S(1)} %get-tuple-element.59), channel_id=1, source_target_pairs={{0,6},{1,7},{2,4},{3,5},{4,2},{5,3},{6,0},{7,1},{8,14},{9,15},{10,... | collective-permute-start | bytes 393224 | tf_op jit(solution)/shard_map/ppermute | solution.py:515
  31.4 1.6 %collective-permute-start.16 = (bf16[128,512]{1,0:T(8,128)(2,1)S(1)}, bf16[128,512]{1,0:T(8,128)(2,1)S(1)}, u32[]{:S(2)}, u32[]{:S(2)}) collective-permute-start(bf16[128,512]{1,0:T(8,128)(2,1)S(1)} %get-tuple-element.61), channel_id=1, source_target_pairs={{0,7},{1,6},{2,5},{3,4},{4,3},{5,2},{6,1},{7,0},{8,15},{9,14},{10,... | collective-permute-start | bytes 393224 | tf_op jit(solution)/shard_map/ppermute | solution.py:515
  33.0 4.5 %local_mixer.3 = (f32[1024,512]{1,0:T(8,128)S(1)}, bf16[1024,256]{1,0:T(8,128)(2,1)S(1)}) custom-call(s32[64]{0:T(128)S(1)} %copy-done.8, f32[16,1024]{1,0:T(8,128)S(1)} %bitcast.22, f32[7,16,1024]{2,1,0:T(8,128)S(1)} %bitcast.25, bf16[1024,1024]{1,0:T(8,128)(2,1)S(1)} %copy-done.3, bf16[1024,128]{1,0:T(8,128)(2,1)S(1)} %bitcast.13, ...), custom_call_target="tpu_custom_call" | custom-call | flops 1073741824 | bytes 6291456 | tf_op jit(solution)/shard_map/local_mixer/pallas_call | solution.py:383
  37.5 1.5 %far_and_gate.3 = (bf16[128,512]{1,0:T(8,128)(2,1)S(1)}, bf16[128,1024]{1,0:T(8,128)(2,1)S(1)}, bf16[128,1024]{1,0:T(8,128)(2,1)S(1)}, bf16[128,512]{1,0:T(8,128...) custom-call(s32[1]{0:T(128)} %bitcast.me, ...), custom_call_target="tpu_custom_call" | custom-call | flops 268435456 | bytes 4194304 | tf_op jit(solution)/shard_map/far_and_gate/pallas_call | solution.py:416
  39.2 1.4 %collective-permute-start.11 = (bf16[128,512]{1,0:T(8,128)(2,1)S(1)}, bf16[128,512]{1,0:T(8,128)(2,1)S(1)}, u32[]{:S(2)}, u32[]{:S(2)}) collective-permute-start(bf16[128,512]{1,0:T(8,128)(2,1)S(1)} %get-tuple-element.56), channel_id=1, source_target_pairs={{0,4},{1,5},{2,6},{3,7},{4,0},{5,1},{6,2},{7,3},{8,12},{9,13},{10,... | collective-permute-start | bytes 393224 | tf_op jit(solution)/shard_map/ppermute | solution.py:515
  40.7 1.0 %collective-permute-done.12.rest_8_ = bf16[128,512]{1,0:T(8,128)(2,1)S(1)} collective-permute-done((bf16[128,512]{1,0:T(8,128)(2,1)S(1)}, bf16[128,512]{1,0:T(8,128)(2,1)S(1)}, u32[]{:S(2)}, u32[]{:S(2)}) %collective-permute-start.12) | collective-permute-done | bytes 131104 | tf_op jit(solution)/shard_map/ppermute | solution.py:515
  42.9 2.1 %collective-permute-start.13 = (bf16[128,512]{1,0:T(8,128)(2,1)S(1)}, bf16[128,512]{1,0:T(8,128)(2,1)S(1)}, u32[]{:S(2)}, u32[]{:S(2)}) collective-permute-start(bf16[128,512]{1,0:T(8,128)(2,1)S(1)} %get-tuple-element.58), channel_id=1, source_target_pairs={{0,5},{1,4},{2,7},{3,6},{4,1},{5,0},{6,3},{7,2},{8,13},{9,12},{10,... | collective-permute-start | bytes 393224 | tf_op jit(solution)/shard_map/ppermute | solution.py:515
  45.7 1.7 %collective-permute-start.17 = (bf16[128,512]{1,0:T(8,128)(2,1)S(1)}, bf16[128,512]{1,0:T(8,128)(2,1)S(1)}, u32[]{:S(2)}, u32[]{:S(2)}) collective-permute-start(bf16[128,512]{1,0:T(8,128)(2,1)S(1)} %get-tuple-element.62), channel_id=1, source_target_pairs={{0,7},{1,6},{2,5},{3,4},{4,3},{5,2},{6,1},{7,0},{8,15},{9,14},{10,... | collective-permute-start | bytes 393224 | tf_op jit(solution)/shard_map/ppermute | solution.py:515
  47.3 1.7 %collective-permute-done.13.rest_9_ = bf16[128,512]{1,0:T(8,128)(2,1)S(1)} collective-permute-done((bf16[128,512]{1,0:T(8,128)(2,1)S(1)}, bf16[128,512]{1,0:T(8,128)(2,1)S(1)}, u32[]{:S(2)}, u32[]{:S(2)}) %collective-permute-start.13) | collective-permute-done | bytes 131104 | tf_op jit(solution)/shard_map/ppermute | solution.py:515
  49.0 5.1 %collective-permute-done.15.rest_11_ = bf16[128,512]{1,0:T(8,128)(2,1)S(1)} collective-permute-done((bf16[128,512]{1,0:T(8,128)(2,1)S(1)}, bf16[128,512]{1,0:T(8,128)(2,1)S(1)}, u32[]{:S(2)}, u32[]{:S(2)}) %collective-permute-start.15) | collective-permute-done | bytes 131104 | tf_op jit(solution)/shard_map/ppermute | solution.py:515
  54.1 2.9 %collective-permute-done.17.rest_13_ = bf16[128,512]{1,0:T(8,128)(2,1)S(1)} collective-permute-done((bf16[128,512]{1,0:T(8,128)(2,1)S(1)}, bf16[128,512]{1,0:T(8,128)(2,1)S(1)}, u32[]{:S(2)}, u32[]{:S(2)}) %collective-permute-start.17) | collective-permute-done | bytes 131104 | tf_op jit(solution)/shard_map/ppermute | solution.py:515
  57.0 1.7 %norm_rows.1 = bf16[128,8192]{1,0:T(8,128)(2,1)} custom-call(s32[1]{0:T(128)} %bitcast.me, f32[1,8192]{1,0:T(1,128)S(1)} %bitcast.23, bf16[128,512]{1,0:T(8,128)(2,1)S(1)} %get-tuple-element.45.rest_0_, bf16[128,512]{1,0:T(8,128)(2,1)S(1)} %get-tuple-element.50.rest_1_, bf16[128,1024]{1,0:T(8,128)(2,1)S(1)} %collective-permute-done.6.rest_2_, ...), custom_call_target="tpu_custom_call" | custom-call | flops 8388608 | bytes 4194304 | tf_op jit(solution)/shard_map/norm_rows/pallas_call | solution.py:536
  (47 shorter events, 9.1 us)
Async XLA Ops:
  4.7 4.5 %copy-start.3 = (bf16[1024,1024]{1,0:T(8,128)(2,1)S(1)}, bf16[1024,1024]{1,0:T(8,128)(2,1)}, u32[]{:S(2)}) copy-start(bf16[1024,1024]{1,0:T(8,128)(2,1)} %values.7) | copy-start | bytes 6291460
  5.7 6.6 %collective-permute-start.1 = (bf16[144,512]{1,0:T(8,128)(2,1)S(1)}, bf16[144,512]{1,0:T(8,128)(2,1)S(1)}, u32[]{:S(2)}, u32[]{:S(2)}) collective-permute-start(bf16[144,512]{1,0:T(8,128)(2,1)S(1)} %get-tuple-element.43), channel_id=1, source_target_pairs={{0,8},{1,9},{2,10},{3,11},{4,12},{5,13},{6,14},{7,15}} | collective-permute-start | bytes 442376 | tf_op jit(solution)/shard_map/ppermute | solution.py:475
  9.2 10.7 %copy-start.5 = (f32[1024,16]{0,1:T(8,128)S(1)}, f32[1024,16]{0,1:T(8,128)}, u32[]{:S(2)}) copy-start(f32[1024,16]{0,1:T(8,128)} %param.12) | copy-start | bytes 196612
  9.2 10.7 %copy-start.8 = (s32[64]{0:T(128)S(1)}, s32[64]{0:T(128)}, u32[]{:S(2)}) copy-start(s32[64]{0:T(128)} %docs.5) | copy-start | bytes 772
  9.2 10.7 %copy-start.9 = (f32[1024,16,7]{0,1,2:T(8,128)S(1)}, f32[1024,16,7]{0,1,2:T(8,128)}, u32[]{:S(2)}) copy-start(f32[1024,16,7]{0,1,2:T(8,128)} %param.13) | copy-start | bytes 1376260
  10.3 6.6 %collective-permute-start = (bf16[144,512]{1,0:T(8,128)(2,1)S(1)}, bf16[144,512]{1,0:T(8,128)(2,1)S(1)}, u32[]{:S(2)}, u32[]{:S(2)}) collective-permute-start(bf16[144,512]{1,0:T(8,128)(2,1)S(1)} %get-tuple-element.38), channel_id=1, source_target_pairs={{0,8},{1,9},{2,10},{3,11},{4,12},{5,13},{6,14},{7,15}} | collective-permute-start | bytes 442376 | tf_op jit(solution)/shard_map/ppermute | solution.py:475
  12.4 12.0 %collective-permute-start.3 = (bf16[144,512]{1,0:T(8,128)(2,1)S(1)}, bf16[144,512]{1,0:T(8,128)(2,1)S(1)}, u32[]{:S(2)}, u32[]{:S(2)}) collective-permute-start(bf16[144,512]{1,0:T(8,128)(2,1)S(1)} %merge_blocks.3), channel_id=1, source_target_pairs={{8,24},{9,25},{10,26},{11,27},{12,28},{13,29},{14,30},{15,31}} | collective-permute-start | bytes 442376 | tf_op jit(solution)/shard_map/ppermute | solution.py:475
  14.6 9.8 %collective-permute-start.2 = (bf16[144,512]{1,0:T(8,128)(2,1)S(1)}, bf16[144,512]{1,0:T(8,128)(2,1)S(1)}, u32[]{:S(2)}, u32[]{:S(2)}) collective-permute-start(bf16[144,512]{1,0:T(8,128)(2,1)S(1)} %merge_blocks.3), channel_id=1, source_target_pairs={{8,16},{16,24},{9,17},{17,25},{10,18},{18,26},{11,19},{19,27},{12,... | collective-permute-start | bytes 442376 | tf_op jit(solution)/shard_map/ppermute | solution.py:475
  16.9 7.5 %copy-start.1 = (bf16[1024,1024]{1,0:T(8,128)(2,1)S(1)}, bf16[1024,1024]{1,0:T(8,128)(2,1)}, u32[]{:S(2)}) copy-start(bf16[1024,1024]{1,0:T(8,128)(2,1)} %refs_3_.3) | copy-start | bytes 6291460
  17.0 12.9 %collective-permute-start.5 = (bf16[144,512]{1,0:T(8,128)(2,1)S(1)}, bf16[144,512]{1,0:T(8,128)(2,1)S(1)}, u32[]{:S(2)}, u32[]{:S(2)}) collective-permute-start(bf16[144,512]{1,0:T(8,128)(2,1)S(1)} %merge_blocks.2.rest_0_), channel_id=1, source_target_pairs={{8,24},{9,25},{10,26},{11,27},{12,28},{13,29},{14,30},{15,31}} | collective-permute-start | bytes 442376 | tf_op jit(solution)/shard_map/ppermute | solution.py:475
  18.4 13.0 %collective-permute-start.4 = (bf16[144,512]{1,0:T(8,128)(2,1)S(1)}, bf16[144,512]{1,0:T(8,128)(2,1)S(1)}, u32[]{:S(2)}, u32[]{:S(2)}) collective-permute-start(bf16[144,512]{1,0:T(8,128)(2,1)S(1)} %merge_blocks.2.rest_0_), channel_id=1, source_target_pairs={{8,16},{16,24},{9,17},{17,25},{10,18},{18,26},{11,19},{19,27},{12,... | collective-permute-start | bytes 442376 | tf_op jit(solution)/shard_map/ppermute | solution.py:475
  25.9 13.1 %collective-permute-start.8 = (bf16[128,512]{1,0:T(8,128)(2,1)S(1)}, bf16[128,512]{1,0:T(8,128)(2,1)S(1)}, u32[]{:S(2)}, u32[]{:S(2)}) collective-permute-start(bf16[128,512]{1,0:T(8,128)(2,1)S(1)} %get-tuple-element.53), channel_id=1, source_target_pairs={{0,3},{1,2},{2,1},{3,0},{4,7},{5,6},{6,5},{7,4},{8,11},{9,10},{10,... | collective-permute-start | bytes 393224 | tf_op jit(solution)/shard_map/ppermute | solution.py:515
  28.6 10.6 %collective-permute-start.10 = (bf16[128,512]{1,0:T(8,128)(2,1)S(1)}, bf16[128,512]{1,0:T(8,128)(2,1)S(1)}, u32[]{:S(2)}, u32[]{:S(2)}) collective-permute-start(bf16[128,512]{1,0:T(8,128)(2,1)S(1)} %get-tuple-element.55), channel_id=1, source_target_pairs={{0,4},{1,5},{2,6},{3,7},{4,0},{5,1},{6,2},{7,3},{8,12},{9,13},{10,... | collective-permute-start | bytes 393224 | tf_op jit(solution)/shard_map/ppermute | solution.py:515
  29.9 11.8 %collective-permute-start.12 = (bf16[128,512]{1,0:T(8,128)(2,1)S(1)}, bf16[128,512]{1,0:T(8,128)(2,1)S(1)}, u32[]{:S(2)}, u32[]{:S(2)}) collective-permute-start(bf16[128,512]{1,0:T(8,128)(2,1)S(1)} %get-tuple-element.57), channel_id=1, source_target_pairs={{0,5},{1,4},{2,7},{3,6},{4,1},{5,0},{6,3},{7,2},{8,13},{9,12},{10,... | collective-permute-start | bytes 393224 | tf_op jit(solution)/shard_map/ppermute | solution.py:515
  29.9 12.5 %collective-permute-start.14 = (bf16[128,512]{1,0:T(8,128)(2,1)S(1)}, bf16[128,512]{1,0:T(8,128)(2,1)S(1)}, u32[]{:S(2)}, u32[]{:S(2)}) collective-permute-start(bf16[128,512]{1,0:T(8,128)(2,1)S(1)} %get-tuple-element.59), channel_id=1, source_target_pairs={{0,6},{1,7},{2,4},{3,5},{4,2},{5,3},{6,0},{7,1},{8,14},{9,15},{10,... | collective-permute-start | bytes 393224 | tf_op jit(solution)/shard_map/ppermute | solution.py:515
  31.4 11.5 %collective-permute-start.16 = (bf16[128,512]{1,0:T(8,128)(2,1)S(1)}, bf16[128,512]{1,0:T(8,128)(2,1)S(1)}, u32[]{:S(2)}, u32[]{:S(2)}) collective-permute-start(bf16[128,512]{1,0:T(8,128)(2,1)S(1)} %get-tuple-element.61), channel_id=1, source_target_pairs={{0,7},{1,6},{2,5},{3,4},{4,3},{5,2},{6,1},{7,0},{8,15},{9,14},{10,... | collective-permute-start | bytes 393224 | tf_op jit(solution)/shard_map/ppermute | solution.py:515
  37.5 19.5 %copy-start.6 = (f32[8192]{0:T(1024)S(1)}, f32[8192]{0:T(1024)}, u32[]{:S(2)}) copy-start(f32[8192]{0:T(1024)} %param.15) | copy-start | bytes 98308
  39.1 6.0 %collective-permute-start.9 = (bf16[128,512]{1,0:T(8,128)(2,1)S(1)}, bf16[128,512]{1,0:T(8,128)(2,1)S(1)}, u32[]{:S(2)}, u32[]{:S(2)}) collective-permute-start(bf16[128,512]{1,0:T(8,128)(2,1)S(1)} %get-tuple-element.54), channel_id=1, source_target_pairs={{0,3},{1,2},{2,1},{3,0},{4,7},{5,6},{6,5},{7,4},{8,11},{9,10},{10,... | collective-permute-start | bytes 393224 | tf_op jit(solution)/shard_map/ppermute | solution.py:515
  39.2 6.4 %collective-permute-start.11 = (bf16[128,512]{1,0:T(8,128)(2,1)S(1)}, bf16[128,512]{1,0:T(8,128)(2,1)S(1)}, u32[]{:S(2)}, u32[]{:S(2)}) collective-permute-start(bf16[128,512]{1,0:T(8,128)(2,1)S(1)} %get-tuple-element.56), channel_id=1, source_target_pairs={{0,4},{1,5},{2,6},{3,7},{4,0},{5,1},{6,2},{7,3},{8,12},{9,13},{10,... | collective-permute-start | bytes 393224 | tf_op jit(solution)/shard_map/ppermute | solution.py:515
  41.7 15.4 %collective-permute-start.6 = (bf16[128,1024]{1,0:T(8,128)(2,1)S(1)}, bf16[128,1024]{1,0:T(8,128)(2,1)S(1)}, u32[]{:S(2)}, u32[]{:S(2)}) collective-permute-start(bf16[128,1024]{1,0:T(8,128)(2,1)S(1)} %get-tuple-element.51), channel_id=1, source_target_pairs={{0,1},{1,0},{2,3},{3,2},{4,5},{5,4},{6,7},{7,6},{8,9},{9,8},{10,11... | collective-permute-start | bytes 786440 | tf_op jit(solution)/shard_map/ppermute | solution.py:515
  42.4 14.6 %collective-permute-start.7 = (bf16[128,1024]{1,0:T(8,128)(2,1)S(1)}, bf16[128,1024]{1,0:T(8,128)(2,1)S(1)}, u32[]{:S(2)}, u32[]{:S(2)}) collective-permute-start(bf16[128,1024]{1,0:T(8,128)(2,1)S(1)} %get-tuple-element.52), channel_id=1, source_target_pairs={{0,2},{1,3},{2,0},{3,1},{4,6},{5,7},{6,4},{7,5},{8,10},{9,11},{10,... | collective-permute-start | bytes 786440 | tf_op jit(solution)/shard_map/ppermute | solution.py:515
  42.9 6.1 %collective-permute-start.13 = (bf16[128,512]{1,0:T(8,128)(2,1)S(1)}, bf16[128,512]{1,0:T(8,128)(2,1)S(1)}, u32[]{:S(2)}, u32[]{:S(2)}) collective-permute-start(bf16[128,512]{1,0:T(8,128)(2,1)S(1)} %get-tuple-element.58), channel_id=1, source_target_pairs={{0,5},{1,4},{2,7},{3,6},{4,1},{5,0},{6,3},{7,2},{8,13},{9,12},{10,... | collective-permute-start | bytes 393224 | tf_op jit(solution)/shard_map/ppermute | solution.py:515
  45.1 9.0 %collective-permute-start.15 = (bf16[128,512]{1,0:T(8,128)(2,1)S(1)}, bf16[128,512]{1,0:T(8,128)(2,1)S(1)}, u32[]{:S(2)}, u32[]{:S(2)}) collective-permute-start(bf16[128,512]{1,0:T(8,128)(2,1)S(1)} %get-tuple-element.60), channel_id=1, source_target_pairs={{0,6},{1,7},{2,4},{3,5},{4,2},{5,3},{6,0},{7,1},{8,14},{9,15},{10,... | collective-permute-start | bytes 393224 | tf_op jit(solution)/shard_map/ppermute | solution.py:515
  45.7 11.3 %collective-permute-start.17 = (bf16[128,512]{1,0:T(8,128)(2,1)S(1)}, bf16[128,512]{1,0:T(8,128)(2,1)S(1)}, u32[]{:S(2)}, u32[]{:S(2)}) collective-permute-start(bf16[128,512]{1,0:T(8,128)(2,1)S(1)} %get-tuple-element.62), channel_id=1, source_target_pairs={{0,7},{1,6},{2,5},{3,4},{4,3},{5,2},{6,1},{7,0},{8,15},{9,14},{10,... | collective-permute-start | bytes 393224 | tf_op jit(solution)/shard_map/ppermute | solution.py:515
  (4 other events, 5.8 us)

commit v7 on v6

--- a/solution.py
+++ b/solution.py
@@ -335,6 +335,7 @@
     part = width // chunks
     levels = weight.shape[0]
     smem = pl.BlockSpec(memory_space=pltpu.SMEM)
+    parts = [values[:, :part]] + [values] * (chunks - 1)
 
     whole = pl.BlockSpec(memory_space=pltpu.VMEM)
     anywhere = pl.BlockSpec(memory_space=pl.ANY)
@@ -376,7 +377,7 @@
                 flops=4 * tokens * state_size * part, bytes_accessed=3 * tokens * part, transcendentals=0
             ),
             name="block_state",
-        )(terms, through, key_rows, values, key_rows if c == 0 else query_rows)
+        )(terms, through, key_rows, parts[c], key_rows if c == 0 else query_rows)
         return state, message, through
 
     def local_call(c, follow):

time: 59.2 us -> 58.9 us (level)
    unnamed x22 -> x20, local copies, waits for them, and re-layouts: 3.34 us -> 1.76 us
    slice x0 -> x1, local copies, waits for them, and re-layouts: none -> 1.3 us  [body(): parts = [values[:, :part]] + [values] * (chunks - 1)]
where the time goes in v7:
time: 58.9 us; the launch traced here: 58.6 us
  starting transfers between devices  23.4 us (40%)
  Pallas kernels  16.6 us (28%)
  waiting for transfers between devices  12.4 us (21%)
  local copies, waits for them, and re-layouts  5.74 us (10%)
    ppermute x12, starting transfers between devices, body(): got[apart] = lax.ppermute(out[apart], 'head', pairs)  14.3 us
    ppermute x12, waiting for transfers between devices, body(): got[apart] = lax.ppermute(out[apart], 'head', pairs)  10.7 us
    ppermute x6, starting transfers between devices, post(): lax.ppermute(self.moving, 'seq', p)  9.03 us
    pallas_call x2, Pallas kernels, local_call(): pl.pallas_call(functools.partial(local_kernel, head_dim, heads, c, far),...  9.02 us
    pallas_call x2, Pallas kernels, gate_call(): pl.pallas_call(functools.partial(gate_kernel, head_dim, heads, (near + 3)...  2.98 us
    dynamic_slice x1, local copies, waits for them, and re-layouts, body(): lax.dynamic_index_in_dim(c_queries, group_index, 1, keepdims=False)  2.14 us
    pallas_call x2, Pallas kernels, state_call(): pl.pallas_call(functools.partial(state_kernel, head_dim, heads, c * part,...  1.96 us
    unnamed x20, local copies, waits for them, and re-layouts  1.76 us
  transfers between devices with their start and end apart: 18, of which 6 were waited for; matrix products, arithmetic and copies ran while one was open for 4% of the time, Pallas kernels for 22%

profile of v7, /device:TPU:9, one launch (start us, length us, event | category | flops | bytes accessed | tf_op | source)
XLA Modules:
  0.0 58.6 jit_solution(1435623363549853982)
XLA Ops:
  3.1 1.3 %slice.3.values = bf16[1024,512]{1,0:T(8,128)(2,1)S(1)} slice(bf16[1024,1024]{1,0:T(8,128)(2,1)} %values.5), slice={[0:1024], [0:512]} | slice | bytes 2097152 | tf_op jit(solution)/shard_map/slice | solution.py:338
  5.4 1.3 %collective-permute-start.1 = (bf16[144,512]{1,0:T(8,128)(2,1)S(1)}, bf16[144,512]{1,0:T(8,128)(2,1)S(1)}, u32[]{:S(2)}, u32[]{:S(2)}) collective-permute-start(bf16[144,512]{1,0:T(8,128)(2,1)S(1)} %get-tuple-element.43), channel_id=1, source_target_pairs={{0,8},{1,9},{2,10},{3,11},{4,12},{5,13},{6,14},{7,15}} | collective-permute-start | bytes 442376 | tf_op jit(solution)/shard_map/ppermute | solution.py:476
  6.7 2.1 %constant_dynamic-slice_fusion.1 = bf16[1024,1,128]{2,1,0:T(2,128)(2,1)S(1)} fusion(bf16[1024,8,128]{2,1,0:T(8,128)(2,1)} %param.11, s32[]{:T(128)S(6)} %select_n.11), kind=kLoop, calls=%fused_computation.3 | loop fusion | bytes 524292 | tf_op jit(solution)/shard_map/jit(dynamic_index_in_dim)/dynamic_slice | solution.py:362
  10.0 1.3 %collective-permute-start = (bf16[144,512]{1,0:T(8,128)(2,1)S(1)}, bf16[144,512]{1,0:T(8,128)(2,1)S(1)}, u32[]{:S(2)}, u32[]{:S(2)}) collective-permute-start(bf16[144,512]{1,0:T(8,128)(2,1)S(1)} %get-tuple-element.38), channel_id=1, source_target_pairs={{0,8},{1,9},{2,10},{3,11},{4,12},{5,13},{6,14},{7,15}} | collective-permute-start | bytes 442376 | tf_op jit(solution)/shard_map/ppermute | solution.py:476
  12.1 2.2 %collective-permute-start.3 = (bf16[144,512]{1,0:T(8,128)(2,1)S(1)}, bf16[144,512]{1,0:T(8,128)(2,1)S(1)}, u32[]{:S(2)}, u32[]{:S(2)}) collective-permute-start(bf16[144,512]{1,0:T(8,128)(2,1)S(1)} %merge_blocks.3), channel_id=1, source_target_pairs={{8,24},{9,25},{10,26},{11,27},{12,28},{13,29},{14,30},{15,31}} | collective-permute-start | bytes 442376 | tf_op jit(solution)/shard_map/ppermute | solution.py:476
  14.3 1.3 %collective-permute-start.2 = (bf16[144,512]{1,0:T(8,128)(2,1)S(1)}, bf16[144,512]{1,0:T(8,128)(2,1)S(1)}, u32[]{:S(2)}, u32[]{:S(2)}) collective-permute-start(bf16[144,512]{1,0:T(8,128)(2,1)S(1)} %merge_blocks.3), channel_id=1, source_target_pairs={{8,16},{16,24},{9,17},{17,25},{10,18},{18,26},{11,19},{19,27},{12,... | collective-permute-start | bytes 442376 | tf_op jit(solution)/shard_map/ppermute | solution.py:476
  16.6 1.4 %collective-permute-start.5 = (bf16[144,512]{1,0:T(8,128)(2,1)S(1)}, bf16[144,512]{1,0:T(8,128)(2,1)S(1)}, u32[]{:S(2)}, u32[]{:S(2)}) collective-permute-start(bf16[144,512]{1,0:T(8,128)(2,1)S(1)} %merge_blocks.2.rest_0_), channel_id=1, source_target_pairs={{8,24},{9,25},{10,26},{11,27},{12,28},{13,29},{14,30},{15,31}} | collective-permute-start | bytes 442376 | tf_op jit(solution)/shard_map/ppermute | solution.py:476
  18.1 1.5 %collective-permute-start.4 = (bf16[144,512]{1,0:T(8,128)(2,1)S(1)}, bf16[144,512]{1,0:T(8,128)(2,1)S(1)}, u32[]{:S(2)}, u32[]{:S(2)}) collective-permute-start(bf16[144,512]{1,0:T(8,128)(2,1)S(1)} %merge_blocks.2.rest_0_), channel_id=1, source_target_pairs={{8,16},{16,24},{9,17},{17,25},{10,18},{18,26},{11,19},{19,27},{12,... | collective-permute-start | bytes 442376 | tf_op jit(solution)/shard_map/ppermute | solution.py:476
  19.6 4.5 %local_mixer.2 = (f32[1024,512]{1,0:T(8,128)S(1)}, bf16[1024,256]{1,0:T(8,128)(2,1)S(1)}) custom-call(s32[64]{0:T(128)S(1)} %copy-done.7, f32[16,1024]{1,0:T(8,128)S(1)} %bitcast.21, f32[7,16,1024]{2,1,0:T(8,128)S(1)} %bitcast.24, bf16[1024,1024]{1,0:T(8,128)(2,1)S(1)} %copy-done.2, bf16[1024,128]{1,0:T(8,128)(2,1)S(1)} %bitcast.16, ...), custom_call_target="tpu_custom_call" | custom-call | flops 1073741824 | bytes 6291456 | tf_op jit(solution)/shard_map/local_mixer/pallas_call | solution.py:384
  24.1 1.5 %far_and_gate.2 = (bf16[128,512]{1,0:T(8,128)(2,1)S(1)}, bf16[128,512]{1,0:T(8,128)(2,1)S(1)}, bf16[128,512]{1,0:T(8,128)(2,1)S(1)}, bf16[128,512]{1,0:T(8,128)(...) custom-call(s32[1]{0:T(128)} %bitcast.me, ...), custom_call_target="tpu_custom_call" | custom-call | flops 268435456 | bytes 4194304 | tf_op jit(solution)/shard_map/far_and_gate/pallas_call | solution.py:417
  25.6 2.7 %collective-permute-start.8 = (bf16[128,512]{1,0:T(8,128)(2,1)S(1)}, bf16[128,512]{1,0:T(8,128)(2,1)S(1)}, u32[]{:S(2)}, u32[]{:S(2)}) collective-permute-start(bf16[128,512]{1,0:T(8,128)(2,1)S(1)} %get-tuple-element.53), channel_id=1, source_target_pairs={{0,3},{1,2},{2,1},{3,0},{4,7},{5,6},{6,5},{7,4},{8,11},{9,10},{10,... | collective-permute-start | bytes 393224 | tf_op jit(solution)/shard_map/ppermute | solution.py:516
  28.4 1.2 %collective-permute-start.10 = (bf16[128,512]{1,0:T(8,128)(2,1)S(1)}, bf16[128,512]{1,0:T(8,128)(2,1)S(1)}, u32[]{:S(2)}, u32[]{:S(2)}) collective-permute-start(bf16[128,512]{1,0:T(8,128)(2,1)S(1)} %get-tuple-element.55), channel_id=1, source_target_pairs={{0,4},{1,5},{2,6},{3,7},{4,0},{5,1},{6,2},{7,3},{8,12},{9,13},{10,... | collective-permute-start | bytes 393224 | tf_op jit(solution)/shard_map/ppermute | solution.py:516
  29.6 1.5 %collective-permute-start.14 = (bf16[128,512]{1,0:T(8,128)(2,1)S(1)}, bf16[128,512]{1,0:T(8,128)(2,1)S(1)}, u32[]{:S(2)}, u32[]{:S(2)}) collective-permute-start(bf16[128,512]{1,0:T(8,128)(2,1)S(1)} %get-tuple-element.59), channel_id=1, source_target_pairs={{0,6},{1,7},{2,4},{3,5},{4,2},{5,3},{6,0},{7,1},{8,14},{9,15},{10,... | collective-permute-start | bytes 393224 | tf_op jit(solution)/shard_map/ppermute | solution.py:516
  31.1 1.6 %collective-permute-start.16 = (bf16[128,512]{1,0:T(8,128)(2,1)S(1)}, bf16[128,512]{1,0:T(8,128)(2,1)S(1)}, u32[]{:S(2)}, u32[]{:S(2)}) collective-permute-start(bf16[128,512]{1,0:T(8,128)(2,1)S(1)} %get-tuple-element.61), channel_id=1, source_target_pairs={{0,7},{1,6},{2,5},{3,4},{4,3},{5,2},{6,1},{7,0},{8,15},{9,14},{10,... | collective-permute-start | bytes 393224 | tf_op jit(solution)/shard_map/ppermute | solution.py:516
  32.8 4.5 %local_mixer.3 = (f32[1024,512]{1,0:T(8,128)S(1)}, bf16[1024,256]{1,0:T(8,128)(2,1)S(1)}) custom-call(s32[64]{0:T(128)S(1)} %copy-done.7, f32[16,1024]{1,0:T(8,128)S(1)} %bitcast.22, f32[7,16,1024]{2,1,0:T(8,128)S(1)} %bitcast.25, bf16[1024,1024]{1,0:T(8,128)(2,1)S(1)} %copy-done.2, bf16[1024,128]{1,0:T(8,128)(2,1)S(1)} %bitcast.18, ...), custom_call_target="tpu_custom_call" | custom-call | flops 1073741824 | bytes 6291456 | tf_op jit(solution)/shard_map/local_mixer/pallas_call | solution.py:384
  37.3 1.5 %far_and_gate.3 = (bf16[128,512]{1,0:T(8,128)(2,1)S(1)}, bf16[128,1024]{1,0:T(8,128)(2,1)S(1)}, bf16[128,1024]{1,0:T(8,128)(2,1)S(1)}, bf16[128,512]{1,0:T(8,128...) custom-call(s32[1]{0:T(128)} %bitcast.me, ...), custom_call_target="tpu_custom_call" | custom-call | flops 268435456 | bytes 4194304 | tf_op jit(solution)/shard_map/far_and_gate/pallas_call | solution.py:417
  39.0 1.4 %collective-permute-start.11 = (bf16[128,512]{1,0:T(8,128)(2,1)S(1)}, bf16[128,512]{1,0:T(8,128)(2,1)S(1)}, u32[]{:S(2)}, u32[]{:S(2)}) collective-permute-start(bf16[128,512]{1,0:T(8,128)(2,1)S(1)} %get-tuple-element.56), channel_id=1, source_target_pairs={{0,4},{1,5},{2,6},{3,7},{4,0},{5,1},{6,2},{7,3},{8,12},{9,13},{10,... | collective-permute-start | bytes 393224 | tf_op jit(solution)/shard_map/ppermute | solution.py:516
  40.4 1.0 %collective-permute-done.12.rest_8_ = bf16[128,512]{1,0:T(8,128)(2,1)S(1)} collective-permute-done((bf16[128,512]{1,0:T(8,128)(2,1)S(1)}, bf16[128,512]{1,0:T(8,128)(2,1)S(1)}, u32[]{:S(2)}, u32[]{:S(2)}) %collective-permute-start.12) | collective-permute-done | bytes 131104 | tf_op jit(solution)/shard_map/ppermute | solution.py:516
  42.6 2.2 %collective-permute-start.13 = (bf16[128,512]{1,0:T(8,128)(2,1)S(1)}, bf16[128,512]{1,0:T(8,128)(2,1)S(1)}, u32[]{:S(2)}, u32[]{:S(2)}) collective-permute-start(bf16[128,512]{1,0:T(8,128)(2,1)S(1)} %get-tuple-element.58), channel_id=1, source_target_pairs={{0,5},{1,4},{2,7},{3,6},{4,1},{5,0},{6,3},{7,2},{8,13},{9,12},{10,... | collective-permute-start | bytes 393224 | tf_op jit(solution)/shard_map/ppermute | solution.py:516
  45.4 1.6 %collective-permute-start.17 = (bf16[128,512]{1,0:T(8,128)(2,1)S(1)}, bf16[128,512]{1,0:T(8,128)(2,1)S(1)}, u32[]{:S(2)}, u32[]{:S(2)}) collective-permute-start(bf16[128,512]{1,0:T(8,128)(2,1)S(1)} %get-tuple-element.62), channel_id=1, source_target_pairs={{0,7},{1,6},{2,5},{3,4},{4,3},{5,2},{6,1},{7,0},{8,15},{9,14},{10,... | collective-permute-start | bytes 393224 | tf_op jit(solution)/shard_map/ppermute | solution.py:516
  47.0 1.7 %collective-permute-done.13.rest_9_ = bf16[128,512]{1,0:T(8,128)(2,1)S(1)} collective-permute-done((bf16[128,512]{1,0:T(8,128)(2,1)S(1)}, bf16[128,512]{1,0:T(8,128)(2,1)S(1)}, u32[]{:S(2)}, u32[]{:S(2)}) %collective-permute-start.13) | collective-permute-done | bytes 131104 | tf_op jit(solution)/shard_map/ppermute | solution.py:516
  48.7 5.1 %collective-permute-done.15.rest_11_ = bf16[128,512]{1,0:T(8,128)(2,1)S(1)} collective-permute-done((bf16[128,512]{1,0:T(8,128)(2,1)S(1)}, bf16[128,512]{1,0:T(8,128)(2,1)S(1)}, u32[]{:S(2)}, u32[]{:S(2)}) %collective-permute-start.15) | collective-permute-done | bytes 131104 | tf_op jit(solution)/shard_map/ppermute | solution.py:516
  53.8 2.9 %collective-permute-done.17.rest_13_ = bf16[128,512]{1,0:T(8,128)(2,1)S(1)} collective-permute-done((bf16[128,512]{1,0:T(8,128)(2,1)S(1)}, bf16[128,512]{1,0:T(8,128)(2,1)S(1)}, u32[]{:S(2)}, u32[]{:S(2)}) %collective-permute-start.17) | collective-permute-done | bytes 131104 | tf_op jit(solution)/shard_map/ppermute | solution.py:516
  56.8 1.7 %norm_rows.1 = bf16[128,8192]{1,0:T(8,128)(2,1)} custom-call(s32[1]{0:T(128)} %bitcast.me, f32[1,8192]{1,0:T(1,128)S(1)} %bitcast.23, bf16[128,512]{1,0:T(8,128)(2,1)S(1)} %get-tuple-element.45.rest_0_, bf16[128,512]{1,0:T(8,128)(2,1)S(1)} %get-tuple-element.50.rest_1_, bf16[128,1024]{1,0:T(8,128)(2,1)S(1)} %collective-permute-done.6.rest_2_, ...), custom_call_target="tpu_custom_call" | custom-call | flops 8388608 | bytes 4194304 | tf_op jit(solution)/shard_map/norm_rows/pallas_call | solution.py:537
  (46 shorter events, 9.0 us)
Async XLA Ops:
  4.4 4.5 %copy-start.2 = (bf16[1024,1024]{1,0:T(8,128)(2,1)S(1)}, bf16[1024,1024]{1,0:T(8,128)(2,1)}, u32[]{:S(2)}) copy-start(bf16[1024,1024]{1,0:T(8,128)(2,1)} %values.5) | copy-start | bytes 6291460
  5.4 6.6 %collective-permute-start.1 = (bf16[144,512]{1,0:T(8,128)(2,1)S(1)}, bf16[144,512]{1,0:T(8,128)(2,1)S(1)}, u32[]{:S(2)}, u32[]{:S(2)}) collective-permute-start(bf16[144,512]{1,0:T(8,128)(2,1)S(1)} %get-tuple-element.43), channel_id=1, source_target_pairs={{0,8},{1,9},{2,10},{3,11},{4,12},{5,13},{6,14},{7,15}} | collective-permute-start | bytes 442376 | tf_op jit(solution)/shard_map/ppermute | solution.py:476
  8.9 10.6 %copy-start.4 = (f32[1024,16]{0,1:T(8,128)S(1)}, f32[1024,16]{0,1:T(8,128)}, u32[]{:S(2)}) copy-start(f32[1024,16]{0,1:T(8,128)} %param.12) | copy-start | bytes 196612
  8.9 10.6 %copy-start.7 = (s32[64]{0:T(128)S(1)}, s32[64]{0:T(128)}, u32[]{:S(2)}) copy-start(s32[64]{0:T(128)} %docs.5) | copy-start | bytes 772
  9.0 10.6 %copy-start.8 = (f32[1024,16,7]{0,1,2:T(8,128)S(1)}, f32[1024,16,7]{0,1,2:T(8,128)}, u32[]{:S(2)}) copy-start(f32[1024,16,7]{0,1,2:T(8,128)} %param.13) | copy-start | bytes 1376260
  10.0 6.6 %collective-permute-start = (bf16[144,512]{1,0:T(8,128)(2,1)S(1)}, bf16[144,512]{1,0:T(8,128)(2,1)S(1)}, u32[]{:S(2)}, u32[]{:S(2)}) collective-permute-start(bf16[144,512]{1,0:T(8,128)(2,1)S(1)} %get-tuple-element.38), channel_id=1, source_target_pairs={{0,8},{1,9},{2,10},{3,11},{4,12},{5,13},{6,14},{7,15}} | collective-permute-start | bytes 442376 | tf_op jit(solution)/shard_map/ppermute | solution.py:476
  12.1 12.0 %collective-permute-start.3 = (bf16[144,512]{1,0:T(8,128)(2,1)S(1)}, bf16[144,512]{1,0:T(8,128)(2,1)S(1)}, u32[]{:S(2)}, u32[]{:S(2)}) collective-permute-start(bf16[144,512]{1,0:T(8,128)(2,1)S(1)} %merge_blocks.3), channel_id=1, source_target_pairs={{8,24},{9,25},{10,26},{11,27},{12,28},{13,29},{14,30},{15,31}} | collective-permute-start | bytes 442376 | tf_op jit(solution)/shard_map/ppermute | solution.py:476
  14.3 9.8 %collective-permute-start.2 = (bf16[144,512]{1,0:T(8,128)(2,1)S(1)}, bf16[144,512]{1,0:T(8,128)(2,1)S(1)}, u32[]{:S(2)}, u32[]{:S(2)}) collective-permute-start(bf16[144,512]{1,0:T(8,128)(2,1)S(1)} %merge_blocks.3), channel_id=1, source_target_pairs={{8,16},{16,24},{9,17},{17,25},{10,18},{18,26},{11,19},{19,27},{12,... | collective-permute-start | bytes 442376 | tf_op jit(solution)/shard_map/ppermute | solution.py:476
  16.6 7.5 %copy-start.1 = (bf16[1024,1024]{1,0:T(8,128)(2,1)S(1)}, bf16[1024,1024]{1,0:T(8,128)(2,1)}, u32[]{:S(2)}) copy-start(bf16[1024,1024]{1,0:T(8,128)(2,1)} %refs_3_.3) | copy-start | bytes 6291460
  16.6 13.0 %collective-permute-start.5 = (bf16[144,512]{1,0:T(8,128)(2,1)S(1)}, bf16[144,512]{1,0:T(8,128)(2,1)S(1)}, u32[]{:S(2)}, u32[]{:S(2)}) collective-permute-start(bf16[144,512]{1,0:T(8,128)(2,1)S(1)} %merge_blocks.2.rest_0_), channel_id=1, source_target_pairs={{8,24},{9,25},{10,26},{11,27},{12,28},{13,29},{14,30},{15,31}} | collective-permute-start | bytes 442376 | tf_op jit(solution)/shard_map/ppermute | solution.py:476
  18.1 13.1 %collective-permute-start.4 = (bf16[144,512]{1,0:T(8,128)(2,1)S(1)}, bf16[144,512]{1,0:T(8,128)(2,1)S(1)}, u32[]{:S(2)}, u32[]{:S(2)}) collective-permute-start(bf16[144,512]{1,0:T(8,128)(2,1)S(1)} %merge_blocks.2.rest_0_), channel_id=1, source_target_pairs={{8,16},{16,24},{9,17},{17,25},{10,18},{18,26},{11,19},{19,27},{12,... | collective-permute-start | bytes 442376 | tf_op jit(solution)/shard_map/ppermute | solution.py:476
  25.6 13.1 %collective-permute-start.8 = (bf16[128,512]{1,0:T(8,128)(2,1)S(1)}, bf16[128,512]{1,0:T(8,128)(2,1)S(1)}, u32[]{:S(2)}, u32[]{:S(2)}) collective-permute-start(bf16[128,512]{1,0:T(8,128)(2,1)S(1)} %get-tuple-element.53), channel_id=1, source_target_pairs={{0,3},{1,2},{2,1},{3,0},{4,7},{5,6},{6,5},{7,4},{8,11},{9,10},{10,... | collective-permute-start | bytes 393224 | tf_op jit(solution)/shard_map/ppermute | solution.py:516
  28.4 10.6 %collective-permute-start.10 = (bf16[128,512]{1,0:T(8,128)(2,1)S(1)}, bf16[128,512]{1,0:T(8,128)(2,1)S(1)}, u32[]{:S(2)}, u32[]{:S(2)}) collective-permute-start(bf16[128,512]{1,0:T(8,128)(2,1)S(1)} %get-tuple-element.55), channel_id=1, source_target_pairs={{0,4},{1,5},{2,6},{3,7},{4,0},{5,1},{6,2},{7,3},{8,12},{9,13},{10,... | collective-permute-start | bytes 393224 | tf_op jit(solution)/shard_map/ppermute | solution.py:516
  29.6 11.8 %collective-permute-start.12 = (bf16[128,512]{1,0:T(8,128)(2,1)S(1)}, bf16[128,512]{1,0:T(8,128)(2,1)S(1)}, u32[]{:S(2)}, u32[]{:S(2)}) collective-permute-start(bf16[128,512]{1,0:T(8,128)(2,1)S(1)} %get-tuple-element.57), channel_id=1, source_target_pairs={{0,5},{1,4},{2,7},{3,6},{4,1},{5,0},{6,3},{7,2},{8,13},{9,12},{10,... | collective-permute-start | bytes 393224 | tf_op jit(solution)/shard_map/ppermute | solution.py:516
  29.6 12.5 %collective-permute-start.14 = (bf16[128,512]{1,0:T(8,128)(2,1)S(1)}, bf16[128,512]{1,0:T(8,128)(2,1)S(1)}, u32[]{:S(2)}, u32[]{:S(2)}) collective-permute-start(bf16[128,512]{1,0:T(8,128)(2,1)S(1)} %get-tuple-element.59), channel_id=1, source_target_pairs={{0,6},{1,7},{2,4},{3,5},{4,2},{5,3},{6,0},{7,1},{8,14},{9,15},{10,... | collective-permute-start | bytes 393224 | tf_op jit(solution)/shard_map/ppermute | solution.py:516
  31.1 11.5 %collective-permute-start.16 = (bf16[128,512]{1,0:T(8,128)(2,1)S(1)}, bf16[128,512]{1,0:T(8,128)(2,1)S(1)}, u32[]{:S(2)}, u32[]{:S(2)}) collective-permute-start(bf16[128,512]{1,0:T(8,128)(2,1)S(1)} %get-tuple-element.61), channel_id=1, source_target_pairs={{0,7},{1,6},{2,5},{3,4},{4,3},{5,2},{6,1},{7,0},{8,15},{9,14},{10,... | collective-permute-start | bytes 393224 | tf_op jit(solution)/shard_map/ppermute | solution.py:516
  37.3 19.5 %copy-start.5 = (f32[8192]{0:T(1024)S(1)}, f32[8192]{0:T(1024)}, u32[]{:S(2)}) copy-start(f32[8192]{0:T(1024)} %param.15) | copy-start | bytes 98308
  38.8 6.0 %collective-permute-start.9 = (bf16[128,512]{1,0:T(8,128)(2,1)S(1)}, bf16[128,512]{1,0:T(8,128)(2,1)S(1)}, u32[]{:S(2)}, u32[]{:S(2)}) collective-permute-start(bf16[128,512]{1,0:T(8,128)(2,1)S(1)} %get-tuple-element.54), channel_id=1, source_target_pairs={{0,3},{1,2},{2,1},{3,0},{4,7},{5,6},{6,5},{7,4},{8,11},{9,10},{10,... | collective-permute-start | bytes 393224 | tf_op jit(solution)/shard_map/ppermute | solution.py:516
  39.0 6.4 %collective-permute-start.11 = (bf16[128,512]{1,0:T(8,128)(2,1)S(1)}, bf16[128,512]{1,0:T(8,128)(2,1)S(1)}, u32[]{:S(2)}, u32[]{:S(2)}) collective-permute-start(bf16[128,512]{1,0:T(8,128)(2,1)S(1)} %get-tuple-element.56), channel_id=1, source_target_pairs={{0,4},{1,5},{2,6},{3,7},{4,0},{5,1},{6,2},{7,3},{8,12},{9,13},{10,... | collective-permute-start | bytes 393224 | tf_op jit(solution)/shard_map/ppermute | solution.py:516
  41.4 15.4 %collective-permute-start.6 = (bf16[128,1024]{1,0:T(8,128)(2,1)S(1)}, bf16[128,1024]{1,0:T(8,128)(2,1)S(1)}, u32[]{:S(2)}, u32[]{:S(2)}) collective-permute-start(bf16[128,1024]{1,0:T(8,128)(2,1)S(1)} %get-tuple-element.51), channel_id=1, source_target_pairs={{0,1},{1,0},{2,3},{3,2},{4,5},{5,4},{6,7},{7,6},{8,9},{9,8},{10,11... | collective-permute-start | bytes 786440 | tf_op jit(solution)/shard_map/ppermute | solution.py:516
  42.1 14.6 %collective-permute-start.7 = (bf16[128,1024]{1,0:T(8,128)(2,1)S(1)}, bf16[128,1024]{1,0:T(8,128)(2,1)S(1)}, u32[]{:S(2)}, u32[]{:S(2)}) collective-permute-start(bf16[128,1024]{1,0:T(8,128)(2,1)S(1)} %get-tuple-element.52), channel_id=1, source_target_pairs={{0,2},{1,3},{2,0},{3,1},{4,6},{5,7},{6,4},{7,5},{8,10},{9,11},{10,... | collective-permute-start | bytes 786440 | tf_op jit(solution)/shard_map/ppermute | solution.py:516
  42.6 6.1 %collective-permute-start.13 = (bf16[128,512]{1,0:T(8,128)(2,1)S(1)}, bf16[128,512]{1,0:T(8,128)(2,1)S(1)}, u32[]{:S(2)}, u32[]{:S(2)}) collective-permute-start(bf16[128,512]{1,0:T(8,128)(2,1)S(1)} %get-tuple-element.58), channel_id=1, source_target_pairs={{0,5},{1,4},{2,7},{3,6},{4,1},{5,0},{6,3},{7,2},{8,13},{9,12},{10,... | collective-permute-start | bytes 393224 | tf_op jit(solution)/shard_map/ppermute | solution.py:516
  44.8 9.1 %collective-permute-start.15 = (bf16[128,512]{1,0:T(8,128)(2,1)S(1)}, bf16[128,512]{1,0:T(8,128)(2,1)S(1)}, u32[]{:S(2)}, u32[]{:S(2)}) collective-permute-start(bf16[128,512]{1,0:T(8,128)(2,1)S(1)} %get-tuple-element.60), channel_id=1, source_target_pairs={{0,6},{1,7},{2,4},{3,5},{4,2},{5,3},{6,0},{7,1},{8,14},{9,15},{10,... | collective-permute-start | bytes 393224 | tf_op jit(solution)/shard_map/ppermute | solution.py:516
  45.4 11.4 %collective-permute-start.17 = (bf16[128,512]{1,0:T(8,128)(2,1)S(1)}, bf16[128,512]{1,0:T(8,128)(2,1)S(1)}, u32[]{:S(2)}, u32[]{:S(2)}) collective-permute-start(bf16[128,512]{1,0:T(8,128)(2,1)S(1)} %get-tuple-element.62), channel_id=1, source_target_pairs={{0,7},{1,6},{2,5},{3,4},{4,3},{5,2},{6,1},{7,0},{8,15},{9,14},{10,... | collective-permute-start | bytes 393224 | tf_op jit(solution)/shard_map/ppermute | solution.py:516
  (3 other events, 4.2 us)
